TPU v7x, 256 devices: a whole 4x4x8 slice. The times are simulated.
256 devices in a mesh: rep: 2 (over core), fsdp: 32 (over y, z), tp: 4 (over x).
Axes of the slice: x: 4, y: 4, z: 8, core: 2. Of those that a mesh axis runs over, the one named last changes fastest.
Arguments:
- input_query: bfloat16 [4096, 8192], P(('rep', 'tp'), 'fsdp'), may hold values from -6 to 6
- grad_query: bfloat16 [4096, 8192], P('rep', 'tp'), may hold values from -0.125 to 0.125
- input_output: bfloat16 [4096, 8192], P(('rep', 'tp'), 'fsdp'), may hold values from -6 to 6
- grad_output: bfloat16 [4096, 8192], P('rep', 'tp'), may hold values from -0.125 to 0.125
- moment_query: bfloat16 [2, 8192, 8192], P('rep', 'fsdp', 'tp'), may hold values from -6 to 6
- moment_output: bfloat16 [2, 8192, 8192], P('rep', 'fsdp', 'tp'), may hold values from -6 to 6
- basis_query: bfloat16 [8192, 256], P('tp'), may hold values from -0.0625 to 0.0625
- basis_output: bfloat16 [8192, 256], P('tp'), may hold values from -0.0625 to 0.0625
Outputs:
- update_query: bfloat16 [8192, 8192], P('fsdp', 'tp')
- update_output: bfloat16 [8192, 8192], P('fsdp', 'tp')
- next_moment_query: bfloat16 [2, 8192, 8192], P('rep', 'fsdp', 'tp')
- next_moment_output: bfloat16 [2, 8192, 8192], P('rep', 'fsdp', 'tp')
All inputs are finite; a program needn't handle non-finite values.
Results may differ from a plain program's by a relative error of at most 0.017.
Values may be sent and summed in bfloat16 or wider, within the bound.
No kernel may reach another device: no remote copies, remote signals or barrier semaphores. Data moves between devices by JAX's collectives and lax.ppermute only.
A program may use at most 128 MiB of HBM per device.

v0:
```python
import functools

import jax
import jax.numpy as jnp
from jax import lax
from jax.experimental import pallas as pl
from jax.experimental.pallas import tpu as pltpu
from jax.sharding import PartitionSpec as P

D = 8192
RANK = 256
N_TP = 4
N_Y = 4
N_Z = 8
LANES = 128
BLOCK = 64
GROUP = 16
COLUMNS = 512

retain = 0.5
epsilon = 1e-06

Z_GROUPS = [[y * N_Z + z for z in range(N_Z)] for y in range(N_Y)]


def contract_rows(left, right, precision=None):
    return lax.dot_general(
        left,
        right,
        (((0,), (0,)), ((), ())),
        precision=precision,
        preferred_element_type=jnp.float32,
    )


def halves(x):
    high = x.astype(jnp.bfloat16)
    return high, (x - high.astype(jnp.float32)).astype(jnp.bfloat16)


def shift_tp(x, by):
    return lax.ppermute(x, "tp", [(i, (i + by) % N_TP) for i in range(N_TP)])


def shift_y(x, by):
    pairs = [
        (y * N_Z + z, (y + by) % N_Y * N_Z + z) for y in range(N_Y) for z in range(N_Z)
    ]
    return lax.ppermute(x, "fsdp", pairs)


def swap_cores(x):
    return lax.ppermute(x, "rep", [(0, 1), (1, 0)])


def from_all(x, shift):
    return [x] + [shift(x, by) for by in (1, 2, 3)]


def in_order(parts, me):
    n = len(parts)
    rows = parts[0].shape[0]
    whole = jnp.zeros((n,) + parts[0].shape, parts[0].dtype)
    for by in range(n):
        whole = lax.dynamic_update_index_in_dim(whole, parts[by], (me - by) % n, 0)
    return whole.reshape((n * rows,) + parts[0].shape[1:])


def total(parts):
    return functools.reduce(jnp.add, [part.astype(jnp.float32) for part in parts])


def first_kernel(index, *refs):
    for x, y, m, out in zip(refs[0:2], refs[2:4], refs[4:6], refs[6:8]):
        out[...] = m[0].astype(jnp.float32) + contract_rows(x[...], y[...])


def middle_kernel(index, *refs):
    for w in range(2):
        xa, xb, ya, yb, acc, out = refs[w::2]
        out[...] = (
            acc[...] + contract_rows(xa[...], ya[...]) + contract_rows(xb[...], yb[...])
        )


def last_kernel(index, *refs):
    for w in range(2):
        x, y, acc, basis, out, power = refs[w::2]
        buffer = (acc[...] + contract_rows(x[...], y[...])).astype(jnp.bfloat16)
        out[...] = buffer
        term = jnp.dot(buffer, basis[...], preferred_element_type=jnp.float32)

        @pl.when(pl.program_id(0) == 0)
        def _():
            power[...] = term

        @pl.when(pl.program_id(0) > 0)
        def _():
            power[...] += term


def token_kernel(body, index, operands, results, name):
    first = results[0][1].shape
    rows, width = first
    spec = {
        "x": lambda a: pl.BlockSpec(a.shape, lambda j, i: (0, 0)),
        "y0": lambda a: pl.BlockSpec((a.shape[0] // N_TP, COLUMNS), lambda j, i: (i[0], j)),
        "y1": lambda a: pl.BlockSpec((a.shape[0] // N_TP, COLUMNS), lambda j, i: (i[1], j)),
        "y2": lambda a: pl.BlockSpec((a.shape[0] // N_TP, COLUMNS), lambda j, i: (i[2], j)),
        "y3": lambda a: pl.BlockSpec((a.shape[0] // N_TP, COLUMNS), lambda j, i: (i[3], j)),
        "m": lambda a: pl.BlockSpec((1, rows, COLUMNS), lambda j, i: (0, 0, j)),
        "wide": lambda a: pl.BlockSpec((rows, COLUMNS), lambda j, i: (0, j)),
        "q": lambda a: pl.BlockSpec((COLUMNS, a.shape[1]), lambda j, i: (j, 0)),
    }
    arrays = [a for _, a in operands]
    return pl.pallas_call(
        body,
        grid_spec=pltpu.PrefetchScalarGridSpec(
            num_scalar_prefetch=1,
            grid=(width // COLUMNS,),
            in_specs=[spec[kind](a) for kind, a in operands],
            out_specs=[spec[kind](a) for kind, a in results],
        ),
        out_shape=[a for _, a in results],
        compiler_params=pltpu.CompilerParams(
            dimension_semantics=("arbitrary",), vmem_limit_bytes=24 << 20
        ),
        cost_estimate=pl.CostEstimate(
            flops=4 * rows * width * 512, bytes_accessed=12 << 20, transcendentals=0
        ),
        name=name,
    )(index, *arrays)


def make_buffers(inputs, grads, moments, bases):
    me = lax.axis_index("tp")
    index = jnp.stack([(me - by) % N_TP for by in range(N_TP)]).astype(jnp.int32)
    far = [shift_tp(x, 2) for x in inputs]
    near = [shift_tp(x, 1) for x in inputs] + [shift_tp(x, 3) for x in inputs]
    rows, width = inputs[0].shape[1], grads[0].shape[1]
    acc = jax.ShapeDtypeStruct((rows, width), jnp.float32)
    buffer = jax.ShapeDtypeStruct((rows, width), jnp.bfloat16)
    power = jax.ShapeDtypeStruct((rows, bases[0].shape[1]), jnp.float32)
    kinds = lambda kind, arrays: [(kind, a) for a in arrays]
    accs = token_kernel(
        first_kernel,
        index,
        kinds("x", inputs) + kinds("y0", grads) + kinds("m", moments),
        kinds("wide", [acc, acc]),
        "own_tokens",
    )
    accs = token_kernel(
        middle_kernel,
        index,
        kinds("x", near) + kinds("y1", grads) + kinds("y3", grads) + kinds("wide", accs),
        kinds("wide", [acc, acc]),
        "near_tokens",
    )
    out = token_kernel(
        last_kernel,
        index,
        kinds("x", far) + kinds("y2", grads) + kinds("wide", accs) + kinds("q", bases),
        kinds("wide", [buffer, buffer]) + kinds("x", [power, power]),
        "far_tokens",
    )
    return out[:2], out[2:]


def dot_halves(a, b, dims):
    (ah, al), (bh, bl) = halves(a), halves(b)
    dot = lambda x, y: lax.dot_general(
        x, y, (dims, ((), ())), preferred_element_type=jnp.float32
    )
    return dot(ah, bh) + (dot(ah, bl) + dot(al, bh))


def inverse_kernel(gram_ref, out_ref, work):
    n = RANK
    work[:, :n] = gram_ref[...]
    row = lax.broadcasted_iota(jnp.int32, (n, n), 0)
    lane = lax.broadcasted_iota(jnp.int32, (n, n), 1)
    work[:, n:] = jnp.where(row == lane, 1.0, 0.0)
    row = lax.broadcasted_iota(jnp.int32, (BLOCK, LANES), 0)
    lane = lax.broadcasted_iota(jnp.int32, (BLOCK, LANES), 1)
    for r0 in range(0, n, BLOCK):
        c0 = r0 // LANES * LANES
        q0 = r0 - c0
        rest = r0 + BLOCK
        a = work[r0:rest, c0 : c0 + LANES]
        w = jnp.where(lane == row + q0, 1.0, 0.0)
        for k0 in range(0, BLOCK, GROUP):
            columns = [
                jnp.broadcast_to(a[:, q0 + k : q0 + k + 1], (BLOCK, LANES))
                for k in range(k0, k0 + GROUP)
            ]
            for i in range(GROUP):
                k = k0 + i
                factor = jnp.where(row > k, columns[i] * (1.0 / columns[i][k : k + 1, :]), 0.0)
                for j in range(i + 1, GROUP):
                    columns[j] = columns[j] - factor * columns[j][k : k + 1, :]
                a = a - factor * a[k : k + 1, :]
                w = w - factor * w[k : k + 1, :]
        pivots = jnp.sum(jnp.where(lane == row + q0, a, 0.0), axis=1, keepdims=True)
        w = w * lax.rsqrt(pivots)
        end = (rest + LANES - 1) // LANES * LANES
        done = dot_halves(w, work[c0 : c0 + LANES, c0 : n + end], ((1,), (0,)))
        out_ref[r0:rest, :end] = done[:, n - c0 :]
        if end < n:
            out_ref[r0:rest, end:] = jnp.zeros((BLOCK, n - end), jnp.float32)
        if rest < n:
            d0 = rest // LANES * LANES
            term = dot_halves(done[:, d0 - c0 : n - c0], done[:, d0 - c0 :], ((0,), (0,)))
            work[rest:, d0 : n + end] = work[rest:, d0 : n + end] - term[rest - d0 :, :]


def inverse_factor(gram):
    return pl.pallas_call(
        inverse_kernel,
        out_shape=jax.ShapeDtypeStruct((RANK, RANK), jnp.float32),
        in_specs=[pl.BlockSpec(memory_space=pltpu.VMEM)],
        out_specs=pl.BlockSpec(memory_space=pltpu.VMEM),
        scratch_shapes=[pltpu.VMEM((RANK, 2 * RANK), jnp.float32)],
        compiler_params=pltpu.CompilerParams(vmem_limit_bytes=16 << 20),
        cost_estimate=pl.CostEstimate(
            flops=8 * 1000 * 1000 * 1000, bytes_accessed=1 << 20, transcendentals=0
        ),
        name="inverse_factor",
    )(gram)


def per_device(
    input_query,
    grad_query,
    input_output,
    grad_output,
    moment_query,
    moment_output,
    basis_query,
    basis_output,
):
    first = lax.axis_index("rep") == 0
    tp = lax.axis_index("tp")
    y = lax.axis_index("fsdp") // N_Z

    def split(pair):
        return jnp.where(first, pair[0], pair[1]), jnp.where(first, pair[1], pair[0])

    buffers, powers = make_buffers(
        [input_query, input_output],
        [grad_query, grad_output],
        [moment_query, moment_output],
        [basis_query, basis_output],
    )
    mine, other = split(powers)
    mine = mine + swap_cores(other.astype(jnp.bfloat16)).astype(jnp.float32)
    power = total(from_all(mine.astype(jnp.bfloat16), shift_tp))
    power_b = power.astype(jnp.bfloat16)
    powers_b = split([power_b, swap_cores(power_b)])

    rows = RANK // N_TP
    gram = lax.dynamic_slice_in_dim(
        contract_rows(power, power, lax.Precision.HIGHEST), tp * rows, rows, 0
    )
    mine, other = split([contract_rows(buffers[w], powers_b[w]) for w in range(2)])
    mine = mine + swap_cores(other.astype(jnp.bfloat16)).astype(jnp.float32)

    def quarter(x, by):
        return lax.dynamic_slice_in_dim(x, (y + by) % N_Y * (x.shape[0] // N_Y), x.shape[0] // N_Y, 0)

    packed = [
        jnp.concatenate([quarter(mine, by).astype(jnp.bfloat16), *halves(quarter(gram, by))])
        for by in (1, 2, 3)
    ]
    packed = [shift_y(x, by) for x, by in zip(packed, (1, 2, 3))]
    cut = mine.shape[0] // N_Y
    few = gram.shape[0] // N_Y
    mine = total([quarter(mine, 0)] + [x[:cut] for x in packed])
    gram = total(
        [quarter(gram, 0)]
        + [x[cut : cut + few] for x in packed]
        + [x[cut + few :] for x in packed]
    )

    exchange = lambda x: lax.all_to_all(x, "fsdp", 0, 0, axis_index_groups=Z_GROUPS)
    cut = cut // N_Z
    width = mine.shape[1]
    packed = jnp.concatenate(
        [mine.astype(jnp.bfloat16).reshape(N_Z, cut, width)]
        + [jnp.broadcast_to(x[None], (N_Z,) + x.shape) for x in halves(gram)],
        axis=1,
    )
    packed = exchange(packed).astype(jnp.float32)
    mine = jnp.sum(packed[:, :cut], axis=0).astype(jnp.bfloat16)
    gram = jnp.sum(packed[:, cut : cut + few] + packed[:, cut + few :], axis=0)

    gram = in_order(from_all(gram, shift_y), y)
    raw = exchange(jnp.broadcast_to(mine[None], (N_Z,) + mine.shape)).reshape(N_Z * cut, width)
    raw_parts = from_all(raw, shift_y)
    gram = in_order(from_all(gram, shift_tp), tp)
    inverse = inverse_factor(gram)
    raw = in_order(raw_parts, y)

    ortho = jnp.dot(power, inverse.T, precision=lax.Precision.HIGHEST)
    right = jnp.dot(raw, inverse.T.astype(jnp.bfloat16), preferred_element_type=jnp.float32)
    squares = total(from_all(jnp.sum(right * right, axis=0, keepdims=True), shift_tp))
    scale = D / RANK**0.5 / jnp.sqrt(squares + epsilon)
    ortho_b = ortho.astype(jnp.bfloat16)
    scaled_b = (ortho * scale).astype(jnp.bfloat16)
    right_b = right.astype(jnp.bfloat16)
    orthos = split([ortho_b, swap_cores(ortho_b)])
    rights = split([right_b, swap_cores(right_b)])
    scaled = split([scaled_b, swap_cores(scaled_b)])
    moments = []
    for w in range(2):
        feedback = jnp.dot(orthos[w], rights[w].T, preferred_element_type=jnp.float32)
        moments.append(
            (buffers[w].astype(jnp.float32) - (1.0 - retain) / 2 * feedback).astype(jnp.bfloat16)[
                None
            ]
        )
    updates = [
        jnp.dot(scaled[w], rights[w].T, preferred_element_type=jnp.float32).astype(jnp.bfloat16)
        for w in range(2)
    ]
    return (*updates, *moments)


def solution(mesh):
    in_specs = (
        P(("rep", "tp"), "fsdp"),
        P("rep", "tp"),
        P(("rep", "tp"), "fsdp"),
        P("rep", "tp"),
        P("rep", "fsdp", "tp"),
        P("rep", "fsdp", "tp"),
        P("tp", None),
        P("tp", None),
    )
    out_specs = (P("fsdp", "tp"), P("fsdp", "tp"), P("rep", "fsdp", "tp"), P("rep", "fsdp", "tp"))
    return jax.shard_map(
        per_device, mesh=mesh, in_specs=in_specs, out_specs=out_specs, check_vma=False
    )
```

profile of v0, /device:TPU:1, one launch (start us, length us, event | category | flops | bytes accessed | tf_op | source)
XLA Modules:
  0.0 170.2 jit_solution(18130926100931356701)
XLA Ops:
  8.0 3.7 %collective-permute-start.1 = (bf16[512,256]{1,0:T(8,128)(2,1)}, bf16[512,256]{1,0:T(8,128)(2,1)S(1)}, u32[]{:S(2)}, u32[]{:S(2)}) collective-permute-start(bf16[512,256]{1,0:T(8,128)(2,1)} %refs_1_.1), channel_id=1, source_target_pairs={{0,2},{1,3},{2,0},{3,1},{4,6},{5,7},{6,4},{7,5},{8,10},{9,11},{10,... | collective-permute-start | bytes 786440 | tf_op jit(solution)/shard_map/ppermute | solution.py:42
  11.7 3.4 %copy-done = bf16[2048,2048]{1,0:T(8,128)(2,1)S(1)} copy-done((bf16[2048,2048]{1,0:T(8,128)(2,1)S(1)}, bf16[2048,2048]{1,0:T(8,128)(2,1)}, u32[]{:S(2)}) %copy-start) | copy-done | bytes 8388632
  15.1 3.4 %copy-done.2 = bf16[2048,2048]{1,0:T(8,128)(2,1)S(1)} copy-done((bf16[2048,2048]{1,0:T(8,128)(2,1)S(1)}, bf16[2048,2048]{1,0:T(8,128)(2,1)}, u32[]{:S(2)}) %copy-start.2) | copy-done | bytes 8388632
  22.9 3.3 %own_tokens.1 = (f32[256,2048]{1,0:T(8,128)S(1)}, f32[256,2048]{1,0:T(8,128)S(1)}) custom-call(s32[4]{0:T(128)S(1)} %pad_add_fusion.index, bf16[512,256]{1,0:T(8,128)(2,1)S(1)} %copy-done.8, bf16[512,256]{1,0:T(8,128)(2,1)S(1)} %copy-done.9, bf16[2048,2048]{1,0:T(8,128)(2,1)S(1)} %copy-done, bf16[2048,2048]{1,0:T(8,128)(2,1)S(1)} %copy-done.2, ...), custom_call_target="tpu_custom_call" | custom-call | flops 1073741824 | bytes 12582912 | tf_op jit(solution)/shard_map/own_tokens/pallas_call | solution.py:116
  26.2 3.4 %copy-done.3 = bf16[2048,2048]{1,0:T(8,128)(2,1)S(1)} copy-done((bf16[2048,2048]{1,0:T(8,128)(2,1)S(1)}, bf16[2048,2048]{1,0:T(8,128)(2,1)}, u32[]{:S(2)}) %copy-start.3) | copy-done | bytes 8388632
  29.6 5.7 %near_tokens.1 = (f32[256,2048]{1,0:T(8,128)S(1)}, f32[256,2048]{1,0:T(8,128)S(1)}) custom-call(s32[4]{0:T(128)S(1)} %pad_add_fusion.index, bf16[512,256]{1,0:T(8,128)(2,1)S(1)} %collective-permute-done.2.refs_0_, bf16[512,256]{1,0:T(8,128)(2,1)S(1)} %collective-permute-done.3.refs_1_, bf16[512,256]{1,0:T(8,128)(2,1)} %collective-permute-done.4.refs_2_, ...), custom_call_target="tpu_custom_call" | custom-call | flops 1073741824 | bytes 12582912 | tf_op jit(solution)/shard_map/near_tokens/pallas_call | solution.py:116
  35.4 5.7 %far_tokens.1 = (bf16[256,2048]{1,0:T(8,128)(2,1)S(1)}, bf16[256,2048]{1,0:T(8,128)(2,1)S(1)}, f32[256,256]{1,0:T(8,128)S(1)}, f32[256,256]{1,0:T(8,128)S(1)}) custom-call(s32[4]{0:T(128)S(1)} %pad_add_fusion.index, bf16[512,256]{1,0:T(8,128)(2,1)S(1)} %collective-permute-done.refs_0_, bf16[512,256]{1,0:T(8,128)(2,1)S(1)} %collective-permute-done.1.refs_1_, ...), custom_call_target="tpu_custom_call" | custom-call | flops 1073741824 | bytes 12582912 | tf_op jit(solution)/shard_map/far_tokens/pallas_call | solution.py:116
  41.1 3.1 %collective-permute-start.6 = (bf16[256,256]{1,0:T(8,128)(2,1)S(1)}, bf16[256,256]{1,0:T(8,128)(2,1)S(1)}, u32[]{:S(2)}, u32[]{:S(2)}) collective-permute-start(bf16[256,256]{1,0:T(8,128)(2,1)S(1)} %select_convert_fusion.1), channel_id=1, source_target_pairs={{0,128},{128,0},{1,129},{129,1},{2,130},{130,2},{3,131},{131,3},{4... | collective-permute-start | bytes 393224 | tf_op jit(solution)/shard_map/ppermute | solution.py:53
  46.8 2.9 %collective-permute-start.8 = (bf16[256,256]{1,0:T(8,128)(2,1)S(1)}, bf16[256,256]{1,0:T(8,128)(2,1)S(1)}, u32[]{:S(2)}, u32[]{:S(2)}) collective-permute-start(bf16[256,256]{1,0:T(8,128)(2,1)S(1)} %add_convert_fusion.1), channel_id=1, source_target_pairs={{0,2},{1,3},{2,0},{3,1},{4,6},{5,7},{6,4},{7,5},{8,10},{9,11},{10,... | collective-permute-start | bytes 393224 | tf_op jit(solution)/shard_map/ppermute | solution.py:42
  52.1 3.7 %collective-permute-done.8 = bf16[256,256]{1,0:T(8,128)(2,1)S(1)} collective-permute-done((bf16[256,256]{1,0:T(8,128)(2,1)S(1)}, bf16[256,256]{1,0:T(8,128)(2,1)S(1)}, u32[]{:S(2)}, u32[]{:S(2)}) %collective-permute-start.8) | collective-permute-done | bytes 131104 | tf_op jit(solution)/shard_map/ppermute | solution.py:42
  69.8 2.6 %collective-permute-start.13 = (bf16[544,256]{1,0:T(8,128)(2,1)}, bf16[544,256]{1,0:T(8,128)(2,1)}, u32[]{:S(2)}, u32[]{:S(2)}) collective-permute-start(bf16[544,256]{1,0:T(8,128)(2,1)} %pad_maximum_fusion.2), channel_id=1, source_target_pairs={{0,64},{4,68},{8,72},{12,76},{16,80},{20,84},{24,88},{28,92},{32,9... | collective-permute-start | bytes 835592 | tf_op jit(solution)/shard_map/ppermute | solution.py:49
  74.2 2.9 %collective-permute-done.12 = bf16[544,256]{1,0:T(8,128)(2,1)} collective-permute-done((bf16[544,256]{1,0:T(8,128)(2,1)S(1)}, bf16[544,256]{1,0:T(8,128)(2,1)}, u32[]{:S(2)}, u32[]{:S(2)}) %collective-permute-start.12) | collective-permute-done | bytes 278560 | tf_op jit(solution)/shard_map/ppermute | solution.py:49
  77.1 7.1 %collective-permute-done.13 = bf16[544,256]{1,0:T(8,128)(2,1)} collective-permute-done((bf16[544,256]{1,0:T(8,128)(2,1)}, bf16[544,256]{1,0:T(8,128)(2,1)}, u32[]{:S(2)}, u32[]{:S(2)}) %collective-permute-start.13) | collective-permute-done | bytes 278560 | tf_op jit(solution)/shard_map/ppermute | solution.py:49
  87.4 8.2 %all-to-all-start = ((bf16[8,96,256]{2,1,0:T(8,128)(2,1)}), bf16[8,96,256]{2,1,0:T(8,128)(2,1)S(1)}, u32[]{:S(2)}, u32[]{:S(2)}) async-start(bf16[8,96,256]{2,1,0:T(8,128)(2,1)} %pad_maximum_fusion), calls=%async_computation | async-start | bytes 786432 | tf_op jit(solution)/shard_map/all_to_all | solution.py:284
  95.6 12.5 %all-to-all-done = bf16[8,96,256]{2,1,0:T(8,128)(2,1)S(1)} async-done(((bf16[8,96,256]{2,1,0:T(8,128)(2,1)}), bf16[8,96,256]{2,1,0:T(8,128)(2,1)S(1)}, u32[]{:S(2)}, u32[]{:S(2)}) %all-to-all-start) | async-done | bytes 393248 | tf_op jit(solution)/shard_map/all_to_all | solution.py:284
  108.1 5.7 %collective-permute-start.15 = (f32[16,256]{1,0:T(8,128)S(1)}, f32[16,256]{1,0:T(8,128)S(1)}, u32[]{:S(2)}, u32[]{:S(2)}) collective-permute-start(f32[16,256]{1,0:T(8,128)S(1)} %fusion.2), channel_id=1, source_target_pairs={{0,32},{4,36},{8,40},{12,44},{16,48},{20,52},{24,56},{28,60},{32,6... | collective-permute-start | bytes 49160 | tf_op jit(solution)/shard_map/ppermute | solution.py:49
  117.0 3.4 %all-to-all-start.1 = ((bf16[8,64,256]{2,1,0:T(8,128)(2,1)}), bf16[8,64,256]{2,1,0:T(8,128)(2,1)S(1)}, u32[]{:S(2)}, u32[]{:S(2)}) async-start(bf16[8,64,256]{2,1,0:T(8,128)(2,1)} %broadcast_in_dim.88), calls=%async_computation.1 | async-start | bytes 524288 | tf_op jit(solution)/shard_map/all_to_all | solution.py:284
  120.7 3.0 %collective-permute-start.19 = (f32[64,256]{1,0:T(8,128)S(1)}, f32[64,256]{1,0:T(8,128)S(1)}, u32[]{:S(2)}, u32[]{:S(2)}) collective-permute-start(f32[64,256]{1,0:T(8,128)S(1)} %bitcast.53), channel_id=1, source_target_pairs={{0,2},{1,3},{2,0},{3,1},{4,6},{5,7},{6,4},{7,5},{8,10},{9,11},{10,... | collective-permute-start | bytes 196616 | tf_op jit(solution)/shard_map/ppermute | solution.py:42
  127.2 3.3 %all-to-all-done.1 = bf16[8,64,256]{2,1,0:T(8,128)(2,1)S(1)} async-done(((bf16[8,64,256]{2,1,0:T(8,128)(2,1)}), bf16[8,64,256]{2,1,0:T(8,128)(2,1)S(1)}, u32[]{:S(2)}, u32[]{:S(2)}) %all-to-all-start.1) | async-done | bytes 262176 | tf_op jit(solution)/shard_map/all_to_all | solution.py:284
  130.9 7.8 %inverse_factor.1 = f32[256,256]{1,0:T(8,128)S(1)} custom-call(f32[256,256]{1,0:T(8,128)S(1)} %bitcast.45), custom_call_target="tpu_custom_call" | custom-call | flops 8000000000 | bytes 1048576 | tf_op jit(solution)/shard_map/inverse_factor/pallas_call | solution.py:217
  141.4 4.2 %collective-permute-done.22 = bf16[512,256]{1,0:T(8,128)(2,1)S(1)} collective-permute-done((bf16[512,256]{1,0:T(8,128)(2,1)S(1)}, bf16[512,256]{1,0:T(8,128)(2,1)S(1)}, u32[]{:S(2)}, u32[]{:S(2)}) %collective-permute-start.22) | collective-permute-done | bytes 262176 | tf_op jit(solution)/shard_map/ppermute | solution.py:49
  145.6 6.6 %collective-permute-done.23 = bf16[512,256]{1,0:T(8,128)(2,1)S(1)} collective-permute-done((bf16[512,256]{1,0:T(8,128)(2,1)S(1)}, bf16[512,256]{1,0:T(8,128)(2,1)S(1)}, u32[]{:S(2)}, u32[]{:S(2)}) %collective-permute-start.23) | collective-permute-done | bytes 262176 | tf_op jit(solution)/shard_map/ppermute | solution.py:49
  152.9 2.5 %collective-permute-start.28 = (bf16[2048,256]{1,0:T(8,128)(2,1)S(1)}, bf16[2048,256]{1,0:T(8,128)(2,1)S(1)}, u32[]{:S(2)}, u32[]{:S(2)}) collective-permute-start(bf16[2048,256]{1,0:T(8,128)(2,1)S(1)} %get-tuple-element.29), channel_id=1, source_target_pairs={{0,128},{128,0},{1,129},{129,1},{2,130},{130,2},{3,131},{131,3},{4... | collective-permute-start | bytes 3145736 | tf_op jit(solution)/shard_map/ppermute | solution.py:53
  155.4 3.1 %collective-permute-start.25 = (f32[1,256]{1,0:T(1,128)S(1)}, f32[1,256]{1,0:T(1,128)S(1)}, u32[]{:S(2)}, u32[]{:S(2)}) collective-permute-start(f32[1,256]{1,0:T(1,128)S(1)} %bitcast.58), channel_id=1, source_target_pairs={{0,2},{1,3},{2,0},{3,1},{4,6},{5,7},{6,4},{7,5},{8,10},{9,11},{10,... | collective-permute-start | bytes 3080 | tf_op jit(solution)/shard_map/ppermute | solution.py:42
  (112 shorter events, 58.2 us)
Async XLA Ops:
  0.6 7.4 %collective-permute-start.2 = (bf16[512,256]{1,0:T(8,128)(2,1)}, bf16[512,256]{1,0:T(8,128)(2,1)S(1)}, u32[]{:S(2)}, u32[]{:S(2)}) collective-permute-start(bf16[512,256]{1,0:T(8,128)(2,1)} %refs_0_.1), channel_id=1, source_target_pairs={{0,1},{1,2},{2,3},{3,0},{4,5},{5,6},{6,7},{7,4},{8,9},{9,10},{10,1... | collective-permute-start | bytes 786440 | tf_op jit(solution)/shard_map/ppermute | solution.py:42
  2.7 23.4 %collective-permute-start.3 = (bf16[512,256]{1,0:T(8,128)(2,1)}, bf16[512,256]{1,0:T(8,128)(2,1)S(1)}, u32[]{:S(2)}, u32[]{:S(2)}) collective-permute-start(bf16[512,256]{1,0:T(8,128)(2,1)} %refs_1_.1), channel_id=1, source_target_pairs={{0,1},{1,2},{2,3},{3,0},{4,5},{5,6},{6,7},{7,4},{8,9},{9,10},{10,1... | collective-permute-start | bytes 786440 | tf_op jit(solution)/shard_map/ppermute | solution.py:42
  4.0 22.2 %collective-permute-start.4 = (bf16[512,256]{1,0:T(8,128)(2,1)}, bf16[512,256]{1,0:T(8,128)(2,1)}, u32[]{:S(2)}, u32[]{:S(2)}) collective-permute-start(bf16[512,256]{1,0:T(8,128)(2,1)} %refs_0_.1), channel_id=1, source_target_pairs={{0,3},{1,0},{2,1},{3,2},{4,7},{5,4},{6,5},{7,6},{8,11},{9,8},{10,9... | collective-permute-start | bytes 786440 | tf_op jit(solution)/shard_map/ppermute | solution.py:42
  5.4 20.7 %collective-permute-start.5 = (bf16[512,256]{1,0:T(8,128)(2,1)}, bf16[512,256]{1,0:T(8,128)(2,1)}, u32[]{:S(2)}, u32[]{:S(2)}) collective-permute-start(bf16[512,256]{1,0:T(8,128)(2,1)} %refs_1_.1), channel_id=1, source_target_pairs={{0,3},{1,0},{2,1},{3,2},{4,7},{5,4},{6,5},{7,6},{8,11},{9,8},{10,9... | collective-permute-start | bytes 786440 | tf_op jit(solution)/shard_map/ppermute | solution.py:42
  5.6 29.7 %collective-permute-start = (bf16[512,256]{1,0:T(8,128)(2,1)}, bf16[512,256]{1,0:T(8,128)(2,1)S(1)}, u32[]{:S(2)}, u32[]{:S(2)}) collective-permute-start(bf16[512,256]{1,0:T(8,128)(2,1)} %refs_0_.1), channel_id=1, source_target_pairs={{0,2},{1,3},{2,0},{3,1},{4,6},{5,7},{6,4},{7,5},{8,10},{9,11},{10,... | collective-permute-start | bytes 786440 | tf_op jit(solution)/shard_map/ppermute | solution.py:42
  8.0 27.3 %collective-permute-start.1 = (bf16[512,256]{1,0:T(8,128)(2,1)}, bf16[512,256]{1,0:T(8,128)(2,1)S(1)}, u32[]{:S(2)}, u32[]{:S(2)}) collective-permute-start(bf16[512,256]{1,0:T(8,128)(2,1)} %refs_1_.1), channel_id=1, source_target_pairs={{0,2},{1,3},{2,0},{3,1},{4,6},{5,7},{6,4},{7,5},{8,10},{9,11},{10,... | collective-permute-start | bytes 786440 | tf_op jit(solution)/shard_map/ppermute | solution.py:42
  41.1 4.0 %collective-permute-start.6 = (bf16[256,256]{1,0:T(8,128)(2,1)S(1)}, bf16[256,256]{1,0:T(8,128)(2,1)S(1)}, u32[]{:S(2)}, u32[]{:S(2)}) collective-permute-start(bf16[256,256]{1,0:T(8,128)(2,1)S(1)} %select_convert_fusion.1), channel_id=1, source_target_pairs={{0,128},{128,0},{1,129},{129,1},{2,130},{130,2},{3,131},{131,3},{4... | collective-permute-start | bytes 393224 | tf_op jit(solution)/shard_map/ppermute | solution.py:53
  45.2 7.0 %collective-permute-start.7 = (bf16[256,256]{1,0:T(8,128)(2,1)S(1)}, bf16[256,256]{1,0:T(8,128)(2,1)S(1)}, u32[]{:S(2)}, u32[]{:S(2)}) collective-permute-start(bf16[256,256]{1,0:T(8,128)(2,1)S(1)} %add_convert_fusion.1), channel_id=1, source_target_pairs={{0,1},{1,2},{2,3},{3,0},{4,5},{5,6},{6,7},{7,4},{8,9},{9,10},{10,1... | collective-permute-start | bytes 393224 | tf_op jit(solution)/shard_map/ppermute | solution.py:42
  46.8 9.0 %collective-permute-start.8 = (bf16[256,256]{1,0:T(8,128)(2,1)S(1)}, bf16[256,256]{1,0:T(8,128)(2,1)S(1)}, u32[]{:S(2)}, u32[]{:S(2)}) collective-permute-start(bf16[256,256]{1,0:T(8,128)(2,1)S(1)} %add_convert_fusion.1), channel_id=1, source_target_pairs={{0,2},{1,3},{2,0},{3,1},{4,6},{5,7},{6,4},{7,5},{8,10},{9,11},{10,... | collective-permute-start | bytes 393224 | tf_op jit(solution)/shard_map/ppermute | solution.py:42
  49.8 6.1 %collective-permute-start.9 = (bf16[256,256]{1,0:T(8,128)(2,1)S(1)}, bf16[256,256]{1,0:T(8,128)(2,1)S(1)}, u32[]{:S(2)}, u32[]{:S(2)}) collective-permute-start(bf16[256,256]{1,0:T(8,128)(2,1)S(1)} %add_convert_fusion.1), channel_id=1, source_target_pairs={{0,3},{1,0},{2,1},{3,2},{4,7},{5,4},{6,5},{7,6},{8,11},{9,8},{10,9... | collective-permute-start | bytes 393224 | tf_op jit(solution)/shard_map/ppermute | solution.py:42
  67.7 9.4 %collective-permute-start.12 = (bf16[544,256]{1,0:T(8,128)(2,1)S(1)}, bf16[544,256]{1,0:T(8,128)(2,1)}, u32[]{:S(2)}, u32[]{:S(2)}) collective-permute-start(bf16[544,256]{1,0:T(8,128)(2,1)S(1)} %pad_maximum_fusion.1), channel_id=1, source_target_pairs={{0,32},{4,36},{8,40},{12,44},{16,48},{20,52},{24,56},{28,60},{32,6... | collective-permute-start | bytes 835592 | tf_op jit(solution)/shard_map/ppermute | solution.py:49
  69.8 14.4 %collective-permute-start.13 = (bf16[544,256]{1,0:T(8,128)(2,1)}, bf16[544,256]{1,0:T(8,128)(2,1)}, u32[]{:S(2)}, u32[]{:S(2)}) collective-permute-start(bf16[544,256]{1,0:T(8,128)(2,1)} %pad_maximum_fusion.2), channel_id=1, source_target_pairs={{0,64},{4,68},{8,72},{12,76},{16,80},{20,84},{24,88},{28,92},{32,9... | collective-permute-start | bytes 835592 | tf_op jit(solution)/shard_map/ppermute | solution.py:49
  73.2 11.2 %collective-permute-start.14 = (bf16[544,256]{1,0:T(8,128)(2,1)}, bf16[544,256]{1,0:T(8,128)(2,1)}, u32[]{:S(2)}, u32[]{:S(2)}) collective-permute-start(bf16[544,256]{1,0:T(8,128)(2,1)} %pad_maximum_fusion.3), channel_id=1, source_target_pairs={{0,96},{4,100},{8,104},{12,108},{16,112},{20,116},{24,120},{28,124... | collective-permute-start | bytes 835592 | tf_op jit(solution)/shard_map/ppermute | solution.py:49
  87.4 20.7 %all-to-all-start = ((bf16[8,96,256]{2,1,0:T(8,128)(2,1)}), bf16[8,96,256]{2,1,0:T(8,128)(2,1)S(1)}, u32[]{:S(2)}, u32[]{:S(2)}) async-start(bf16[8,96,256]{2,1,0:T(8,128)(2,1)} %pad_maximum_fusion), calls=%async_computation | async-start | bytes 786432 | tf_op jit(solution)/shard_map/all_to_all | solution.py:284
  108.1 12.4 %collective-permute-start.15 = (f32[16,256]{1,0:T(8,128)S(1)}, f32[16,256]{1,0:T(8,128)S(1)}, u32[]{:S(2)}, u32[]{:S(2)}) collective-permute-start(f32[16,256]{1,0:T(8,128)S(1)} %fusion.2), channel_id=1, source_target_pairs={{0,32},{4,36},{8,40},{12,44},{16,48},{20,52},{24,56},{28,60},{32,6... | collective-permute-start | bytes 49160 | tf_op jit(solution)/shard_map/ppermute | solution.py:49
  113.8 6.7 %collective-permute-start.16 = (f32[16,256]{1,0:T(8,128)S(1)}, f32[16,256]{1,0:T(8,128)S(1)}, u32[]{:S(2)}, u32[]{:S(2)}) collective-permute-start(f32[16,256]{1,0:T(8,128)S(1)} %fusion.2), channel_id=1, source_target_pairs={{0,64},{4,68},{8,72},{12,76},{16,80},{20,84},{24,88},{28,92},{32,9... | collective-permute-start | bytes 49160 | tf_op jit(solution)/shard_map/ppermute | solution.py:49
  115.3 5.3 %collective-permute-start.17 = (f32[16,256]{1,0:T(8,128)S(1)}, f32[16,256]{1,0:T(8,128)S(1)}, u32[]{:S(2)}, u32[]{:S(2)}) collective-permute-start(f32[16,256]{1,0:T(8,128)S(1)} %fusion.2), channel_id=1, source_target_pairs={{0,96},{4,100},{8,104},{12,108},{16,112},{20,116},{24,120},{28,124... | collective-permute-start | bytes 49160 | tf_op jit(solution)/shard_map/ppermute | solution.py:49
  117.0 13.5 %all-to-all-start.1 = ((bf16[8,64,256]{2,1,0:T(8,128)(2,1)}), bf16[8,64,256]{2,1,0:T(8,128)(2,1)S(1)}, u32[]{:S(2)}, u32[]{:S(2)}) async-start(bf16[8,64,256]{2,1,0:T(8,128)(2,1)} %broadcast_in_dim.88), calls=%async_computation.1 | async-start | bytes 524288 | tf_op jit(solution)/shard_map/all_to_all | solution.py:284
  120.6 4.4 %collective-permute-start.18 = (f32[64,256]{1,0:T(8,128)S(1)}, f32[64,256]{1,0:T(8,128)S(1)}, u32[]{:S(2)}, u32[]{:S(2)}) collective-permute-start(f32[64,256]{1,0:T(8,128)S(1)} %bitcast.52), channel_id=1, source_target_pairs={{0,1},{1,2},{2,3},{3,0},{4,5},{5,6},{6,7},{7,4},{8,9},{9,10},{10,1... | collective-permute-start | bytes 196616 | tf_op jit(solution)/shard_map/ppermute | solution.py:42
  120.7 5.4 %collective-permute-start.19 = (f32[64,256]{1,0:T(8,128)S(1)}, f32[64,256]{1,0:T(8,128)S(1)}, u32[]{:S(2)}, u32[]{:S(2)}) collective-permute-start(f32[64,256]{1,0:T(8,128)S(1)} %bitcast.53), channel_id=1, source_target_pairs={{0,2},{1,3},{2,0},{3,1},{4,6},{5,7},{6,4},{7,5},{8,10},{9,11},{10,... | collective-permute-start | bytes 196616 | tf_op jit(solution)/shard_map/ppermute | solution.py:42
  130.5 10.8 %collective-permute-start.21 = (bf16[512,256]{1,0:T(8,128)(2,1)S(1)}, bf16[512,256]{1,0:T(8,128)(2,1)S(1)}, u32[]{:S(2)}, u32[]{:S(2)}) collective-permute-start(bf16[512,256]{1,0:T(8,128)(2,1)S(1)} %bitcast.46), channel_id=1, source_target_pairs={{0,32},{4,36},{8,40},{12,44},{16,48},{20,52},{24,56},{28,60},{32,6... | collective-permute-start | bytes 786440 | tf_op jit(solution)/shard_map/ppermute | solution.py:49
  138.8 6.8 %collective-permute-start.22 = (bf16[512,256]{1,0:T(8,128)(2,1)S(1)}, bf16[512,256]{1,0:T(8,128)(2,1)S(1)}, u32[]{:S(2)}, u32[]{:S(2)}) collective-permute-start(bf16[512,256]{1,0:T(8,128)(2,1)S(1)} %bitcast.47), channel_id=1, source_target_pairs={{0,64},{4,68},{8,72},{12,76},{16,80},{20,84},{24,88},{28,92},{32,9... | collective-permute-start | bytes 786440 | tf_op jit(solution)/shard_map/ppermute | solution.py:49
  140.4 11.8 %collective-permute-start.23 = (bf16[512,256]{1,0:T(8,128)(2,1)S(1)}, bf16[512,256]{1,0:T(8,128)(2,1)S(1)}, u32[]{:S(2)}, u32[]{:S(2)}) collective-permute-start(bf16[512,256]{1,0:T(8,128)(2,1)S(1)} %bitcast.48), channel_id=1, source_target_pairs={{0,96},{4,100},{8,104},{12,108},{16,112},{20,116},{24,120},{28,124... | collective-permute-start | bytes 786440 | tf_op jit(solution)/shard_map/ppermute | solution.py:49
  152.9 11.3 %collective-permute-start.28 = (bf16[2048,256]{1,0:T(8,128)(2,1)S(1)}, bf16[2048,256]{1,0:T(8,128)(2,1)S(1)}, u32[]{:S(2)}, u32[]{:S(2)}) collective-permute-start(bf16[2048,256]{1,0:T(8,128)(2,1)S(1)} %get-tuple-element.29), channel_id=1, source_target_pairs={{0,128},{128,0},{1,129},{129,1},{2,130},{130,2},{3,131},{131,3},{4... | collective-permute-start | bytes 3145736 | tf_op jit(solution)/shard_map/ppermute | solution.py:53
  (20 other events, 58.8 us)
where the time goes:
time: 171 us; the launch traced here: 170 us
  starting transfers between devices  58.4 us (34%)
  waiting for transfers between devices  53.8 us (31%)
  Pallas kernels  22.5 us (13%)
  local copies, waits for them, and re-layouts  17 us (10%)
  matrix products  10.5 us (6%)
  other arithmetic  7.06 us (4%)
    ppermute x15, starting transfers between devices, shift_tp(): return lax.ppermute(x, 'tp', [(i, (i + by) % N_TP) for i in range(N_TP)])  21.5 us
    ppermute x9, waiting for transfers between devices, shift_y(): return lax.ppermute(x, 'fsdp', pairs)  21 us
    ppermute x9, starting transfers between devices, shift_y(): return lax.ppermute(x, 'fsdp', pairs)  16.1 us
    unnamed x24, local copies, waits for them, and re-layouts  15.9 us
    all_to_all x2, waiting for transfers between devices, per_device(): lax.all_to_all(x, 'fsdp', 0, 0, axis_index_groups=Z_GROUPS)  15.7 us
    pallas_call x3, Pallas kernels, token_kernel(): pl.pallas_call(body, grid_spec=pltpu.PrefetchScalarGridSpec(num_scalar_pr...  14.6 us
    ppermute x15, waiting for transfers between devices, shift_tp(): return lax.ppermute(x, 'tp', [(i, (i + by) % N_TP) for i in range(N_TP)])  12.2 us
    all_to_all x2, starting transfers between devices, per_device(): lax.all_to_all(x, 'fsdp', 0, 0, axis_index_groups=Z_GROUPS)  11.6 us
  transfers between devices with their start and end apart: 32, of which 20 were waited for; matrix products, arithmetic and copies ran while one was open for 4% of the time, Pallas kernels for 10%

commit v1 on v0

v1 whole, which is shorter than its diff:
```python
import functools

import jax
import jax.numpy as jnp
from jax import lax
from jax.experimental import pallas as pl
from jax.experimental.pallas import tpu as pltpu
from jax.sharding import PartitionSpec as P

D = 8192
RANK = 256
N_TP = 4
N_Y = 4
N_Z = 8
LANES = 128
COLUMNS = 512
BLOCK = 64
GROUP = 16

retain = 0.5
epsilon = 1e-06

Y_GROUPS = [[y * N_Z + z for y in range(N_Y)] for z in range(N_Z)]
Z_GROUPS = [[y * N_Z + z for z in range(N_Z)] for y in range(N_Y)]


def contract_rows(left, right, precision=None):
    return lax.dot_general(
        left,
        right,
        (((0,), (0,)), ((), ())),
        precision=precision,
        preferred_element_type=jnp.float32,
    )


def halves(x):
    high = x.astype(jnp.bfloat16)
    return high, (x - high.astype(jnp.float32)).astype(jnp.bfloat16)


def shift_tp(x, by):
    return lax.ppermute(x, "tp", [(i, (i + by) % N_TP) for i in range(N_TP)])


def shift_y(x, by):
    pairs = [
        (y * N_Z + z, (y + by) % N_Y * N_Z + z) for y in range(N_Y) for z in range(N_Z)
    ]
    return lax.ppermute(x, "fsdp", pairs)


def swap_cores(x):
    return lax.ppermute(x, "rep", [(0, 1), (1, 0)])


def from_all(x, shift):
    return [x] + [shift(x, by) for by in (1, 2, 3)]


def in_order(parts, me):
    n = len(parts)
    whole = jnp.zeros((n,) + parts[0].shape, parts[0].dtype)
    for by in range(n):
        whole = lax.dynamic_update_index_in_dim(whole, parts[by], (me - by) % n, 0)
    return whole.reshape((n * parts[0].shape[0],) + parts[0].shape[1:])


def total(parts):
    return functools.reduce(jnp.add, [part.astype(jnp.float32) for part in parts])


def tokens_by_distance(query, output):
    query_up = shift_tp(query, 1)
    output_down = shift_tp(output, 3)
    query_down = shift_tp(query, 3)
    output_up = shift_tp(output, 1)
    query_far = shift_tp(query_up, 1)
    output_far = shift_tp(output_down, 3)
    return [
        [query, query_up, query_far, query_down],
        [output, output_up, output_far, output_down],
    ]


def exchange(x, groups):
    return lax.all_to_all(x, "fsdp", 0, 0, axis_index_groups=groups)


def copies(x, n):
    return jnp.broadcast_to(x[None], (n,) + x.shape)


def whole(a):
    return pl.BlockSpec(a.shape, lambda *_: (0,) * len(a.shape), pipeline_mode=pl.Buffered(1))


def local_kernel(body, operands, results, name, **more):
    return pl.pallas_call(
        body,
        out_shape=results,
        compiler_params=pltpu.CompilerParams(vmem_limit_bytes=12 << 20),
        cost_estimate=pl.CostEstimate(flops=1 << 20, bytes_accessed=1 << 20, transcendentals=0),
        name=name,
        **more,
    )(*operands)


def token_blocks(body, index, small, grads, results, scratch, name):
    count = grads[0].shape[0] // N_TP
    block = lambda a: pl.BlockSpec((count, a.shape[1]), lambda s, i: (i[s], 0))
    return pl.pallas_call(
        body,
        grid_spec=pltpu.PrefetchScalarGridSpec(
            num_scalar_prefetch=1,
            grid=(N_TP,),
            in_specs=[whole(a) for a in small] + [block(a) for a in grads],
            out_specs=[
                pl.BlockSpec(a.shape, lambda *_, n=len(a.shape): (0,) * n) for a in results
            ],
            scratch_shapes=scratch,
        ),
        out_shape=results,
        compiler_params=pltpu.CompilerParams(
            dimension_semantics=("arbitrary",), vmem_limit_bytes=32 << 20
        ),
        cost_estimate=pl.CostEstimate(flops=1 << 20, bytes_accessed=1 << 20, transcendentals=0),
        name=name,
    )(index, *small, *grads)


def power_kernel(index, *refs):
    step = pl.program_id(0)
    for w in range(2):
        own, up, down, moment, basis, grad, far, near = refs[w::2]
        product = jnp.dot(grad[...], basis[...], preferred_element_type=jnp.float32)
        product = product.astype(jnp.bfloat16)

        @pl.when(step == 0)
        def _():
            far[...] = product
            near[...] = jnp.dot(moment[0], basis[...], preferred_element_type=jnp.float32)

        for at, tokens in ((1, own), (2, up), (3, down)):

            @pl.when(step == at)
            def _():
                near[...] += contract_rows(tokens[...], product)


def buffer_kernel(index, *refs):
    step = pl.program_id(0)
    for w in range(2):
        far, own, up, down, moment, grad, buffer, acc = refs[w::2]

        @pl.when(step == 0)
        def _():
            acc[...] = moment[0].astype(jnp.float32)

        for at, tokens in ((0, far), (1, own), (2, up), (3, down)):

            @pl.when(step == at)
            def _():
                turned = tokens[...].T
                for c in range(0, acc.shape[1], COLUMNS):
                    here = slice(c, c + COLUMNS)
                    acc[:, here] += jnp.dot(
                        turned, grad[:, here], preferred_element_type=jnp.float32
                    )

        @pl.when(step == N_TP - 1)
        def _():
            buffer[...] = acc[...].astype(jnp.bfloat16)


def pack_kernel(mine, other, gram, out):
    many, few = mine.shape[0] // N_Y, gram.shape[0] // N_Y
    for j in range(N_Y):
        rows = slice(j * many, (j + 1) * many)
        term = mine[rows].astype(jnp.float32) + other[rows].astype(jnp.float32)
        out[j, :many] = term.astype(jnp.bfloat16)
        out[j, many:] = gram[j * few : (j + 1) * few]


def sum_y_kernel(pieces, out):
    n, rows, _ = out.shape
    few = RANK // N_TP // N_Y
    many = rows - few
    add = lambda at, size: total([pieces[j, at : at + size] for j in range(N_Y)])
    gram = add(n * many, few).astype(jnp.bfloat16)
    for j in range(n):
        out[j, :many] = add(j * many, many).astype(jnp.bfloat16)
        out[j, many:] = gram


def sum_z_kernel(pieces, out, gram):
    many = out.shape[1]
    rows = total([pieces[j, :many] for j in range(N_Z)]).astype(jnp.bfloat16)
    for j in range(N_Z):
        out[j] = rows
    gram[...] = total([pieces[j, many:] for j in range(N_Z)])


def dot_halves(a, b, dims):
    (ah, al), (bh, bl) = halves(a), halves(b)
    dot = lambda x, y: lax.dot_general(
        x, y, (dims, ((), ())), preferred_element_type=jnp.float32
    )
    return dot(ah, bh) + (dot(ah, bl) + dot(al, bh))


def inverse_kernel(gram_ref, out_ref, work):
    n = RANK
    work[:, :n] = gram_ref[...]
    row = lax.broadcasted_iota(jnp.int32, (n, n), 0)
    lane = lax.broadcasted_iota(jnp.int32, (n, n), 1)
    work[:, n:] = jnp.where(row == lane, 1.0, 0.0)
    row = lax.broadcasted_iota(jnp.int32, (BLOCK, LANES), 0)
    lane = lax.broadcasted_iota(jnp.int32, (BLOCK, LANES), 1)
    for r0 in range(0, n, BLOCK):
        c0 = r0 // LANES * LANES
        q0 = r0 - c0
        rest = r0 + BLOCK
        a = work[r0:rest, c0 : c0 + LANES]
        w = jnp.where(lane == row + q0, 1.0, 0.0)
        for k0 in range(0, BLOCK, GROUP):
            columns = [
                jnp.broadcast_to(a[:, q0 + k : q0 + k + 1], (BLOCK, LANES))
                for k in range(k0, k0 + GROUP)
            ]
            for i in range(GROUP):
                k = k0 + i
                factor = jnp.where(row > k, columns[i] * (1.0 / columns[i][k : k + 1, :]), 0.0)
                for j in range(i + 1, GROUP):
                    columns[j] = columns[j] - factor * columns[j][k : k + 1, :]
                a = a - factor * a[k : k + 1, :]
                w = w - factor * w[k : k + 1, :]
        pivots = jnp.sum(jnp.where(lane == row + q0, a, 0.0), axis=1, keepdims=True)
        w = w * lax.rsqrt(pivots)
        end = (rest + LANES - 1) // LANES * LANES
        done = dot_halves(w, work[c0 : c0 + LANES, c0 : n + end], ((1,), (0,)))
        out_ref[r0:rest, :end] = done[:, n - c0 :]
        if end < n:
            out_ref[r0:rest, end:] = jnp.zeros((BLOCK, n - end), jnp.float32)
        if rest < n:
            d0 = rest // LANES * LANES
            term = dot_halves(done[:, d0 - c0 : n - c0], done[:, d0 - c0 :], ((0,), (0,)))
            work[rest:, d0 : n + end] = work[rest:, d0 : n + end] - term[rest - d0 :, :]


def inverse_factor(gram):
    return pl.pallas_call(
        inverse_kernel,
        out_shape=jax.ShapeDtypeStruct((RANK, RANK), jnp.float32),
        in_specs=[pl.BlockSpec(memory_space=pltpu.VMEM)],
        out_specs=pl.BlockSpec(memory_space=pltpu.VMEM),
        scratch_shapes=[pltpu.VMEM((RANK, 2 * RANK), jnp.float32)],
        compiler_params=pltpu.CompilerParams(vmem_limit_bytes=6 << 20),
        cost_estimate=pl.CostEstimate(
            flops=8 * 1000 * 1000 * 1000, bytes_accessed=1 << 20, transcendentals=0
        ),
        name="inverse_factor",
    )(gram)


def per_device(
    input_query,
    grad_query,
    input_output,
    grad_output,
    moment_query,
    moment_output,
    basis_query,
    basis_output,
):
    first = lax.axis_index("rep") == 0
    tp = lax.axis_index("tp")
    y = lax.axis_index("fsdp") // N_Z

    def split(pair):
        return jnp.where(first, pair[0], pair[1]), jnp.where(first, pair[1], pair[0])

    grads = [grad_query, grad_output]
    bases = [basis_query, basis_output]
    tokens = tokens_by_distance(input_query, input_output)

    index = jnp.stack([(tp - by) % N_TP for by in (2, 0, 1, 3)]).astype(jnp.int32)
    pairs = list(zip(*tokens))
    own, up, far, down = [list(pair) for pair in pairs]
    whole_moments = [moment_query, moment_output]
    rows = own[0].shape[1]
    shape = lambda r, c, dtype: jax.ShapeDtypeStruct((r, c), dtype)
    ahead = token_blocks(
        power_kernel,
        index,
        own + up + down + whole_moments + bases,
        grads,
        [shape(own[0].shape[0], RANK, jnp.bfloat16)] * 2 + [shape(rows, RANK, jnp.float32)] * 2,
        [],
        "power_terms",
    )
    powers = [ahead[2 + w] + contract_rows(far[w], ahead[w]) for w in range(2)]
    mine, other = split(powers)
    mine = mine + swap_cores(other.astype(jnp.bfloat16)).astype(jnp.float32)
    mine, far = lax.optimization_barrier((mine.astype(jnp.bfloat16), far))
    power = total(from_all(mine, shift_tp))
    power_b = power.astype(jnp.bfloat16)
    powers_b = split([power_b, swap_cores(power_b)])

    width = grads[0].shape[1]
    buffers = token_blocks(
        buffer_kernel,
        index,
        far + own + up + down + whole_moments,
        grads,
        [shape(rows, width, jnp.bfloat16)] * 2,
        [pltpu.VMEM((rows, width), jnp.float32)] * 2,
        "buffers",
    )
    mine, other = split(
        [contract_rows(buffers[w], powers_b[w]).astype(jnp.bfloat16) for w in range(2)]
    )
    other = swap_cores(other)

    width = mine.shape[1]
    many, few = mine.shape[0] // N_Y, RANK // N_TP // N_Y
    gram = lax.dynamic_slice_in_dim(
        contract_rows(power, power, lax.Precision.HIGHEST), tp * (RANK // N_TP), RANK // N_TP, 0
    ).astype(jnp.bfloat16)
    half = lambda *dims: jax.ShapeDtypeStruct(dims, jnp.bfloat16)
    packed = local_kernel(
        pack_kernel, [mine, other, gram], half(N_Y, many + few, width), "pack_quarters"
    )
    packed = exchange(packed, Y_GROUPS)
    many = many // N_Z
    packed = local_kernel(sum_y_kernel, [packed], half(N_Z, many + few, width), "sum_over_y")
    packed = exchange(packed, Z_GROUPS)
    mine, gram = local_kernel(
        sum_z_kernel,
        [packed],
        [half(N_Z, many, width), shape(few, width, jnp.float32)],
        "sum_over_z",
    )

    raw = exchange(mine, Z_GROUPS).reshape(N_Z * many, width)
    gram = in_order(from_all(gram, shift_y), y)
    gram = in_order(from_all(gram, shift_tp), tp)
    inverse = inverse_factor(gram)
    ortho = jnp.dot(power, inverse.T, precision=lax.Precision.HIGHEST)
    orthos = split([ortho, swap_cores(ortho)])
    raw = exchange(copies(raw, N_Y), Y_GROUPS).reshape(-1, width)

    right = jnp.dot(raw, inverse.T.astype(jnp.bfloat16), preferred_element_type=jnp.float32)
    sums = from_all(jnp.sum(right * right, axis=0, keepdims=True), shift_tp)
    right_b = right.astype(jnp.bfloat16)
    rights = split([right_b, swap_cores(right_b)])
    nexts = []
    for w in range(2):
        feedback = jnp.dot(
            orthos[w].astype(jnp.bfloat16), rights[w].T, preferred_element_type=jnp.float32
        )
        nexts.append(
            (buffers[w].astype(jnp.float32) - (1.0 - retain) / 2 * feedback).astype(jnp.bfloat16)[
                None
            ]
        )
    sums, nexts[0] = lax.optimization_barrier((sums, nexts[0]))
    scale = D / RANK**0.5 / jnp.sqrt(total(sums) + epsilon)
    scales = split([scale, swap_cores(scale)])
    scales, nexts[1] = lax.optimization_barrier((scales, nexts[1]))
    updates = [
        jnp.dot(
            (orthos[w] * scales[w]).astype(jnp.bfloat16),
            rights[w].T,
            preferred_element_type=jnp.float32,
        ).astype(jnp.bfloat16)
        for w in range(2)
    ]
    return (*updates, *nexts)


def solution(mesh):
    in_specs = (
        P(("rep", "tp"), "fsdp"),
        P("rep", "tp"),
        P(("rep", "tp"), "fsdp"),
        P("rep", "tp"),
        P("rep", "fsdp", "tp"),
        P("rep", "fsdp", "tp"),
        P("tp", None),
        P("tp", None),
    )
    out_specs = (P("fsdp", "tp"), P("fsdp", "tp"), P("rep", "fsdp", "tp"), P("rep", "fsdp", "tp"))
    return jax.shard_map(
        per_device, mesh=mesh, in_specs=in_specs, out_specs=out_specs, check_vma=False
    )
```

time: 171 us -> 158 us (0.924)
  blocking collectives: 0 us -> 18.2 us
  waiting for transfers between devices: 53.8 us -> 39.5 us
  starting transfers between devices: 58.4 us -> 46.9 us
  other arithmetic: 7.06 us -> 0.2 us
  Pallas kernels: 22.5 us -> 28.7 us
  local copies, waits for them, and re-layouts: 17 us -> 11.9 us
    ppermute x9 -> x3, waiting for transfers between devices: 21 us -> 0.35 us  [shift_y(): return lax.ppermute(x, 'fsdp', pairs)]
    all_to_all x0 -> x1, blocking collectives: none -> 18.2 us  [exchange(): return lax.all_to_all(x, 'fsdp', 0, 0, axis_index_groups=groups)]
    ppermute x9 -> x3, starting transfers between devices: 16.1 us -> 2.07 us  [shift_y(): return lax.ppermute(x, 'fsdp', pairs)]
    ppermute x15, waiting for transfers between devices: 12.2 us -> 20 us  [shift_tp(): return lax.ppermute(x, 'tp', [(i, (i + by) % N_TP) for i in range(N_TP)])]
    pallas_call x3 -> x5, Pallas kernels: 14.6 us -> 20.9 us  [the longest x2 19 us: token_blocks(): pl.pallas_call(body, grid_spec=pltpu.PrefetchScalarGridSpec(num_scalar_pr...]
    ppermute x15, starting transfers between devices: 21.5 us -> 15.5 us  [shift_tp(): return lax.ppermute(x, 'tp', [(i, (i + by) % N_TP) for i in range(N_TP)])]
    unnamed x24 -> x32, local copies, waits for them, and re-layouts: 15.9 us -> 10.8 us
    ppermute x6, starting transfers between devices: 9.16 us -> 13.5 us  [swap_cores(): return lax.ppermute(x, 'rep', [(0, 1), (1, 0)])]
  transfers between devices with their start and end apart: 32 -> 27, of which waited for: 20 -> 16; matrix products, arithmetic and copies ran while one was open for 4% -> 4% of each run, Pallas kernels for 10% -> 17%
where the time goes in v1:
time: 158 us; the launch traced here: 157 us
  starting transfers between devices  46.9 us (30%)
  waiting for transfers between devices  39.5 us (25%)
  Pallas kernels  28.7 us (18%)
  blocking collectives  18.2 us (12%)
  local copies, waits for them, and re-layouts  11.9 us (8%)
  matrix products  11.1 us (7%)
    ppermute x15, waiting for transfers between devices, shift_tp(): return lax.ppermute(x, 'tp', [(i, (i + by) % N_TP) for i in range(N_TP)])  20 us
    pallas_call x2, Pallas kernels, token_blocks(): pl.pallas_call(body, grid_spec=pltpu.PrefetchScalarGridSpec(num_scalar_pr...  19 us
    all_to_all x1, blocking collectives, exchange(): return lax.all_to_all(x, 'fsdp', 0, 0, axis_index_groups=groups)  18.2 us
    all_to_all x3, waiting for transfers between devices, exchange(): return lax.all_to_all(x, 'fsdp', 0, 0, axis_index_groups=groups)  16.3 us
    all_to_all x3, starting transfers between devices, exchange(): return lax.all_to_all(x, 'fsdp', 0, 0, axis_index_groups=groups)  15.8 us
    ppermute x15, starting transfers between devices, shift_tp(): return lax.ppermute(x, 'tp', [(i, (i + by) % N_TP) for i in range(N_TP)])  15.5 us
    ppermute x6, starting transfers between devices, swap_cores(): return lax.ppermute(x, 'rep', [(0, 1), (1, 0)])  13.5 us
    unnamed x32, local copies, waits for them, and re-layouts  10.8 us
  transfers between devices with their start and end apart: 27, of which 16 were waited for; matrix products, arithmetic and copies ran while one was open for 4% of the time, Pallas kernels for 17%

profile of v1, /device:TPU:1, one launch (start us, length us, event | category | flops | bytes accessed | tf_op | source)
XLA Modules:
  0.0 157.4 jit_solution(2115935344448466080)
XLA Ops:
  0.6 2.1 %collective-permute-start = (bf16[512,256]{1,0:T(8,128)(2,1)}, bf16[512,256]{1,0:T(8,128)(2,1)S(1)}, u32[]{:S(2)}, u32[]{:S(2)}) collective-permute-start(bf16[512,256]{1,0:T(8,128)(2,1)} %refs_2_.1), channel_id=1, source_target_pairs={{0,1},{1,2},{2,3},{3,0},{4,5},{5,6},{6,7},{7,4},{8,9},{9,10},{10,1... | collective-permute-start | bytes 786440 | tf_op jit(solution)/shard_map/ppermute | solution.py:43
  5.6 2.4 %collective-permute-done.refs_2_.refs_4_ = bf16[512,256]{1,0:T(8,128)(2,1)S(1)} collective-permute-done((bf16[512,256]{1,0:T(8,128)(2,1)}, bf16[512,256]{1,0:T(8,128)(2,1)S(1)}, u32[]{:S(2)}, u32[]{:S(2)}) %collective-permute-start) | collective-permute-done | bytes 262176 | tf_op jit(solution)/shard_map/ppermute | solution.py:43
  8.0 1.9 %collective-permute-start.4 = (bf16[512,256]{1,0:T(8,128)(2,1)S(1)}, bf16[512,256]{1,0:T(8,128)(2,1)S(1)}, u32[]{:S(2)}, u32[]{:S(2)}) collective-permute-start(bf16[512,256]{1,0:T(8,128)(2,1)S(1)} %collective-permute-done.refs_2_.refs_4_), channel_id=1, source_target_pairs={{0,1},{1,2},{2,3},{3,0},{4,5},{5,6},{6,7},{7,4},{8,9},{9,10},{10,1... | collective-permute-start | bytes 786440 | tf_op jit(solution)/shard_map/ppermute | solution.py:43
  9.9 1.6 collective-permute-start.5
  11.5 3.6 %collective-permute-done.2.refs_4_.refs_6_ = bf16[512,256]{1,0:T(8,128)(2,1)S(1)} collective-permute-done((bf16[512,256]{1,0:T(8,128)(2,1)}, bf16[512,256]{1,0:T(8,128)(2,1)S(1)}, u32[]{:S(2)}, u32[]{:S(2)}) %collective-permute-start.2) | collective-permute-done | bytes 262176 | tf_op jit(solution)/shard_map/ppermute | solution.py:43
  15.2 3.4 %copy-done = bf16[2048,2048]{1,0:T(8,128)(2,1)S(1)} copy-done((bf16[2048,2048]{1,0:T(8,128)(2,1)S(1)}, bf16[2048,2048]{1,0:T(8,128)(2,1)}, u32[]{:S(2)}) %copy-start) | copy-done | bytes 8388632
  25.4 10.8 %power_terms.1 = (bf16[512,256]{1,0:T(8,128)(2,1)S(1)}, bf16[512,256]{1,0:T(8,128)(2,1)S(1)}, f32[256,256]{1,0:T(8,128)S(1)}, f32[256,256]{1,0:T(8,128)S(1)}) custom-call(s32[4]{0:T(128)S(1)} %pad_add_fusion.index, bf16[512,256]{1,0:T(8,128)(2,1)S(1)} %copy-done.6, bf16[512,256]{1,0:T(8,128)(2,1)S(1)} %copy-done.8, ...), custom_call_target="tpu_custom_call" | custom-call | flops 1048576 | bytes 1048576 | tf_op jit(solution)/shard_map/power_terms/pallas_call | solution.py:112
  36.8 4.2 %collective-permute-start.6 = (bf16[256,256]{1,0:T(8,128)(2,1)S(1)}, bf16[256,256]{1,0:T(8,128)(2,1)S(1)}, u32[]{:S(2)}, u32[]{:S(2)}) collective-permute-start(bf16[256,256]{1,0:T(8,128)(2,1)S(1)} %get-tuple-element.48), channel_id=1, source_target_pairs={{0,128},{128,0},{1,129},{129,1},{2,130},{130,2},{3,131},{131,3},{4... | collective-permute-start | bytes 393224 | tf_op jit(solution)/shard_map/ppermute | solution.py:54
  42.1 3.4 %collective-permute-start.9 = (bf16[256,256]{1,0:T(8,128)(2,1)S(1)}, bf16[256,256]{1,0:T(8,128)(2,1)S(1)}, u32[]{:S(2)}, u32[]{:S(2)}) collective-permute-start(bf16[256,256]{1,0:T(8,128)(2,1)S(1)} %add_convert_fusion), channel_id=1, source_target_pairs={{0,3},{1,0},{2,1},{3,2},{4,7},{5,4},{6,5},{7,6},{8,11},{9,8},{10,9... | collective-permute-start | bytes 393224 | tf_op jit(solution)/shard_map/ppermute | solution.py:43
  46.2 4.7 %collective-permute-done.9 = bf16[256,256]{1,0:T(8,128)(2,1)S(1)} collective-permute-done((bf16[256,256]{1,0:T(8,128)(2,1)S(1)}, bf16[256,256]{1,0:T(8,128)(2,1)S(1)}, u32[]{:S(2)}, u32[]{:S(2)}) %collective-permute-start.9) | collective-permute-done | bytes 131104 | tf_op jit(solution)/shard_map/ppermute | solution.py:43
  51.5 3.1 %collective-permute-done.7 = bf16[256,256]{1,0:T(8,128)(2,1)S(1)} collective-permute-done((bf16[256,256]{1,0:T(8,128)(2,1)S(1)}, bf16[256,256]{1,0:T(8,128)(2,1)S(1)}, u32[]{:S(2)}, u32[]{:S(2)}) %collective-permute-start.7) | collective-permute-done | bytes 131104 | tf_op jit(solution)/shard_map/ppermute | solution.py:43
  56.1 8.3 %buffers.1 = (bf16[256,2048]{1,0:T(8,128)(2,1)S(1)}, bf16[256,2048]{1,0:T(8,128)(2,1)S(1)}) custom-call(s32[4]{0:T(128)S(1)} %pad_add_fusion.index, bf16[512,256]{1,0:T(8,128)(2,1)S(1)} %collective-permute-done.4.refs_0_, bf16[512,256]{1,0:T(8,128)(2,1)S(1)} %collective-permute-done.5.refs_1_, bf16[512,256]{1,0:T(8,128)(2,1)S(1)} %copy-done.7, ...), custom_call_target="tpu_custom_call" | custom-call | flops 1048576 | bytes 1048576 | tf_op jit(solution)/shard_map/buffers/pallas_call | solution.py:112
  66.4 1.6 %fusion.15 = bf16[256,256]{1,0:T(8,128)(2,1)S(1)} fusion(bf16[256,256]{1,0:T(8,128)(2,1)S(1)} %collective-permute-done.9, bf16[256,256]{1,0:T(8,128)(2,1)S(1)} %collective-permute-done.8, bf16[256,256]{1,0:T(8,128)(2,1)} %copy-done.14, bf16[256,256]{1,0:T(8,128)(2,1)S(1)} %add_convert_fusion), kind=kOutput, calls=%fused_computation.50 | convolution fusion | flops 201785344 | bytes 655360 | tf_op jit(solution)/shard_map/dot_general | solution.py:28
  69.5 18.2 %all_to_all.20.pieces = bf16[4,528,256]{2,1,0:T(8,128)(2,1)S(1)} all-to-all(bf16[4,528,256]{2,1,0:T(8,128)(2,1)S(1)} %pack_quarters.1), channel_id=1, replica_groups={{0,32,64,96},{4,36,68,100},{8,40,72,104},{12,44,76,108},{16,48,80,112},..., dimensions={0} | all-to-all | bytes 2162688 | tf_op jit(solution)/shard_map/all_to_all | solution.py:87
  88.5 8.2 %all-to-all-start.1 = ((bf16[8,80,256]{2,1,0:T(8,128)(2,1)}), bf16[8,80,256]{2,1,0:T(8,128)(2,1)S(1)}, u32[]{:S(2)}, u32[]{:S(2)}) async-start(bf16[8,80,256]{2,1,0:T(8,128)(2,1)} %sum_over_y.1), calls=%async_computation.1 | async-start | bytes 655360 | tf_op jit(solution)/shard_map/all_to_all | solution.py:87
  96.7 11.2 %all-to-all-done.1.pieces = bf16[8,80,256]{2,1,0:T(8,128)(2,1)S(1)} async-done(((bf16[8,80,256]{2,1,0:T(8,128)(2,1)}), bf16[8,80,256]{2,1,0:T(8,128)(2,1)S(1)}, u32[]{:S(2)}, u32[]{:S(2)}) %all-to-all-start.1) | async-done | bytes 327712 | tf_op jit(solution)/shard_map/all_to_all | solution.py:87
  110.6 3.4 %all-to-all-start.2 = ((bf16[8,64,256]{2,1,0:T(8,128)(2,1)}), bf16[8,64,256]{2,1,0:T(8,128)(2,1)S(1)}, u32[]{:S(2)}, u32[]{:S(2)}) async-start(bf16[8,64,256]{2,1,0:T(8,128)(2,1)} %get-tuple-element.33), calls=%async_computation.2 | async-start | bytes 524288 | tf_op jit(solution)/shard_map/all_to_all | solution.py:87
  116.1 4.1 %collective-permute-done.15 = f32[64,256]{1,0:T(8,128)S(1)} collective-permute-done((f32[64,256]{1,0:T(8,128)S(1)}, f32[64,256]{1,0:T(8,128)S(1)}, u32[]{:S(2)}, u32[]{:S(2)}) %collective-permute-start.15) | collective-permute-done | bytes 65568 | tf_op jit(solution)/shard_map/ppermute | solution.py:43
  120.2 3.2 %all-to-all-done.2 = bf16[8,64,256]{2,1,0:T(8,128)(2,1)S(1)} async-done(((bf16[8,64,256]{2,1,0:T(8,128)(2,1)}), bf16[8,64,256]{2,1,0:T(8,128)(2,1)S(1)}, u32[]{:S(2)}, u32[]{:S(2)}) %all-to-all-start.2) | async-done | bytes 262176 | tf_op jit(solution)/shard_map/all_to_all | solution.py:87
  124.5 4.2 %all-to-all-start.3 = ((bf16[4,512,256]{2,1,0:T(8,128)(2,1)}), bf16[4,512,256]{2,1,0:T(8,128)(2,1)S(1)}, u32[]{:S(2)}, u32[]{:S(2)}) async-start(bf16[4,512,256]{2,1,0:T(8,128)(2,1)} %broadcast_in_dim.59), calls=%async_computation.3 | async-start | bytes 2097152 | tf_op jit(solution)/shard_map/all_to_all | solution.py:87
  128.7 7.8 %inverse_factor.1 = f32[256,256]{1,0:T(8,128)S(1)} custom-call(f32[256,256]{1,0:T(8,128)S(1)} %bitcast.48), custom_call_target="tpu_custom_call" | custom-call | flops 8000000000 | bytes 1048576 | tf_op jit(solution)/shard_map/inverse_factor/pallas_call | solution.py:252
  136.6 1.9 %all-to-all-done.3 = bf16[4,512,256]{2,1,0:T(8,128)(2,1)S(1)} async-done(((bf16[4,512,256]{2,1,0:T(8,128)(2,1)}), bf16[4,512,256]{2,1,0:T(8,128)(2,1)S(1)}, u32[]{:S(2)}, u32[]{:S(2)}) %all-to-all-start.3) | async-done | bytes 1048608 | tf_op jit(solution)/shard_map/all_to_all | solution.py:87
  139.1 6.4 %collective-permute-start.22 = (bf16[2048,256]{1,0:T(8,128)(2,1)S(1)}, bf16[2048,256]{1,0:T(8,128)(2,1)S(1)}, u32[]{:S(2)}, u32[]{:S(2)}) collective-permute-start(bf16[2048,256]{1,0:T(8,128)(2,1)S(1)} %get-tuple-element.43), channel_id=1, source_target_pairs={{0,128},{128,0},{1,129},{129,1},{2,130},{130,2},{3,131},{131,3},{4... | collective-permute-start | bytes 3145736 | tf_op jit(solution)/shard_map/ppermute | solution.py:54
  151.0 1.9 %collective-permute-start.23 = (f32[1,256]{1,0:T(1,128)S(1)}, f32[1,256]{1,0:T(1,128)S(1)}, u32[]{:S(2)}, u32[]{:S(2)}) collective-permute-start(f32[1,256]{1,0:T(1,128)S(1)} %rsqrt_multiply_fusion), channel_id=1, source_target_pairs={{0,128},{128,0},{1,129},{129,1},{2,130},{130,2},{3,131},{131,3},{4... | collective-permute-start | bytes 3080 | tf_op jit(solution)/shard_map/ppermute | solution.py:54
  (97 shorter events, 35.0 us)
Async XLA Ops:
  0.6 7.4 %collective-permute-start = (bf16[512,256]{1,0:T(8,128)(2,1)}, bf16[512,256]{1,0:T(8,128)(2,1)S(1)}, u32[]{:S(2)}, u32[]{:S(2)}) collective-permute-start(bf16[512,256]{1,0:T(8,128)(2,1)} %refs_2_.1), channel_id=1, source_target_pairs={{0,1},{1,2},{2,3},{3,0},{4,5},{5,6},{6,7},{7,4},{8,9},{9,10},{10,1... | collective-permute-start | bytes 786440 | tf_op jit(solution)/shard_map/ppermute | solution.py:43
  2.7 7.1 %collective-permute-start.3 = (bf16[512,256]{1,0:T(8,128)(2,1)}, bf16[512,256]{1,0:T(8,128)(2,1)S(1)}, u32[]{:S(2)}, u32[]{:S(2)}) collective-permute-start(bf16[512,256]{1,0:T(8,128)(2,1)} %refs_3_.1), channel_id=1, source_target_pairs={{0,3},{1,0},{2,1},{3,2},{4,7},{5,4},{6,5},{7,6},{8,11},{9,8},{10,9... | collective-permute-start | bytes 786440 | tf_op jit(solution)/shard_map/ppermute | solution.py:43
  4.1 11.0 %collective-permute-start.2 = (bf16[512,256]{1,0:T(8,128)(2,1)}, bf16[512,256]{1,0:T(8,128)(2,1)S(1)}, u32[]{:S(2)}, u32[]{:S(2)}) collective-permute-start(bf16[512,256]{1,0:T(8,128)(2,1)} %refs_2_.1), channel_id=1, source_target_pairs={{0,3},{1,0},{2,1},{3,2},{4,7},{5,4},{6,5},{7,6},{8,11},{9,8},{10,9... | collective-permute-start | bytes 786440 | tf_op jit(solution)/shard_map/ppermute | solution.py:43
  5.5 9.7 %collective-permute-start.1 = (bf16[512,256]{1,0:T(8,128)(2,1)}, bf16[512,256]{1,0:T(8,128)(2,1)S(1)}, u32[]{:S(2)}, u32[]{:S(2)}) collective-permute-start(bf16[512,256]{1,0:T(8,128)(2,1)} %refs_3_.1), channel_id=1, source_target_pairs={{0,1},{1,2},{2,3},{3,0},{4,5},{5,6},{6,7},{7,4},{8,9},{9,10},{10,1... | collective-permute-start | bytes 786440 | tf_op jit(solution)/shard_map/ppermute | solution.py:43
  8.0 28.2 %collective-permute-start.4 = (bf16[512,256]{1,0:T(8,128)(2,1)S(1)}, bf16[512,256]{1,0:T(8,128)(2,1)S(1)}, u32[]{:S(2)}, u32[]{:S(2)}) collective-permute-start(bf16[512,256]{1,0:T(8,128)(2,1)S(1)} %collective-permute-done.refs_2_.refs_4_), channel_id=1, source_target_pairs={{0,1},{1,2},{2,3},{3,0},{4,5},{5,6},{6,7},{7,4},{8,9},{9,10},{10,1... | collective-permute-start | bytes 786440 | tf_op jit(solution)/shard_map/ppermute | solution.py:43
  9.9 26.7 %collective-permute-start.5 = (bf16[512,256]{1,0:T(8,128)(2,1)S(1)}, bf16[512,256]{1,0:T(8,128)(2,1)S(1)}, u32[]{:S(2)}, u32[]{:S(2)}) collective-permute-start(bf16[512,256]{1,0:T(8,128)(2,1)S(1)} %collective-permute-done.3.refs_5_.refs_7_), channel_id=1, source_target_pairs={{0,3},{1,0},{2,1},{3,2},{4,7},{5,4},{6,5},{7,6},{8,11},{9,8},{10,9... | collective-permute-start | bytes 786440 | tf_op jit(solution)/shard_map/ppermute | solution.py:43
  36.8 5.2 %collective-permute-start.6 = (bf16[256,256]{1,0:T(8,128)(2,1)S(1)}, bf16[256,256]{1,0:T(8,128)(2,1)S(1)}, u32[]{:S(2)}, u32[]{:S(2)}) collective-permute-start(bf16[256,256]{1,0:T(8,128)(2,1)S(1)} %get-tuple-element.48), channel_id=1, source_target_pairs={{0,128},{128,0},{1,129},{129,1},{2,130},{130,2},{3,131},{131,3},{4... | collective-permute-start | bytes 393224 | tf_op jit(solution)/shard_map/ppermute | solution.py:54
  42.1 8.8 %collective-permute-start.9 = (bf16[256,256]{1,0:T(8,128)(2,1)S(1)}, bf16[256,256]{1,0:T(8,128)(2,1)S(1)}, u32[]{:S(2)}, u32[]{:S(2)}) collective-permute-start(bf16[256,256]{1,0:T(8,128)(2,1)S(1)} %add_convert_fusion), channel_id=1, source_target_pairs={{0,3},{1,0},{2,1},{3,2},{4,7},{5,4},{6,5},{7,6},{8,11},{9,8},{10,9... | collective-permute-start | bytes 393224 | tf_op jit(solution)/shard_map/ppermute | solution.py:43
  45.5 6.0 %collective-permute-start.8 = (bf16[256,256]{1,0:T(8,128)(2,1)S(1)}, bf16[256,256]{1,0:T(8,128)(2,1)S(1)}, u32[]{:S(2)}, u32[]{:S(2)}) collective-permute-start(bf16[256,256]{1,0:T(8,128)(2,1)S(1)} %add_convert_fusion), channel_id=1, source_target_pairs={{0,2},{1,3},{2,0},{3,1},{4,6},{5,7},{6,4},{7,5},{8,10},{9,11},{10,... | collective-permute-start | bytes 393224 | tf_op jit(solution)/shard_map/ppermute | solution.py:43
  45.5 9.1 %collective-permute-start.7 = (bf16[256,256]{1,0:T(8,128)(2,1)S(1)}, bf16[256,256]{1,0:T(8,128)(2,1)S(1)}, u32[]{:S(2)}, u32[]{:S(2)}) collective-permute-start(bf16[256,256]{1,0:T(8,128)(2,1)S(1)} %add_convert_fusion), channel_id=1, source_target_pairs={{0,1},{1,2},{2,3},{3,0},{4,5},{5,6},{6,7},{7,4},{8,9},{9,10},{10,1... | collective-permute-start | bytes 393224 | tf_op jit(solution)/shard_map/ppermute | solution.py:43
  55.3 9.1 %collective-permute-start.10 = (bf16[256,256]{1,0:T(8,128)(2,1)S(1)}, bf16[256,256]{1,0:T(8,128)(2,1)S(1)}, u32[]{:S(2)}, u32[]{:S(2)}) collective-permute-start(bf16[256,256]{1,0:T(8,128)(2,1)S(1)} %fusion.16), channel_id=1, source_target_pairs={{0,128},{128,0},{1,129},{129,1},{2,130},{130,2},{3,131},{131,3},{4... | collective-permute-start | bytes 393224 | tf_op jit(solution)/shard_map/ppermute | solution.py:54
  88.5 19.3 %all-to-all-start.1 = ((bf16[8,80,256]{2,1,0:T(8,128)(2,1)}), bf16[8,80,256]{2,1,0:T(8,128)(2,1)S(1)}, u32[]{:S(2)}, u32[]{:S(2)}) async-start(bf16[8,80,256]{2,1,0:T(8,128)(2,1)} %sum_over_y.1), calls=%async_computation.1 | async-start | bytes 655360 | tf_op jit(solution)/shard_map/all_to_all | solution.py:87
  108.6 5.9 %collective-permute-start.14 = (f32[16,256]{1,0:T(8,128)S(1)}, f32[16,256]{1,0:T(8,128)S(1)}, u32[]{:S(2)}, u32[]{:S(2)}) collective-permute-start(f32[16,256]{1,0:T(8,128)S(1)} %get-tuple-element.32), channel_id=1, source_target_pairs={{0,96},{4,100},{8,104},{12,108},{16,112},{20,116},{24,120},{28,124... | collective-permute-start | bytes 49160 | tf_op jit(solution)/shard_map/ppermute | solution.py:50
  109.5 5.0 %collective-permute-start.13 = (f32[16,256]{1,0:T(8,128)S(1)}, f32[16,256]{1,0:T(8,128)S(1)}, u32[]{:S(2)}, u32[]{:S(2)}) collective-permute-start(f32[16,256]{1,0:T(8,128)S(1)} %get-tuple-element.32), channel_id=1, source_target_pairs={{0,64},{4,68},{8,72},{12,76},{16,80},{20,84},{24,88},{28,92},{32,9... | collective-permute-start | bytes 49160 | tf_op jit(solution)/shard_map/ppermute | solution.py:50
  110.6 3.8 %collective-permute-start.12 = (f32[16,256]{1,0:T(8,128)S(1)}, f32[16,256]{1,0:T(8,128)S(1)}, u32[]{:S(2)}, u32[]{:S(2)}) collective-permute-start(f32[16,256]{1,0:T(8,128)S(1)} %get-tuple-element.32), channel_id=1, source_target_pairs={{0,32},{4,36},{8,40},{12,44},{16,48},{20,52},{24,56},{28,60},{32,6... | collective-permute-start | bytes 49160 | tf_op jit(solution)/shard_map/ppermute | solution.py:50
  110.6 12.8 %all-to-all-start.2 = ((bf16[8,64,256]{2,1,0:T(8,128)(2,1)}), bf16[8,64,256]{2,1,0:T(8,128)(2,1)S(1)}, u32[]{:S(2)}, u32[]{:S(2)}) async-start(bf16[8,64,256]{2,1,0:T(8,128)(2,1)} %get-tuple-element.33), calls=%async_computation.2 | async-start | bytes 524288 | tf_op jit(solution)/shard_map/all_to_all | solution.py:87
  114.5 14.2 %collective-permute-start.17 = (f32[64,256]{1,0:T(8,128)S(1)}, f32[64,256]{1,0:T(8,128)S(1)}, u32[]{:S(2)}, u32[]{:S(2)}) collective-permute-start(f32[64,256]{1,0:T(8,128)S(1)} %bitcast.51), channel_id=1, source_target_pairs={{0,3},{1,0},{2,1},{3,2},{4,7},{5,4},{6,5},{7,6},{8,11},{9,8},{10,9... | collective-permute-start | bytes 196616 | tf_op jit(solution)/shard_map/ppermute | solution.py:43
  114.9 5.3 %collective-permute-start.16 = (f32[64,256]{1,0:T(8,128)S(1)}, f32[64,256]{1,0:T(8,128)S(1)}, u32[]{:S(2)}, u32[]{:S(2)}) collective-permute-start(f32[64,256]{1,0:T(8,128)S(1)} %bitcast.52), channel_id=1, source_target_pairs={{0,2},{1,3},{2,0},{3,1},{4,6},{5,7},{6,4},{7,5},{8,10},{9,11},{10,... | collective-permute-start | bytes 196616 | tf_op jit(solution)/shard_map/ppermute | solution.py:43
  115.2 5.0 %collective-permute-start.15 = (f32[64,256]{1,0:T(8,128)S(1)}, f32[64,256]{1,0:T(8,128)S(1)}, u32[]{:S(2)}, u32[]{:S(2)}) collective-permute-start(f32[64,256]{1,0:T(8,128)S(1)} %bitcast.53), channel_id=1, source_target_pairs={{0,1},{1,2},{2,3},{3,0},{4,5},{5,6},{6,7},{7,4},{8,9},{9,10},{10,1... | collective-permute-start | bytes 196616 | tf_op jit(solution)/shard_map/ppermute | solution.py:43
  124.5 14.0 %all-to-all-start.3 = ((bf16[4,512,256]{2,1,0:T(8,128)(2,1)}), bf16[4,512,256]{2,1,0:T(8,128)(2,1)S(1)}, u32[]{:S(2)}, u32[]{:S(2)}) async-start(bf16[4,512,256]{2,1,0:T(8,128)(2,1)} %broadcast_in_dim.59), calls=%async_computation.3 | async-start | bytes 2097152 | tf_op jit(solution)/shard_map/all_to_all | solution.py:87
  139.1 9.1 %collective-permute-start.22 = (bf16[2048,256]{1,0:T(8,128)(2,1)S(1)}, bf16[2048,256]{1,0:T(8,128)(2,1)S(1)}, u32[]{:S(2)}, u32[]{:S(2)}) collective-permute-start(bf16[2048,256]{1,0:T(8,128)(2,1)S(1)} %get-tuple-element.43), channel_id=1, source_target_pairs={{0,128},{128,0},{1,129},{129,1},{2,130},{130,2},{3,131},{131,3},{4... | collective-permute-start | bytes 3145736 | tf_op jit(solution)/shard_map/ppermute | solution.py:54
  146.1 3.6 %collective-permute-start.21 = (f32[1,256]{1,0:T(1,128)S(1)}, f32[1,256]{1,0:T(1,128)S(1)}, u32[]{:S(2)}, u32[]{:S(2)}) collective-permute-start(f32[1,256]{1,0:T(1,128)S(1)} %bitcast.57), channel_id=1, source_target_pairs={{0,3},{1,0},{2,1},{3,2},{4,7},{5,4},{6,5},{7,6},{8,11},{9,8},{10,9... | collective-permute-start | bytes 3080 | tf_op jit(solution)/shard_map/ppermute | solution.py:43
  146.5 3.9 %collective-permute-start.20 = (f32[1,256]{1,0:T(1,128)S(1)}, f32[1,256]{1,0:T(1,128)S(1)}, u32[]{:S(2)}, u32[]{:S(2)}) collective-permute-start(f32[1,256]{1,0:T(1,128)S(1)} %bitcast.58), channel_id=1, source_target_pairs={{0,2},{1,3},{2,0},{3,1},{4,6},{5,7},{6,4},{7,5},{8,10},{9,11},{10,... | collective-permute-start | bytes 3080 | tf_op jit(solution)/shard_map/ppermute | solution.py:43
  146.8 4.2 %collective-permute-start.19 = (f32[1,256]{1,0:T(1,128)S(1)}, f32[1,256]{1,0:T(1,128)S(1)}, u32[]{:S(2)}, u32[]{:S(2)}) collective-permute-start(f32[1,256]{1,0:T(1,128)S(1)} %bitcast.59), channel_id=1, source_target_pairs={{0,1},{1,2},{2,3},{3,0},{4,5},{5,6},{6,7},{7,4},{8,9},{9,10},{10,1... | collective-permute-start | bytes 3080 | tf_op jit(solution)/shard_map/ppermute | solution.py:43
  (19 other events, 147.2 us)

commit v2 on v1

--- a/solution.py
+++ b/solution.py
@@ -87,10 +87,6 @@
     return lax.all_to_all(x, "fsdp", 0, 0, axis_index_groups=groups)
 
 
-def copies(x, n):
-    return jnp.broadcast_to(x[None], (n,) + x.shape)
-
-
 def whole(a):
     return pl.BlockSpec(a.shape, lambda *_: (0,) * len(a.shape), pipeline_mode=pl.Buffered(1))
 
@@ -106,7 +102,7 @@
     )(*operands)
 
 
-def token_blocks(body, index, small, grads, results, scratch, name):
+def token_blocks(body, index, small, grads, results, specs, scratch, cost, name):
     count = grads[0].shape[0] // N_TP
     block = lambda a: pl.BlockSpec((count, a.shape[1]), lambda s, i: (i[s], 0))
     return pl.pallas_call(
@@ -115,37 +111,25 @@
             num_scalar_prefetch=1,
             grid=(N_TP,),
             in_specs=[whole(a) for a in small] + [block(a) for a in grads],
-            out_specs=[
-                pl.BlockSpec(a.shape, lambda *_, n=len(a.shape): (0,) * n) for a in results
-            ],
+            out_specs=specs,
             scratch_shapes=scratch,
         ),
         out_shape=results,
         compiler_params=pltpu.CompilerParams(
-            dimension_semantics=("arbitrary",), vmem_limit_bytes=32 << 20
+            dimension_semantics=("arbitrary",), vmem_limit_bytes=56 << 20
         ),
-        cost_estimate=pl.CostEstimate(flops=1 << 20, bytes_accessed=1 << 20, transcendentals=0),
+        cost_estimate=pl.CostEstimate(flops=cost, bytes_accessed=1 << 20, transcendentals=0),
         name=name,
     )(index, *small, *grads)
 
 
-def power_kernel(index, *refs):
-    step = pl.program_id(0)
-    for w in range(2):
-        own, up, down, moment, basis, grad, far, near = refs[w::2]
-        product = jnp.dot(grad[...], basis[...], preferred_element_type=jnp.float32)
-        product = product.astype(jnp.bfloat16)
-
-        @pl.when(step == 0)
-        def _():
-            far[...] = product
-            near[...] = jnp.dot(moment[0], basis[...], preferred_element_type=jnp.float32)
-
-        for at, tokens in ((1, own), (2, up), (3, down)):
-
-            @pl.when(step == at)
-            def _():
-                near[...] += contract_rows(tokens[...], product)
+def product_kernel(index, moment, basis, grad, product, near):
+    term = jnp.dot(grad[...], basis[...], preferred_element_type=jnp.float32)
+    product[...] = term.astype(jnp.bfloat16)
+
+    @pl.when(pl.program_id(0) == 0)
+    def _():
+        near[...] = jnp.dot(moment[0], basis[...], preferred_element_type=jnp.float32)
 
 
 def buffer_kernel(index, *refs):
@@ -173,6 +157,80 @@
             buffer[...] = acc[...].astype(jnp.bfloat16)
 
 
+def near_kernel(index, *refs):
+    for w in range(2):
+        own, up, down, product_own, product_up, product_down, base, out = refs[w::2]
+        out[...] = (
+            base[...]
+            + contract_rows(own[...], product_own[...])
+            + contract_rows(up[...], product_up[...])
+            + contract_rows(down[...], product_down[...])
+        )
+
+
+def far_kernel(index, *refs):
+    mine, other = refs[6:]
+    query, output = [
+        near[...] + contract_rows(far[...], product[...])
+        for far, product, near in (refs[0:6:2], refs[1:6:2])
+    ]
+    first = index[N_TP] == 0
+    mine[...] = jnp.where(first, query, output)
+    other[...] = jnp.where(first, output, query).astype(jnp.bfloat16)
+
+
+def indexed_kernel(body, index, operands, results, name, grid=(1,), limit=16 << 20):
+    spec = lambda block, place: pl.BlockSpec(block, place)
+    return pl.pallas_call(
+        body,
+        grid_spec=pltpu.PrefetchScalarGridSpec(
+            num_scalar_prefetch=1,
+            grid=grid,
+            in_specs=[spec(block, place) for _, block, place in operands],
+            out_specs=[spec(block, place) for _, block, place in results],
+        ),
+        out_shape=[shape for shape, _, _ in results],
+        compiler_params=pltpu.CompilerParams(
+            dimension_semantics=("arbitrary",), vmem_limit_bytes=limit
+        ),
+        cost_estimate=pl.CostEstimate(flops=1 << 28, bytes_accessed=1 << 20, transcendentals=0),
+        name=name,
+    )(index, *[a for a, _, _ in operands])
+
+
+def all_of(a):
+    return (a, a.shape, lambda s, i: (0,) * len(a.shape))
+
+
+def feedback_kernel(index, right_mine, right_other, *refs):
+    first = index[N_TP] == 0
+    sides = (right_mine[...], right_other[...])
+    for w in range(2):
+        ortho, buffer, out = refs[w::2]
+        right = jnp.where(first, sides[w], sides[1 - w])
+        term = lax.dot_general(
+            ortho[...].astype(jnp.bfloat16),
+            right,
+            (((1,), (1,)), ((), ())),
+            preferred_element_type=jnp.float32,
+        )
+        out[0] = (buffer[...].astype(jnp.float32) - (1.0 - retain) / 2 * term).astype(jnp.bfloat16)
+
+
+def update_kernel(index, right_mine, right_other, *refs):
+    first = index[N_TP] == 0
+    sides = (right_mine[...], right_other[...])
+    for w in range(2):
+        ortho, scale, out = refs[w::2]
+        right = jnp.where(first, sides[w], sides[1 - w])
+        out[...] = lax.dot_general(
+            (ortho[...] * scale[...]).astype(jnp.bfloat16),
+            right,
+            (((1,), (1,)), ((), ())),
+            preferred_element_type=jnp.float32,
+        ).astype(jnp.bfloat16)
+
+
 def pack_kernel(mine, other, gram, out):
     many, few = mine.shape[0] // N_Y, gram.shape[0] // N_Y
     for j in range(N_Y):
@@ -182,23 +240,41 @@
         out[j, many:] = gram[j * few : (j + 1) * few]
 
 
+def both_halves(x):
+    high = x.astype(jnp.bfloat16).astype(jnp.float32)
+    return jnp.concatenate([high, x - high], axis=0).astype(jnp.bfloat16)
+
+
 def sum_y_kernel(pieces, out):
-    n, rows, _ = out.shape
-    few = RANK // N_TP // N_Y
-    many = rows - few
+    few = RANK // N_Y // N_Z
+    many = out.shape[1] - 2 * few
     add = lambda at, size: total([pieces[j, at : at + size] for j in range(N_Y)])
-    gram = add(n * many, few).astype(jnp.bfloat16)
-    for j in range(n):
+    gram = add(N_Z * many, N_Z * few)
+    for j in range(N_Z):
         out[j, :many] = add(j * many, many).astype(jnp.bfloat16)
+        out[j, many:] = both_halves(gram[j * few : (j + 1) * few])
+
+
+def sum_z_kernel(pieces, out):
+    few = RANK // N_Y // N_Z
+    many = out.shape[1] - 2 * few
+    rows = total([pieces[j, :many] for j in range(N_Z)]).astype(jnp.bfloat16)
+    gram = total([pieces[j, many:] for j in range(N_Z)])
+    gram = both_halves(gram[:few] + gram[few:])
+    for j in range(N_Z):
+        out[j, :many] = rows
         out[j, many:] = gram
 
 
-def sum_z_kernel(pieces, out, gram):
-    many = out.shape[1]
-    rows = total([pieces[j, :many] for j in range(N_Z)]).astype(jnp.bfloat16)
+def unpack_kernel(pieces, out, gram):
+    few = RANK // N_Y // N_Z
+    many = pieces.shape[1] - 2 * few
     for j in range(N_Z):
-        out[j] = rows
-    gram[...] = total([pieces[j, many:] for j in range(N_Z)])
+        rows = pieces[j, :many]
+        for k in range(N_Y):
+            out[k, j * many : (j + 1) * many] = rows
+        pair = pieces[j, many:].astype(jnp.float32)
+        gram[j * few : (j + 1) * few] = pair[:few] + pair[few:]
 
 
 def dot_halves(a, b, dims):
@@ -284,98 +360,125 @@
     bases = [basis_query, basis_output]
     tokens = tokens_by_distance(input_query, input_output)
 
-    index = jnp.stack([(tp - by) % N_TP for by in (2, 0, 1, 3)]).astype(jnp.int32)
-    pairs = list(zip(*tokens))
-    own, up, far, down = [list(pair) for pair in pairs]
-    whole_moments = [moment_query, moment_output]
-    rows = own[0].shape[1]
-    shape = lambda r, c, dtype: jax.ShapeDtypeStruct((r, c), dtype)
-    ahead = token_blocks(
-        power_kernel,
+    index = jnp.stack([(tp - by) % N_TP for by in (2, 0, 1, 3)] + [lax.axis_index("rep")])
+    index = index.astype(jnp.int32)
+    own, up, far, down = [list(pair) for pair in zip(*tokens)]
+    rows, count = own[0].shape[1], own[0].shape[0]
+    shape = lambda dtype, *dims: jax.ShapeDtypeStruct(dims, dtype)
+    square = shape(jnp.float32, rows, RANK)
+    moments = [moment_query, moment_output]
+    products, bases_terms = [], []
+    for w in range(2):
+        grad = grads[w] if w == 0 else lax.optimization_barrier((grads[w], up[0], down[1]))[0]
+        product, term = token_blocks(
+            product_kernel,
+            index,
+            [moments[w], bases[w]],
+            [grad],
+            [shape(jnp.bfloat16, N_TP * count, RANK), square],
+            [
+                pl.BlockSpec((count, RANK), lambda s, i: (i[s], 0)),
+                pl.BlockSpec(square.shape, lambda s, i: (0, 0)),
+            ],
+            [],
+            1 << 20,
+            "basis_products",
+        )
+        products.append(product)
+        bases_terms.append(term)
+    part = lambda a, at: (a, (count, RANK), lambda s, i: (i[at], 0))
+    near = indexed_kernel(
+        near_kernel,
         index,
-        own + up + down + whole_moments + bases,
-        grads,
-        [shape(own[0].shape[0], RANK, jnp.bfloat16)] * 2 + [shape(rows, RANK, jnp.float32)] * 2,
-        [],
-        "power_terms",
-    )
-    powers = [ahead[2 + w] + contract_rows(far[w], ahead[w]) for w in range(2)]
-    mine, other = split(powers)
-    mine = mine + swap_cores(other.astype(jnp.bfloat16)).astype(jnp.float32)
+        [all_of(a) for a in own + up + down]
+        + [part(a, at) for at in (1, 2, 3) for a in products]
+        + [all_of(a) for a in bases_terms],
+        [all_of(square)] * 2,
+        "near_tokens",
+    )
+    mine, other = indexed_kernel(
+        far_kernel,
+        index,
+        [all_of(a) for a in far] + [part(a, 0) for a in products] + [all_of(a) for a in near],
+        [all_of(square), all_of(shape(jnp.bfloat16, rows, RANK))],
+        "far_tokens",
+    )
+    mine = mine + swap_cores(other).astype(jnp.float32)
     mine, far = lax.optimization_barrier((mine.astype(jnp.bfloat16), far))
-    power = total(from_all(mine, shift_tp))
-    power_b = power.astype(jnp.bfloat16)
-    powers_b = split([power_b, swap_cores(power_b)])
-
     width = grads[0].shape[1]
     buffers = token_blocks(
         buffer_kernel,
         index,
-        far + own + up + down + whole_moments,
+        far + own + up + down + moments,
         grads,
-        [shape(rows, width, jnp.bfloat16)] * 2,
+        [shape(jnp.bfloat16, rows, width)] * 2,
+        [pl.BlockSpec((rows, width), lambda s, i: (0, 0))] * 2,
         [pltpu.VMEM((rows, width), jnp.float32)] * 2,
+        1 << 33,
         "buffers",
     )
+    parts, buffers = lax.optimization_barrier((from_all(mine, shift_tp), buffers))
+    power = total(parts)
+    power_b = power.astype(jnp.bfloat16)
+    powers_b = split([power_b, swap_cores(power_b)])
     mine, other = split(
         [contract_rows(buffers[w], powers_b[w]).astype(jnp.bfloat16) for w in range(2)]
     )
     other = swap_cores(other)
 
     width = mine.shape[1]
-    many, few = mine.shape[0] // N_Y, RANK // N_TP // N_Y
-    gram = lax.dynamic_slice_in_dim(
-        contract_rows(power, power, lax.Precision.HIGHEST), tp * (RANK // N_TP), RANK // N_TP, 0
-    ).astype(jnp.bfloat16)
-    half = lambda *dims: jax.ShapeDtypeStruct(dims, jnp.bfloat16)
+    many, few = mine.shape[0] // N_Y, RANK // N_Y
+    gram = contract_rows(power, power, lax.Precision.HIGHEST).astype(jnp.bfloat16)
+    half = lambda *dims: shape(jnp.bfloat16, *dims)
     packed = local_kernel(
         pack_kernel, [mine, other, gram], half(N_Y, many + few, width), "pack_quarters"
     )
     packed = exchange(packed, Y_GROUPS)
-    many = many // N_Z
-    packed = local_kernel(sum_y_kernel, [packed], half(N_Z, many + few, width), "sum_over_y")
+    sent = half(N_Z, (many + 2 * few) // N_Z, width)
+    packed = local_kernel(sum_y_kernel, [packed], sent, "sum_over_y")
     packed = exchange(packed, Z_GROUPS)
-    mine, gram = local_kernel(
-        sum_z_kernel,
+    packed = local_kernel(sum_z_kernel, [packed], sent, "sum_over_z")
+
+    packed = exchange(packed, Z_GROUPS)
+    raw, gram = local_kernel(
+        unpack_kernel,
         [packed],
-        [half(N_Z, many, width), shape(few, width, jnp.float32)],
-        "sum_over_z",
-    )
-
-    raw = exchange(mine, Z_GROUPS).reshape(N_Z * many, width)
+        [half(N_Y, many, width), shape(jnp.float32, few, width)],
+        "unpack_rows",
+    )
     gram = in_order(from_all(gram, shift_y), y)
-    gram = in_order(from_all(gram, shift_tp), tp)
     inverse = inverse_factor(gram)
     ortho = jnp.dot(power, inverse.T, precision=lax.Precision.HIGHEST)
     orthos = split([ortho, swap_cores(ortho)])
-    raw = exchange(copies(raw, N_Y), Y_GROUPS).reshape(-1, width)
+    raw = exchange(raw, Y_GROUPS).reshape(-1, width)
 
     right = jnp.dot(raw, inverse.T.astype(jnp.bfloat16), preferred_element_type=jnp.float32)
     sums = from_all(jnp.sum(right * right, axis=0, keepdims=True), shift_tp)
     right_b = right.astype(jnp.bfloat16)
-    rights = split([right_b, swap_cores(right_b)])
-    nexts = []
-    for w in range(2):
-        feedback = jnp.dot(
-            orthos[w].astype(jnp.bfloat16), rights[w].T, preferred_element_type=jnp.float32
-        )
-        nexts.append(
-            (buffers[w].astype(jnp.float32) - (1.0 - retain) / 2 * feedback).astype(jnp.bfloat16)[
-                None
-            ]
-        )
-    sums, nexts[0] = lax.optimization_barrier((sums, nexts[0]))
+    rights = [right_b, swap_cores(right_b)]
+    steps = grads[0].shape[1] // COLUMNS
+    tall = lambda a: (a, (COLUMNS, a.shape[1]), lambda s, i: (s, 0))
+    wide = lambda a: (a, (rows, COLUMNS), lambda s, i: (0, s))
+    result = shape(jnp.bfloat16, 1, rows, grads[0].shape[1])
+    nexts = indexed_kernel(
+        feedback_kernel,
+        index,
+        [tall(a) for a in rights] + [all_of(a) for a in orthos] + [wide(a) for a in buffers],
+        [(result, (1, rows, COLUMNS), lambda s, i: (0, 0, s))] * 2,
+        "feedback",
+        grid=(steps,),
+    )
+    sums, nexts = lax.optimization_barrier((sums, nexts))
     scale = D / RANK**0.5 / jnp.sqrt(total(sums) + epsilon)
     scales = split([scale, swap_cores(scale)])
-    scales, nexts[1] = lax.optimization_barrier((scales, nexts[1]))
-    updates = [
-        jnp.dot(
-            (orthos[w] * scales[w]).astype(jnp.bfloat16),
-            rights[w].T,
-            preferred_element_type=jnp.float32,
-        ).astype(jnp.bfloat16)
-        for w in range(2)
-    ]
+    updates = indexed_kernel(
+        update_kernel,
+        index,
+        [tall(a) for a in rights] + [all_of(a) for a in orthos] + [all_of(a) for a in scales],
+        [wide(shape(jnp.bfloat16, rows, grads[0].shape[1]))] * 2,
+        "updates",
+        grid=(steps,),
+    )
     return (*updates, *nexts)
 
 

time: 158 us -> 155 us (0.981)
  waiting for transfers between devices: 39.5 us -> 19.3 us
  Pallas kernels: 28.7 us -> 47.1 us
  blocking collectives: 18.2 us -> 36.2 us
  local copies, waits for them, and re-layouts: 11.9 us -> 3.07 us
  matrix products: 11.1 us -> 3.84 us
  starting transfers between devices: 46.9 us -> 43.8 us
    ppermute x15 -> x12, waiting for transfers between devices: 20 us -> 1.23 us  [shift_tp(): return lax.ppermute(x, 'tp', [(i, (i + by) % N_TP) for i in range(N_TP)])]
    all_to_all x1 -> x2, blocking collectives: 18.2 us -> 36.2 us  [exchange(): return lax.all_to_all(x, 'fsdp', 0, 0, axis_index_groups=groups)]
    pallas_call x2 -> x3, Pallas kernels: 19 us -> 28.7 us  [token_blocks(): pl.pallas_call(body, grid_spec=pltpu.PrefetchScalarGridSpec(num_scalar_pr...]
    all_to_all x3 -> x2, starting transfers between devices: 15.8 us -> 7.17 us  [exchange(): return lax.all_to_all(x, 'fsdp', 0, 0, axis_index_groups=groups)]
    unnamed x32, local copies, waits for them, and re-layouts: 10.8 us -> 2.34 us
    pallas_call x0 -> x4, Pallas kernels: none -> 8.32 us  [indexed_kernel(): pl.pallas_call(body, grid_spec=pltpu.PrefetchScalarGridSpec(num_scalar_pr...]
    dot_general x4 -> x0, matrix products: 5.99 us -> none  [the longest x2 3.01 us: per_device(): jnp.dot((orthos[w] * scales[w]).astype(jnp.bfloat16), rights[w].T, prefer...]
    all_to_all x3 -> x2, waiting for transfers between devices: 16.3 us -> 11.5 us  [exchange(): return lax.all_to_all(x, 'fsdp', 0, 0, axis_index_groups=groups)]
  transfers between devices with their start and end apart: 27 -> 23, of which waited for: 16 -> 8; matrix products, arithmetic and copies ran while one was open for 4% -> 1% of each run, Pallas kernels for 17% -> 26%
where the time goes in v2:
time: 155 us
  Pallas kernels  47.1 us (30%)
  starting transfers between devices  43.8 us (28%)
  blocking collectives  36.2 us (23%)
  waiting for transfers between devices  19.3 us (12%)
  matrix products  3.84 us (2%)
  local copies, waits for them, and re-layouts  3.07 us (2%)
    all_to_all x2, blocking collectives, exchange(): return lax.all_to_all(x, 'fsdp', 0, 0, axis_index_groups=groups)  36.2 us
    pallas_call x3, Pallas kernels, token_blocks(): pl.pallas_call(body, grid_spec=pltpu.PrefetchScalarGridSpec(num_scalar_pr...  28.7 us
    ppermute x12, starting transfers between devices, shift_tp(): return lax.ppermute(x, 'tp', [(i, (i + by) % N_TP) for i in range(N_TP)])  17.2 us
    ppermute x6, starting transfers between devices, swap_cores(): return lax.ppermute(x, 'rep', [(0, 1), (1, 0)])  16.5 us
    all_to_all x2, waiting for transfers between devices, exchange(): return lax.all_to_all(x, 'fsdp', 0, 0, axis_index_groups=groups)  11.5 us
    pallas_call x4, Pallas kernels, indexed_kernel(): pl.pallas_call(body, grid_spec=pltpu.PrefetchScalarGridSpec(num_scalar_pr...  8.32 us
    pallas_call x1, Pallas kernels, inverse_factor(): pl.pallas_call(inverse_kernel, out_shape=jax.ShapeDtypeStruct((RANK, RANK...  7.84 us
    all_to_all x2, starting transfers between devices, exchange(): return lax.all_to_all(x, 'fsdp', 0, 0, axis_index_groups=groups)  7.17 us
  transfers between devices with their start and end apart: 23, of which 8 were waited for; matrix products, arithmetic and copies ran while one was open for 1% of the time, Pallas kernels for 26%

profile of v2, /device:TPU:1, one launch (start us, length us, event | category | flops | bytes accessed | tf_op | source)
XLA Modules:
  0.0 154.6 jit_solution(9924271031764799956)
XLA Ops:
  0.6 2.1 %collective-permute-start = (bf16[512,256]{1,0:T(8,128)(2,1)}, bf16[512,256]{1,0:T(8,128)(2,1)S(1)}, u32[]{:S(2)}, u32[]{:S(2)}) collective-permute-start(bf16[512,256]{1,0:T(8,128)(2,1)} %refs_2_.1), channel_id=1, source_target_pairs={{0,1},{1,2},{2,3},{3,0},{4,5},{5,6},{6,7},{7,4},{8,9},{9,10},{10,1... | collective-permute-start | bytes 786440 | tf_op jit(solution)/shard_map/ppermute | solution.py:43
  4.2 2.6 %collective-permute-start.5 = (bf16[512,256]{1,0:T(8,128)(2,1)}, bf16[512,256]{1,0:T(8,128)(2,1)S(1)}, u32[]{:S(2)}, u32[]{:S(2)}) collective-permute-start(bf16[512,256]{1,0:T(8,128)(2,1)} %refs_2_.1), channel_id=1, source_target_pairs={{0,3},{1,0},{2,1},{3,2},{4,7},{5,4},{6,5},{7,6},{8,11},{9,8},{10,9... | collective-permute-start | bytes 786440 | tf_op jit(solution)/shard_map/ppermute | solution.py:43
  8.0 1.9 %collective-permute-start.1 = (bf16[512,256]{1,0:T(8,128)(2,1)S(1)}, bf16[512,256]{1,0:T(8,128)(2,1)S(1)}, u32[]{:S(2)}, u32[]{:S(2)}) collective-permute-start(bf16[512,256]{1,0:T(8,128)(2,1)S(1)} %collective-permute-done.refs_2_.refs_4_), channel_id=1, source_target_pairs={{0,1},{1,2},{2,3},{3,0},{4,5},{5,6},{6,7},{7,4},{8,9},{9,10},{10,1... | collective-permute-start | bytes 786440 | tf_op jit(solution)/shard_map/ppermute | solution.py:43
  9.9 1.6 %collective-permute-start.3 = (bf16[512,256]{1,0:T(8,128)(2,1)S(1)}, bf16[512,256]{1,0:T(8,128)(2,1)S(1)}, u32[]{:S(2)}, u32[]{:S(2)}) collective-permute-start(bf16[512,256]{1,0:T(8,128)(2,1)S(1)} %collective-permute-done.2.refs_5_.refs_7_), channel_id=1, source_target_pairs={{0,3},{1,0},{2,1},{3,2},{4,7},{5,4},{6,5},{7,6},{8,11},{9,8},{10,9... | collective-permute-start | bytes 786440 | tf_op jit(solution)/shard_map/ppermute | solution.py:43
  12.2 8.1 %basis_products.2 = (bf16[2048,256]{1,0:T(8,128)(2,1)}, f32[256,256]{1,0:T(8,128)}) custom-call(s32[5]{0:T(128)} %stack.23.index, bf16[1,256,2048]{2,1,0:T(8,128)(2,1)} %refs_8_.1, bf16[2048,256]{1,0:T(8,128)(2,1)} %basis.2, bf16[2048,2048]{1,0:T(8,128)(2,1)} %refs_10_.1), custom_call_target="tpu_custom_call" | custom-call | flops 1048576 | bytes 1048576 | tf_op jit(solution)/shard_map/basis_products/pallas_call | solution.py:108
  20.3 8.2 %basis_products.3 = (bf16[2048,256]{1,0:T(8,128)(2,1)}, f32[256,256]{1,0:T(8,128)}) custom-call(s32[5]{0:T(128)} %stack.23.index, bf16[1,256,2048]{2,1,0:T(8,128)(2,1)} %refs_9_.1, bf16[2048,256]{1,0:T(8,128)(2,1)} %basis.3, bf16[2048,2048]{1,0:T(8,128)(2,1)} %refs_11_.1), custom_call_target="tpu_custom_call" | custom-call | flops 1048576 | bytes 1048576 | tf_op jit(solution)/shard_map/basis_products/pallas_call | solution.py:108
  33.1 6.5 %collective-permute-start.6 = (bf16[256,256]{1,0:T(8,128)(2,1)S(1)}, bf16[256,256]{1,0:T(8,128)(2,1)S(1)}, u32[]{:S(2)}, u32[]{:S(2)}) collective-permute-start(bf16[256,256]{1,0:T(8,128)(2,1)S(1)} %get-tuple-element.44), channel_id=1, source_target_pairs={{0,128},{128,0},{1,129},{129,1},{2,130},{130,2},{3,131},{131,3},{4... | collective-permute-start | bytes 393224 | tf_op jit(solution)/shard_map/ppermute | solution.py:54
  41.6 1.7 %collective-permute-start.9 = (bf16[256,256]{1,0:T(8,128)(2,1)S(1)}, bf16[256,256]{1,0:T(8,128)(2,1)S(1)}, u32[]{:S(2)}, u32[]{:S(2)}) collective-permute-start(bf16[256,256]{1,0:T(8,128)(2,1)S(1)} %add_convert_fusion), channel_id=1, source_target_pairs={{0,3},{1,0},{2,1},{3,2},{4,7},{5,4},{6,5},{7,6},{8,11},{9,8},{10,9... | collective-permute-start | bytes 393224 | tf_op jit(solution)/shard_map/ppermute | solution.py:43
  43.3 12.3 %buffers.1 = (bf16[256,2048]{1,0:T(8,128)(2,1)}, bf16[256,2048]{1,0:T(8,128)(2,1)}) custom-call(s32[5]{0:T(128)} %stack.23.index, bf16[512,256]{1,0:T(8,128)(2,1)} %copy-done.12, bf16[512,256]{1,0:T(8,128)(2,1)} %copy-done.13, bf16[512,256]{1,0:T(8,128)(2,1)} %refs_2_.1, bf16[512,256]{1,0:T(8,128)(2,1)} %refs_3_.1, bf16[512,256]{1,0:T(8,128)(2,1)} %copy-done.6, ...), custom_call_target="tpu_custom_call" | custom-call | flops 8589934592 | bytes 1048576 | tf_op jit(solution)/shard_map/buffers/pallas_call | solution.py:108
  57.8 1.7 %convolution_convert_fusion.1 = bf16[2048,256]{1,0:T(8,128)(2,1)S(1)} fusion(bf16[256,2048]{1,0:T(8,128)(2,1)} %get-tuple-element.50.refs_2_, bf16[256,256]{1,0:T(8,128)(2,1)S(1)} %fusion.7, bf16[256,256]{1,0:T(8,128)(2,1)S(1)} %collective-permute-done.10, pred[]{:T(512)S(6)} %eq.12), kind=kOutput, calls=%fused_computation.1 | convolution fusion | flops 269025280 | bytes 2359297 | tf_op jit(solution)/shard_map/dot_general | solution.py:28
  61.0 1.7 %collective-permute-done.11.other = bf16[2048,256]{1,0:T(8,128)(2,1)S(1)} collective-permute-done((bf16[2048,256]{1,0:T(8,128)(2,1)S(1)}, bf16[2048,256]{1,0:T(8,128)(2,1)S(1)}, u32[]{:S(2)}, u32[]{:S(2)}) %collective-permute-start.11) | collective-permute-done | bytes 1048608 | tf_op jit(solution)/shard_map/ppermute | solution.py:54
  63.0 18.6 %all_to_all.20.pieces = bf16[4,576,256]{2,1,0:T(8,128)(2,1)S(1)} all-to-all(bf16[4,576,256]{2,1,0:T(8,128)(2,1)S(1)} %pack_quarters.1), channel_id=1, replica_groups={{0,32,64,96},{4,36,68,100},{8,40,72,104},{12,44,76,108},{16,48,80,112},..., dimensions={0} | all-to-all | bytes 2359296 | tf_op jit(solution)/shard_map/all_to_all | solution.py:87
  81.8 17.6 %all_to_all.21.pieces = bf16[8,80,256]{2,1,0:T(8,128)(2,1)S(1)} all-to-all(bf16[8,80,256]{2,1,0:T(8,128)(2,1)S(1)} %sum_over_y.1), channel_id=1, replica_groups={{0,4,8,12,16,20,24,28},{32,36,40,44,48,52,56,60},{64,68,72,76,80,84,88,..., dimensions={0} | all-to-all | bytes 655360 | tf_op jit(solution)/shard_map/all_to_all | solution.py:87
  100.1 3.4 %all-to-all-start.2 = ((bf16[8,80,256]{2,1,0:T(8,128)(2,1)}), bf16[8,80,256]{2,1,0:T(8,128)(2,1)S(1)}, u32[]{:S(2)}, u32[]{:S(2)}) async-start(bf16[8,80,256]{2,1,0:T(8,128)(2,1)} %sum_over_z.1), calls=%async_computation.2 | async-start | bytes 655360 | tf_op jit(solution)/shard_map/all_to_all | solution.py:87
  103.7 10.0 %all-to-all-done.2.pieces = bf16[8,80,256]{2,1,0:T(8,128)(2,1)S(1)} async-done(((bf16[8,80,256]{2,1,0:T(8,128)(2,1)}), bf16[8,80,256]{2,1,0:T(8,128)(2,1)S(1)}, u32[]{:S(2)}, u32[]{:S(2)}) %all-to-all-start.2) | async-done | bytes 327712 | tf_op jit(solution)/shard_map/all_to_all | solution.py:87
  115.0 1.8 %collective-permute-start.13 = (f32[64,256]{1,0:T(8,128)S(1)}, f32[64,256]{1,0:T(8,128)S(1)}, u32[]{:S(2)}, u32[]{:S(2)}) collective-permute-start(f32[64,256]{1,0:T(8,128)S(1)} %get-tuple-element.57), channel_id=1, source_target_pairs={{0,64},{4,68},{8,72},{12,76},{16,80},{20,84},{24,88},{28,92},{32,9... | collective-permute-start | bytes 196616 | tf_op jit(solution)/shard_map/ppermute | solution.py:50
  117.6 3.7 %all-to-all-start.3 = ((bf16[4,512,256]{2,1,0:T(8,128)(2,1)}), bf16[4,512,256]{2,1,0:T(8,128)(2,1)S(1)}, u32[]{:S(2)}, u32[]{:S(2)}) async-start(bf16[4,512,256]{2,1,0:T(8,128)(2,1)} %get-tuple-element.56), calls=%async_computation.3 | async-start | bytes 2097152 | tf_op jit(solution)/shard_map/all_to_all | solution.py:87
  121.5 7.8 %inverse_factor.1 = f32[256,256]{1,0:T(8,128)S(1)} custom-call(f32[256,256]{1,0:T(8,128)S(1)} %bitcast.20), custom_call_target="tpu_custom_call" | custom-call | flops 8000000000 | bytes 1048576 | tf_op jit(solution)/shard_map/inverse_factor/pallas_call | solution.py:328
  131.5 7.2 %collective-permute-start.15 = (bf16[2048,256]{1,0:T(8,128)(2,1)S(1)}, bf16[2048,256]{1,0:T(8,128)(2,1)S(1)}, u32[]{:S(2)}, u32[]{:S(2)}) collective-permute-start(bf16[2048,256]{1,0:T(8,128)(2,1)S(1)} %get-tuple-element.69.right_mine), channel_id=1, source_target_pairs={{0,128},{128,0},{1,129},{129,1},{2,130},{130,2},{3,131},{131,3},{4... | collective-permute-start | bytes 3145736 | tf_op jit(solution)/shard_map/ppermute | solution.py:54
  139.2 2.1 %collective-permute-done.16 = f32[256,256]{1,0:T(8,128)S(1)} collective-permute-done((f32[256,256]{1,0:T(8,128)S(1)}, f32[256,256]{1,0:T(8,128)S(1)}, u32[]{:S(2)}, u32[]{:S(2)}) %collective-permute-start.16) | collective-permute-done | bytes 262176 | tf_op jit(solution)/shard_map/ppermute | solution.py:54
  142.0 2.2 %collective-permute-start.18 = (f32[1,256]{1,0:T(1,128)S(1)}, f32[1,256]{1,0:T(1,128)S(1)}, u32[]{:S(2)}, u32[]{:S(2)}) collective-permute-start(f32[1,256]{1,0:T(1,128)S(1)} %bitcast.23), channel_id=1, source_target_pairs={{0,2},{1,3},{2,0},{3,1},{4,6},{5,7},{6,4},{7,5},{8,10},{9,11},{10,... | collective-permute-start | bytes 3080 | tf_op jit(solution)/shard_map/ppermute | solution.py:43
  144.2 2.0 %collective-permute-start.19 = (f32[1,256]{1,0:T(1,128)S(1)}, f32[1,256]{1,0:T(1,128)S(1)}, u32[]{:S(2)}, u32[]{:S(2)}) collective-permute-start(f32[1,256]{1,0:T(1,128)S(1)} %bitcast.24), channel_id=1, source_target_pairs={{0,3},{1,0},{2,1},{3,2},{4,7},{5,4},{6,5},{7,6},{8,11},{9,8},{10,9... | collective-permute-start | bytes 3080 | tf_op jit(solution)/shard_map/ppermute | solution.py:43
  146.2 3.2 %feedback.1 = (bf16[1,256,2048]{2,1,0:T(8,128)(2,1)}, bf16[1,256,2048]{2,1,0:T(8,128)(2,1)}) custom-call(s32[5]{0:T(128)S(1)} %copy-done.15, bf16[2048,256]{1,0:T(8,128)(2,1)S(1)} %get-tuple-element.69.right_mine, bf16[2048,256]{1,0:T(8,128)(2,1)S(1)} %collective-permute-done.15.right_other, f32[256,256]{1,0:T(8,128)S(1)} %get-tuple-element.73.refs_0_, ...), custom_call_target="tpu_custom_call" | custom-call | flops 268435456 | bytes 1048576 | tf_op jit(solution)/shard_map/feedback/pallas_call | solution.py:184
  151.5 3.1 %updates.1 = (bf16[256,2048]{1,0:T(8,128)(2,1)}, bf16[256,2048]{1,0:T(8,128)(2,1)}) custom-call(s32[5]{0:T(128)S(1)} %copy-done.15, bf16[2048,256]{1,0:T(8,128)(2,1)S(1)} %get-tuple-element.69.right_mine, bf16[2048,256]{1,0:T(8,128)(2,1)S(1)} %collective-permute-done.15.right_other, f32[256,256]{1,0:T(8,128)S(1)} %get-tuple-element.73.refs_0_, ...), custom_call_target="tpu_custom_call" | custom-call | flops 268435456 | bytes 1048576 | tf_op jit(solution)/shard_map/updates/pallas_call | solution.py:184
  (84 shorter events, 22.4 us)
Async XLA Ops:
  0.6 7.4 %collective-permute-start = (bf16[512,256]{1,0:T(8,128)(2,1)}, bf16[512,256]{1,0:T(8,128)(2,1)S(1)}, u32[]{:S(2)}, u32[]{:S(2)}) collective-permute-start(bf16[512,256]{1,0:T(8,128)(2,1)} %refs_2_.1), channel_id=1, source_target_pairs={{0,1},{1,2},{2,3},{3,0},{4,5},{5,6},{6,7},{7,4},{8,9},{9,10},{10,1... | collective-permute-start | bytes 786440 | tf_op jit(solution)/shard_map/ppermute | solution.py:43
  2.7 7.1 %collective-permute-start.2 = (bf16[512,256]{1,0:T(8,128)(2,1)}, bf16[512,256]{1,0:T(8,128)(2,1)S(1)}, u32[]{:S(2)}, u32[]{:S(2)}) collective-permute-start(bf16[512,256]{1,0:T(8,128)(2,1)} %refs_3_.1), channel_id=1, source_target_pairs={{0,3},{1,0},{2,1},{3,2},{4,7},{5,4},{6,5},{7,6},{8,11},{9,8},{10,9... | collective-permute-start | bytes 786440 | tf_op jit(solution)/shard_map/ppermute | solution.py:43
  4.1 24.4 %collective-permute-start.4 = (bf16[512,256]{1,0:T(8,128)(2,1)}, bf16[512,256]{1,0:T(8,128)(2,1)S(1)}, u32[]{:S(2)}, u32[]{:S(2)}) collective-permute-start(bf16[512,256]{1,0:T(8,128)(2,1)} %refs_3_.1), channel_id=1, source_target_pairs={{0,1},{1,2},{2,3},{3,0},{4,5},{5,6},{6,7},{7,4},{8,9},{9,10},{10,1... | collective-permute-start | bytes 786440 | tf_op jit(solution)/shard_map/ppermute | solution.py:43
  4.2 24.3 %collective-permute-start.5 = (bf16[512,256]{1,0:T(8,128)(2,1)}, bf16[512,256]{1,0:T(8,128)(2,1)S(1)}, u32[]{:S(2)}, u32[]{:S(2)}) collective-permute-start(bf16[512,256]{1,0:T(8,128)(2,1)} %refs_2_.1), channel_id=1, source_target_pairs={{0,3},{1,0},{2,1},{3,2},{4,7},{5,4},{6,5},{7,6},{8,11},{9,8},{10,9... | collective-permute-start | bytes 786440 | tf_op jit(solution)/shard_map/ppermute | solution.py:43
  8.0 20.6 %copy-start.6 = (bf16[512,256]{1,0:T(8,128)(2,1)}, bf16[512,256]{1,0:T(8,128)(2,1)S(1)}, u32[]{:S(2)}) copy-start(bf16[512,256]{1,0:T(8,128)(2,1)S(1)} %collective-permute-done.refs_2_.refs_4_) | copy-start | bytes 786436
  8.0 24.1 %collective-permute-start.1 = (bf16[512,256]{1,0:T(8,128)(2,1)S(1)}, bf16[512,256]{1,0:T(8,128)(2,1)S(1)}, u32[]{:S(2)}, u32[]{:S(2)}) collective-permute-start(bf16[512,256]{1,0:T(8,128)(2,1)S(1)} %collective-permute-done.refs_2_.refs_4_), channel_id=1, source_target_pairs={{0,1},{1,2},{2,3},{3,0},{4,5},{5,6},{6,7},{7,4},{8,9},{9,10},{10,1... | collective-permute-start | bytes 786440 | tf_op jit(solution)/shard_map/ppermute | solution.py:43
  9.9 22.3 %collective-permute-start.3 = (bf16[512,256]{1,0:T(8,128)(2,1)S(1)}, bf16[512,256]{1,0:T(8,128)(2,1)S(1)}, u32[]{:S(2)}, u32[]{:S(2)}) collective-permute-start(bf16[512,256]{1,0:T(8,128)(2,1)S(1)} %collective-permute-done.2.refs_5_.refs_7_), channel_id=1, source_target_pairs={{0,3},{1,0},{2,1},{3,2},{4,7},{5,4},{6,5},{7,6},{8,11},{9,8},{10,9... | collective-permute-start | bytes 786440 | tf_op jit(solution)/shard_map/ppermute | solution.py:43
  33.1 7.5 %collective-permute-start.6 = (bf16[256,256]{1,0:T(8,128)(2,1)S(1)}, bf16[256,256]{1,0:T(8,128)(2,1)S(1)}, u32[]{:S(2)}, u32[]{:S(2)}) collective-permute-start(bf16[256,256]{1,0:T(8,128)(2,1)S(1)} %get-tuple-element.44), channel_id=1, source_target_pairs={{0,128},{128,0},{1,129},{129,1},{2,130},{130,2},{3,131},{131,3},{4... | collective-permute-start | bytes 393224 | tf_op jit(solution)/shard_map/ppermute | solution.py:54
  40.6 15.1 %collective-permute-start.7 = (bf16[256,256]{1,0:T(8,128)(2,1)S(1)}, bf16[256,256]{1,0:T(8,128)(2,1)S(1)}, u32[]{:S(2)}, u32[]{:S(2)}) collective-permute-start(bf16[256,256]{1,0:T(8,128)(2,1)S(1)} %add_convert_fusion), channel_id=1, source_target_pairs={{0,1},{1,2},{2,3},{3,0},{4,5},{5,6},{6,7},{7,4},{8,9},{9,10},{10,1... | collective-permute-start | bytes 393224 | tf_op jit(solution)/shard_map/ppermute | solution.py:43
  40.7 15.0 %collective-permute-start.8 = (bf16[256,256]{1,0:T(8,128)(2,1)S(1)}, bf16[256,256]{1,0:T(8,128)(2,1)S(1)}, u32[]{:S(2)}, u32[]{:S(2)}) collective-permute-start(bf16[256,256]{1,0:T(8,128)(2,1)S(1)} %add_convert_fusion), channel_id=1, source_target_pairs={{0,2},{1,3},{2,0},{3,1},{4,6},{5,7},{6,4},{7,5},{8,10},{9,11},{10,... | collective-permute-start | bytes 393224 | tf_op jit(solution)/shard_map/ppermute | solution.py:43
  41.6 14.1 %collective-permute-start.9 = (bf16[256,256]{1,0:T(8,128)(2,1)S(1)}, bf16[256,256]{1,0:T(8,128)(2,1)S(1)}, u32[]{:S(2)}, u32[]{:S(2)}) collective-permute-start(bf16[256,256]{1,0:T(8,128)(2,1)S(1)} %add_convert_fusion), channel_id=1, source_target_pairs={{0,3},{1,0},{2,1},{3,2},{4,7},{5,4},{6,5},{7,6},{8,11},{9,8},{10,9... | collective-permute-start | bytes 393224 | tf_op jit(solution)/shard_map/ppermute | solution.py:43
  55.8 2.0 %collective-permute-start.10 = (bf16[256,256]{1,0:T(8,128)(2,1)S(1)}, bf16[256,256]{1,0:T(8,128)(2,1)S(1)}, u32[]{:S(2)}, u32[]{:S(2)}) collective-permute-start(bf16[256,256]{1,0:T(8,128)(2,1)S(1)} %fusion.7), channel_id=1, source_target_pairs={{0,128},{128,0},{1,129},{129,1},{2,130},{130,2},{3,131},{131,3},{4... | collective-permute-start | bytes 393224 | tf_op jit(solution)/shard_map/ppermute | solution.py:54
  60.0 2.7 %collective-permute-start.11 = (bf16[2048,256]{1,0:T(8,128)(2,1)S(1)}, bf16[2048,256]{1,0:T(8,128)(2,1)S(1)}, u32[]{:S(2)}, u32[]{:S(2)}) collective-permute-start(bf16[2048,256]{1,0:T(8,128)(2,1)S(1)} %get-tuple-element.70), channel_id=1, source_target_pairs={{0,128},{128,0},{1,129},{129,1},{2,130},{130,2},{3,131},{131,3},{4... | collective-permute-start | bytes 3145736 | tf_op jit(solution)/shard_map/ppermute | solution.py:54
  100.1 13.5 %all-to-all-start.2 = ((bf16[8,80,256]{2,1,0:T(8,128)(2,1)}), bf16[8,80,256]{2,1,0:T(8,128)(2,1)S(1)}, u32[]{:S(2)}, u32[]{:S(2)}) async-start(bf16[8,80,256]{2,1,0:T(8,128)(2,1)} %sum_over_z.1), calls=%async_computation.2 | async-start | bytes 655360 | tf_op jit(solution)/shard_map/all_to_all | solution.py:87
  114.7 6.7 %collective-permute-start.12 = (f32[64,256]{1,0:T(8,128)S(1)}, f32[64,256]{1,0:T(8,128)S(1)}, u32[]{:S(2)}, u32[]{:S(2)}) collective-permute-start(f32[64,256]{1,0:T(8,128)S(1)} %get-tuple-element.57), channel_id=1, source_target_pairs={{0,32},{4,36},{8,40},{12,44},{16,48},{20,52},{24,56},{28,60},{32,6... | collective-permute-start | bytes 196616 | tf_op jit(solution)/shard_map/ppermute | solution.py:50
  115.0 6.5 %collective-permute-start.13 = (f32[64,256]{1,0:T(8,128)S(1)}, f32[64,256]{1,0:T(8,128)S(1)}, u32[]{:S(2)}, u32[]{:S(2)}) collective-permute-start(f32[64,256]{1,0:T(8,128)S(1)} %get-tuple-element.57), channel_id=1, source_target_pairs={{0,64},{4,68},{8,72},{12,76},{16,80},{20,84},{24,88},{28,92},{32,9... | collective-permute-start | bytes 196616 | tf_op jit(solution)/shard_map/ppermute | solution.py:50
  116.7 4.7 %collective-permute-start.14 = (f32[64,256]{1,0:T(8,128)S(1)}, f32[64,256]{1,0:T(8,128)S(1)}, u32[]{:S(2)}, u32[]{:S(2)}) collective-permute-start(f32[64,256]{1,0:T(8,128)S(1)} %get-tuple-element.57), channel_id=1, source_target_pairs={{0,96},{4,100},{8,104},{12,108},{16,112},{20,116},{24,120},{28,124... | collective-permute-start | bytes 196616 | tf_op jit(solution)/shard_map/ppermute | solution.py:50
  117.6 13.2 %all-to-all-start.3 = ((bf16[4,512,256]{2,1,0:T(8,128)(2,1)}), bf16[4,512,256]{2,1,0:T(8,128)(2,1)S(1)}, u32[]{:S(2)}, u32[]{:S(2)}) async-start(bf16[4,512,256]{2,1,0:T(8,128)(2,1)} %get-tuple-element.56), calls=%async_computation.3 | async-start | bytes 2097152 | tf_op jit(solution)/shard_map/all_to_all | solution.py:87
  131.5 14.7 %collective-permute-start.15 = (bf16[2048,256]{1,0:T(8,128)(2,1)S(1)}, bf16[2048,256]{1,0:T(8,128)(2,1)S(1)}, u32[]{:S(2)}, u32[]{:S(2)}) collective-permute-start(bf16[2048,256]{1,0:T(8,128)(2,1)S(1)} %get-tuple-element.69.right_mine), channel_id=1, source_target_pairs={{0,128},{128,0},{1,129},{129,1},{2,130},{130,2},{3,131},{131,3},{4... | collective-permute-start | bytes 3145736 | tf_op jit(solution)/shard_map/ppermute | solution.py:54
  139.1 2.2 %collective-permute-start.16 = (f32[256,256]{1,0:T(8,128)S(1)}, f32[256,256]{1,0:T(8,128)S(1)}, u32[]{:S(2)}, u32[]{:S(2)}) collective-permute-start(f32[256,256]{1,0:T(8,128)S(1)} %fusion.6), channel_id=1, source_target_pairs={{0,128},{128,0},{1,129},{129,1},{2,130},{130,2},{3,131},{131,3},{4... | collective-permute-start | bytes 786440 | tf_op jit(solution)/shard_map/ppermute | solution.py:54
  141.3 8.0 %collective-permute-start.17 = (f32[1,256]{1,0:T(1,128)S(1)}, f32[1,256]{1,0:T(1,128)S(1)}, u32[]{:S(2)}, u32[]{:S(2)}) collective-permute-start(f32[1,256]{1,0:T(1,128)S(1)} %bitcast.22), channel_id=1, source_target_pairs={{0,1},{1,2},{2,3},{3,0},{4,5},{5,6},{6,7},{7,4},{8,9},{9,10},{10,1... | collective-permute-start | bytes 3080 | tf_op jit(solution)/shard_map/ppermute | solution.py:43
  142.0 7.3 %collective-permute-start.18 = (f32[1,256]{1,0:T(1,128)S(1)}, f32[1,256]{1,0:T(1,128)S(1)}, u32[]{:S(2)}, u32[]{:S(2)}) collective-permute-start(f32[1,256]{1,0:T(1,128)S(1)} %bitcast.23), channel_id=1, source_target_pairs={{0,2},{1,3},{2,0},{3,1},{4,6},{5,7},{6,4},{7,5},{8,10},{9,11},{10,... | collective-permute-start | bytes 3080 | tf_op jit(solution)/shard_map/ppermute | solution.py:43
  144.2 5.2 %collective-permute-start.19 = (f32[1,256]{1,0:T(1,128)S(1)}, f32[1,256]{1,0:T(1,128)S(1)}, u32[]{:S(2)}, u32[]{:S(2)}) collective-permute-start(f32[1,256]{1,0:T(1,128)S(1)} %bitcast.24), channel_id=1, source_target_pairs={{0,3},{1,0},{2,1},{3,2},{4,7},{5,4},{6,5},{7,6},{8,11},{9,8},{10,9... | collective-permute-start | bytes 3080 | tf_op jit(solution)/shard_map/ppermute | solution.py:43
  149.4 2.1 %collective-permute-start.20 = (f32[1,256]{1,0:T(1,128)S(1)}, f32[1,256]{1,0:T(1,128)S(1)}, u32[]{:S(2)}, u32[]{:S(2)}) collective-permute-start(f32[1,256]{1,0:T(1,128)S(1)} %rsqrt_multiply_fusion), channel_id=1, source_target_pairs={{0,128},{128,0},{1,129},{129,1},{2,130},{130,2},{3,131},{131,3},{4... | collective-permute-start | bytes 3080 | tf_op jit(solution)/shard_map/ppermute | solution.py:54
  (15 other events, 126.6 us)

commit v3 on v2

--- a/solution.py
+++ b/solution.py
@@ -13,7 +13,6 @@
 N_Y = 4
 N_Z = 8
 LANES = 128
-COLUMNS = 512
 BLOCK = 64
 GROUP = 16
 
@@ -87,81 +86,21 @@
     return lax.all_to_all(x, "fsdp", 0, 0, axis_index_groups=groups)
 
 
-def whole(a):
-    return pl.BlockSpec(a.shape, lambda *_: (0,) * len(a.shape), pipeline_mode=pl.Buffered(1))
-
-
-def local_kernel(body, operands, results, name, **more):
+def local_kernel(body, operands, results, name, cost=1 << 20):
     return pl.pallas_call(
         body,
         out_shape=results,
         compiler_params=pltpu.CompilerParams(vmem_limit_bytes=12 << 20),
-        cost_estimate=pl.CostEstimate(flops=1 << 20, bytes_accessed=1 << 20, transcendentals=0),
-        name=name,
-        **more,
-    )(*operands)
-
-
-def token_blocks(body, index, small, grads, results, specs, scratch, cost, name):
-    count = grads[0].shape[0] // N_TP
-    block = lambda a: pl.BlockSpec((count, a.shape[1]), lambda s, i: (i[s], 0))
-    return pl.pallas_call(
-        body,
-        grid_spec=pltpu.PrefetchScalarGridSpec(
-            num_scalar_prefetch=1,
-            grid=(N_TP,),
-            in_specs=[whole(a) for a in small] + [block(a) for a in grads],
-            out_specs=specs,
-            scratch_shapes=scratch,
-        ),
-        out_shape=results,
-        compiler_params=pltpu.CompilerParams(
-            dimension_semantics=("arbitrary",), vmem_limit_bytes=56 << 20
-        ),
         cost_estimate=pl.CostEstimate(flops=cost, bytes_accessed=1 << 20, transcendentals=0),
         name=name,
-    )(index, *small, *grads)
-
-
-def product_kernel(index, moment, basis, grad, product, near):
-    term = jnp.dot(grad[...], basis[...], preferred_element_type=jnp.float32)
-    product[...] = term.astype(jnp.bfloat16)
-
-    @pl.when(pl.program_id(0) == 0)
-    def _():
-        near[...] = jnp.dot(moment[0], basis[...], preferred_element_type=jnp.float32)
-
-
-def buffer_kernel(index, *refs):
-    step = pl.program_id(0)
-    for w in range(2):
-        far, own, up, down, moment, grad, buffer, acc = refs[w::2]
-
-        @pl.when(step == 0)
-        def _():
-            acc[...] = moment[0].astype(jnp.float32)
-
-        for at, tokens in ((0, far), (1, own), (2, up), (3, down)):
-
-            @pl.when(step == at)
-            def _():
-                turned = tokens[...].T
-                for c in range(0, acc.shape[1], COLUMNS):
-                    here = slice(c, c + COLUMNS)
-                    acc[:, here] += jnp.dot(
-                        turned, grad[:, here], preferred_element_type=jnp.float32
-                    )
-
-        @pl.when(step == N_TP - 1)
-        def _():
-            buffer[...] = acc[...].astype(jnp.bfloat16)
+    )(*operands)
 
 
 def near_kernel(index, *refs):
     for w in range(2):
-        own, up, down, product_own, product_up, product_down, base, out = refs[w::2]
+        own, up, down, product_own, product_up, product_down, moment, basis, out = refs[w::2]
         out[...] = (
-            base[...]
+            jnp.dot(moment[0], basis[...], preferred_element_type=jnp.float32)
             + contract_rows(own[...], product_own[...])
             + contract_rows(up[...], product_up[...])
             + contract_rows(down[...], product_down[...])
@@ -179,56 +118,27 @@
     other[...] = jnp.where(first, output, query).astype(jnp.bfloat16)
 
 
-def indexed_kernel(body, index, operands, results, name, grid=(1,), limit=16 << 20):
+def indexed_kernel(body, index, operands, results, name):
     spec = lambda block, place: pl.BlockSpec(block, place)
     return pl.pallas_call(
         body,
         grid_spec=pltpu.PrefetchScalarGridSpec(
             num_scalar_prefetch=1,
-            grid=grid,
+            grid=(1,),
             in_specs=[spec(block, place) for _, block, place in operands],
             out_specs=[spec(block, place) for _, block, place in results],
         ),
         out_shape=[shape for shape, _, _ in results],
         compiler_params=pltpu.CompilerParams(
-            dimension_semantics=("arbitrary",), vmem_limit_bytes=limit
+            dimension_semantics=("arbitrary",), vmem_limit_bytes=24 << 20
         ),
-        cost_estimate=pl.CostEstimate(flops=1 << 28, bytes_accessed=1 << 20, transcendentals=0),
+        cost_estimate=pl.CostEstimate(flops=1 << 20, bytes_accessed=1 << 20, transcendentals=0),
         name=name,
     )(index, *[a for a, _, _ in operands])
 
 
 def all_of(a):
     return (a, a.shape, lambda s, i: (0,) * len(a.shape))
-
-
-def feedback_kernel(index, right_mine, right_other, *refs):
-    first = index[N_TP] == 0
-    sides = (right_mine[...], right_other[...])
-    for w in range(2):
-        ortho, buffer, out = refs[w::2]
-        right = jnp.where(first, sides[w], sides[1 - w])
-        term = lax.dot_general(
-            ortho[...].astype(jnp.bfloat16),
-            right,
-            (((1,), (1,)), ((), ())),
-            preferred_element_type=jnp.float32,
-        )
-        out[0] = (buffer[...].astype(jnp.float32) - (1.0 - retain) / 2 * term).astype(jnp.bfloat16)
-
-
-def update_kernel(index, right_mine, right_other, *refs):
-    first = index[N_TP] == 0
-    sides = (right_mine[...], right_other[...])
-    for w in range(2):
-        ortho, scale, out = refs[w::2]
-        right = jnp.where(first, sides[w], sides[1 - w])
-        out[...] = lax.dot_general(
-            (ortho[...] * scale[...]).astype(jnp.bfloat16),
-            right,
-            (((1,), (1,)), ((), ())),
-            preferred_element_type=jnp.float32,
-        ).astype(jnp.bfloat16)
 
 
 def pack_kernel(mine, other, gram, out):
@@ -367,32 +277,18 @@
     shape = lambda dtype, *dims: jax.ShapeDtypeStruct(dims, dtype)
     square = shape(jnp.float32, rows, RANK)
     moments = [moment_query, moment_output]
-    products, bases_terms = [], []
+    products = []
     for w in range(2):
         grad = grads[w] if w == 0 else lax.optimization_barrier((grads[w], up[0], down[1]))[0]
-        product, term = token_blocks(
-            product_kernel,
-            index,
-            [moments[w], bases[w]],
-            [grad],
-            [shape(jnp.bfloat16, N_TP * count, RANK), square],
-            [
-                pl.BlockSpec((count, RANK), lambda s, i: (i[s], 0)),
-                pl.BlockSpec(square.shape, lambda s, i: (0, 0)),
-            ],
-            [],
-            1 << 20,
-            "basis_products",
-        )
-        products.append(product)
-        bases_terms.append(term)
+        product = jnp.dot(grad, bases[w], preferred_element_type=jnp.float32)
+        products.append(lax.optimization_barrier(product.astype(jnp.bfloat16)))
     part = lambda a, at: (a, (count, RANK), lambda s, i: (i[at], 0))
     near = indexed_kernel(
         near_kernel,
         index,
         [all_of(a) for a in own + up + down]
         + [part(a, at) for at in (1, 2, 3) for a in products]
-        + [all_of(a) for a in bases_terms],
+        + [all_of(a) for a in moments + bases],
         [all_of(square)] * 2,
         "near_tokens",
     )
@@ -405,19 +301,14 @@
     )
     mine = mine + swap_cores(other).astype(jnp.float32)
     mine, far = lax.optimization_barrier((mine.astype(jnp.bfloat16), far))
-    width = grads[0].shape[1]
-    buffers = token_blocks(
-        buffer_kernel,
-        index,
-        far + own + up + down + moments,
-        grads,
-        [shape(jnp.bfloat16, rows, width)] * 2,
-        [pl.BlockSpec((rows, width), lambda s, i: (0, 0))] * 2,
-        [pltpu.VMEM((rows, width), jnp.float32)] * 2,
-        1 << 33,
-        "buffers",
-    )
-    parts, buffers = lax.optimization_barrier((from_all(mine, shift_tp), buffers))
+    buffers = [
+        (
+            moments[w][0].astype(jnp.float32)
+            + contract_rows(in_order([own[w], up[w], far[w], down[w]], tp), grads[w])
+        ).astype(jnp.bfloat16)
+        for w in range(2)
+    ]
+    parts, buffers[0] = lax.optimization_barrier((from_all(mine, shift_tp), buffers[0]))
     power = total(parts)
     power_b = power.astype(jnp.bfloat16)
     powers_b = split([power_b, swap_cores(power_b)])
@@ -455,30 +346,29 @@
     right = jnp.dot(raw, inverse.T.astype(jnp.bfloat16), preferred_element_type=jnp.float32)
     sums = from_all(jnp.sum(right * right, axis=0, keepdims=True), shift_tp)
     right_b = right.astype(jnp.bfloat16)
-    rights = [right_b, swap_cores(right_b)]
-    steps = grads[0].shape[1] // COLUMNS
-    tall = lambda a: (a, (COLUMNS, a.shape[1]), lambda s, i: (s, 0))
-    wide = lambda a: (a, (rows, COLUMNS), lambda s, i: (0, s))
-    result = shape(jnp.bfloat16, 1, rows, grads[0].shape[1])
-    nexts = indexed_kernel(
-        feedback_kernel,
-        index,
-        [tall(a) for a in rights] + [all_of(a) for a in orthos] + [wide(a) for a in buffers],
-        [(result, (1, rows, COLUMNS), lambda s, i: (0, 0, s))] * 2,
-        "feedback",
-        grid=(steps,),
-    )
-    sums, nexts = lax.optimization_barrier((sums, nexts))
+    rights = split([right_b, swap_cores(right_b)])
+    nexts = []
+    for w in range(2):
+        feedback = jnp.dot(
+            orthos[w].astype(jnp.bfloat16), rights[w].T, preferred_element_type=jnp.float32
+        )
+        nexts.append(
+            (buffers[w].astype(jnp.float32) - (1.0 - retain) / 2 * feedback).astype(jnp.bfloat16)[
+                None
+            ]
+        )
+    sums, nexts[0] = lax.optimization_barrier((sums, nexts[0]))
     scale = D / RANK**0.5 / jnp.sqrt(total(sums) + epsilon)
     scales = split([scale, swap_cores(scale)])
-    updates = indexed_kernel(
-        update_kernel,
-        index,
-        [tall(a) for a in rights] + [all_of(a) for a in orthos] + [all_of(a) for a in scales],
-        [wide(shape(jnp.bfloat16, rows, grads[0].shape[1]))] * 2,
-        "updates",
-        grid=(steps,),
-    )
+    scales, nexts[1] = lax.optimization_barrier((scales, nexts[1]))
+    updates = [
+        jnp.dot(
+            (orthos[w] * scales[w]).astype(jnp.bfloat16),
+            rights[w].T,
+            preferred_element_type=jnp.float32,
+        ).astype(jnp.bfloat16)
+        for w in range(2)
+    ]
     return (*updates, *nexts)
 
 

time: 155 us -> 144 us (0.929)
  Pallas kernels: 47.1 us -> 13.9 us
  matrix products: 3.84 us -> 27.6 us
  starting transfers between devices: 43.8 us -> 34.4 us
  blocking collectives: 36.2 us -> 39.1 us
  waiting for transfers between devices: 19.3 us -> 22 us
  local copies, waits for them, and re-layouts: 3.07 us -> 5.24 us
    pallas_call x3 -> x0, Pallas kernels: 28.7 us -> none  [token_blocks(): pl.pallas_call(body, grid_spec=pltpu.PrefetchScalarGridSpec(num_scalar_pr...]
    dot_general x0 -> x6, matrix products: none -> 17.8 us  [the longest x2 11.9 us: per_device(): product = jnp.dot(grad, bases[w], preferred_element_type=jnp.float32)]
    ppermute x6, starting transfers between devices: 16.5 us -> 11 us  [swap_cores(): return lax.ppermute(x, 'rep', [(0, 1), (1, 0)])]
    dot_general x3 -> x5, matrix products: 2.8 us -> 7.51 us  [contract_rows(): lax.dot_general(left, right, (((0,), (0,)), ((), ())), precision=precisio...]
    pallas_call x4 -> x2, Pallas kernels: 8.32 us -> 3.86 us  [indexed_kernel(): pl.pallas_call(body, grid_spec=pltpu.PrefetchScalarGridSpec(num_scalar_pr...]
    dynamic_update_slice x4 -> x11, local copies, waits for them, and re-layouts: 0.05 us -> 3.97 us  [in_order(): whole = lax.dynamic_update_index_in_dim(whole, parts[by], (me - by) % n, 0)]
    ppermute x12, starting transfers between devices: 17.2 us -> 13.3 us  [shift_tp(): return lax.ppermute(x, 'tp', [(i, (i + by) % N_TP) for i in range(N_TP)])]
    ppermute x12, waiting for transfers between devices: 1.23 us -> 5.09 us  [shift_tp(): return lax.ppermute(x, 'tp', [(i, (i + by) % N_TP) for i in range(N_TP)])]
  transfers between devices with their start and end apart: 23 -> 23, of which waited for: 8 -> 10; matrix products, arithmetic and copies ran while one was open for 1% -> 19% of each run, Pallas kernels for 26% -> 8%
where the time goes in v3:
time: 144 us; the launch traced here: 143 us
  blocking collectives  39.1 us (27%)
  starting transfers between devices  34.4 us (24%)
  matrix products  27.6 us (19%)
  waiting for transfers between devices  22 us (15%)
  Pallas kernels  13.9 us (10%)
  local copies, waits for them, and re-layouts  5.24 us (4%)
    all_to_all x2, blocking collectives, exchange(): return lax.all_to_all(x, 'fsdp', 0, 0, axis_index_groups=groups)  39.1 us
    all_to_all x2, waiting for transfers between devices, exchange(): return lax.all_to_all(x, 'fsdp', 0, 0, axis_index_groups=groups)  13.4 us
    ppermute x12, starting transfers between devices, shift_tp(): return lax.ppermute(x, 'tp', [(i, (i + by) % N_TP) for i in range(N_TP)])  13.3 us
    dot_general x2, matrix products, per_device(): product = jnp.dot(grad, bases[w], preferred_element_type=jnp.float32)  11.9 us
    ppermute x6, starting transfers between devices, swap_cores(): return lax.ppermute(x, 'rep', [(0, 1), (1, 0)])  11 us
    all_to_all x2, starting transfers between devices, exchange(): return lax.all_to_all(x, 'fsdp', 0, 0, axis_index_groups=groups)  8.01 us
    pallas_call x1, Pallas kernels, inverse_factor(): pl.pallas_call(inverse_kernel, out_shape=jax.ShapeDtypeStruct((RANK, RANK...  7.84 us
    dot_general x5, matrix products, contract_rows(): lax.dot_general(left, right, (((0,), (0,)), ((), ())), precision=precisio...  7.51 us
  transfers between devices with their start and end apart: 23, of which 10 were waited for; matrix products, arithmetic and copies ran while one was open for 19% of the time, Pallas kernels for 8%

profile of v3, /device:TPU:1, one launch (start us, length us, event | category | flops | bytes accessed | tf_op | source)
XLA Modules:
  0.0 143.5 jit_solution(5911502157796480332)
XLA Ops:
  0.6 3.4 %collective-permute-start.5 = (bf16[512,256]{1,0:T(8,128)(2,1)}, bf16[512,256]{1,0:T(8,128)(2,1)S(1)}, u32[]{:S(2)}, u32[]{:S(2)}) collective-permute-start(bf16[512,256]{1,0:T(8,128)(2,1)} %refs_0_.1), channel_id=1, source_target_pairs={{0,3},{1,0},{2,1},{3,2},{4,7},{5,4},{6,5},{7,6},{8,11},{9,8},{10,9... | collective-permute-start | bytes 786440 | tf_op jit(solution)/shard_map/ppermute | solution.py:42
  4.2 2.5 %collective-permute-start.2 = (bf16[512,256]{1,0:T(8,128)(2,1)}, bf16[512,256]{1,0:T(8,128)(2,1)}, u32[]{:S(2)}, u32[]{:S(2)}) collective-permute-start(bf16[512,256]{1,0:T(8,128)(2,1)} %refs_1_.1), channel_id=1, source_target_pairs={{0,3},{1,0},{2,1},{3,2},{4,7},{5,4},{6,5},{7,6},{8,11},{9,8},{10,9... | collective-permute-start | bytes 786440 | tf_op jit(solution)/shard_map/ppermute | solution.py:42
  6.7 6.0 %convolution_convert_fusion.5.refs_6_.refs_8_.refs_10_.refs_2_ = bf16[2048,256]{1,0:T(8,128)(2,1)S(1)} fusion(bf16[2048,2048]{1,0:T(8,128)(2,1)} %param.9, bf16[2048,256]{1,0:T(8,128)(2,1)} %refs_14_.1), kind=kOutput, calls=%fused_computation.13 | convolution fusion | flops 2148007936 | bytes 10485760 | tf_op jit(solution)/shard_map/dot_general | solution.py:283
  15.9 2.5 %collective-permute-start.3 = (bf16[512,256]{1,0:T(8,128)(2,1)}, bf16[512,256]{1,0:T(8,128)(2,1)S(1)}, u32[]{:S(2)}, u32[]{:S(2)}) collective-permute-start(bf16[512,256]{1,0:T(8,128)(2,1)} %collective-permute-done.2.refs_5_), channel_id=1, source_target_pairs={{0,3},{1,0},{2,1},{3,2},{4,7},{5,4},{6,5},{7,6},{8,11},{9,8},{10,9... | collective-permute-start | bytes 786440 | tf_op jit(solution)/shard_map/ppermute | solution.py:42
  18.3 5.9 %convolution_convert_fusion.4.refs_7_.refs_9_.refs_11_.refs_3_ = bf16[2048,256]{1,0:T(8,128)(2,1)S(1)} fusion(bf16[2048,2048]{1,0:T(8,128)(2,1)} %param.11, bf16[2048,256]{1,0:T(8,128)(2,1)S(1)} %copy-done.3), kind=kOutput, calls=%fused_computation.12 | convolution fusion | flops 2148007936 | bytes 10485760 | tf_op jit(solution)/shard_map/dot_general | solution.py:283
  24.3 3.0 %near_tokens.1 = (f32[256,256]{1,0:T(8,128)S(1)}, f32[256,256]{1,0:T(8,128)S(1)}) custom-call(s32[5]{0:T(128)S(1)} %stack.23.index, bf16[512,256]{1,0:T(8,128)(2,1)S(1)} %copy-done.5, bf16[512,256]{1,0:T(8,128)(2,1)S(1)} %copy-done.4, bf16[512,256]{1,0:T(8,128)(2,1)S(1)} %collective-permute-done.refs_2_, ...), custom_call_target="tpu_custom_call" | custom-call | flops 1048576 | bytes 1048576 | tf_op jit(solution)/shard_map/near_tokens/pallas_call | solution.py:123
  28.9 2.3 %collective-permute-start.6 = (bf16[256,256]{1,0:T(8,128)(2,1)S(1)}, bf16[256,256]{1,0:T(8,128)(2,1)S(1)}, u32[]{:S(2)}, u32[]{:S(2)}) collective-permute-start(bf16[256,256]{1,0:T(8,128)(2,1)S(1)} %get-tuple-element.31), channel_id=1, source_target_pairs={{0,128},{128,0},{1,129},{129,1},{2,130},{130,2},{3,131},{131,3},{4... | collective-permute-start | bytes 393224 | tf_op jit(solution)/shard_map/ppermute | solution.py:53
  32.2 1.6 %collective-permute-start.9 = (bf16[256,256]{1,0:T(8,128)(2,1)S(1)}, bf16[256,256]{1,0:T(8,128)(2,1)S(1)}, u32[]{:S(2)}, u32[]{:S(2)}) collective-permute-start(bf16[256,256]{1,0:T(8,128)(2,1)S(1)} %add_convert_fusion), channel_id=1, source_target_pairs={{0,3},{1,0},{2,1},{3,2},{4,7},{5,4},{6,5},{7,6},{8,11},{9,8},{10,9... | collective-permute-start | bytes 393224 | tf_op jit(solution)/shard_map/ppermute | solution.py:42
  35.3 1.7 %bitcast_dynamic-update-slice_fusion = (bf16[4,512,256]{2,1,0:T(8,128)(2,1)}, bf16[4,512,256]{2,1,0:T(8,128)(2,1)S(1)}) fusion(bf16[4,512,256]{2,1,0:T(8,128)(2,1)} %bitcast_dynamic-update-slice_fusion.1, s32[]{:T(128)S(6)} %select_n.147, bf16[512,256]{1,0:T(8,128)(2,1)} %collective-permute-done.2.refs_5_, ...), kind=kLoop, calls=%fused_computation.23 | loop fusion | bytes 1048580 | tf_op jit(solution)/shard_map/jit(dynamic_update_index_in_dim)/dynamic_update_slice | solution.py:64
  37.0 2.3 %fusion.1 = bf16[256,2048]{1,0:T(8,128)(2,1)S(1)} fusion(bf16[2048,256]{1,0:T(8,128)(2,1)S(1)} %bitcast.63, bf16[2048,2048]{1,0:T(8,128)(2,1)S(1)} %bitcast.60, bf16[1,256,2048]{2,1,0:T(8,128)(2,1)S(1)} %copy-done), kind=kOutput, calls=%fused_computation.5 | convolution fusion | flops 2149056512 | bytes 11534336 | tf_op jit(solution)/shard_map/dot_general | solution.py:27
  39.8 3.1 %collective-permute-done.7 = bf16[256,256]{1,0:T(8,128)(2,1)S(1)} collective-permute-done((bf16[256,256]{1,0:T(8,128)(2,1)S(1)}, bf16[256,256]{1,0:T(8,128)(2,1)S(1)}, u32[]{:S(2)}, u32[]{:S(2)}) %collective-permute-start.7) | collective-permute-done | bytes 131104 | tf_op jit(solution)/shard_map/ppermute | solution.py:42
  43.9 3.6 %fusion.2 = bf16[256,2048]{1,0:T(8,128)(2,1)S(1)} fusion(bf16[2048,256]{1,0:T(8,128)(2,1)} %bitcast.16, bf16[2048,2048]{1,0:T(8,128)(2,1)S(1)} %bitcast.62, bf16[1,256,2048]{2,1,0:T(8,128)(2,1)S(1)} %copy-done.1), kind=kOutput, calls=%fused_computation.6 | convolution fusion | flops 2149056512 | bytes 11534336 | tf_op jit(solution)/shard_map/dot_general | solution.py:27
  49.2 2.0 %collective-permute-done.11.other = bf16[2048,256]{1,0:T(8,128)(2,1)S(1)} collective-permute-done((bf16[2048,256]{1,0:T(8,128)(2,1)S(1)}, bf16[2048,256]{1,0:T(8,128)(2,1)S(1)}, u32[]{:S(2)}, u32[]{:S(2)}) %collective-permute-start.11) | collective-permute-done | bytes 1048608 | tf_op jit(solution)/shard_map/ppermute | solution.py:53
  51.5 20.2 %all_to_all.20.pieces = bf16[4,576,256]{2,1,0:T(8,128)(2,1)S(1)} all-to-all(bf16[4,576,256]{2,1,0:T(8,128)(2,1)S(1)} %pack_quarters.1), channel_id=1, replica_groups={{0,32,64,96},{4,36,68,100},{8,40,72,104},{12,44,76,108},{16,48,80,112},..., dimensions={0} | all-to-all | bytes 2359296 | tf_op jit(solution)/shard_map/all_to_all | solution.py:86
  71.8 18.9 %all_to_all.21.pieces = bf16[8,80,256]{2,1,0:T(8,128)(2,1)S(1)} all-to-all(bf16[8,80,256]{2,1,0:T(8,128)(2,1)S(1)} %sum_over_y.1), channel_id=1, replica_groups={{0,4,8,12,16,20,24,28},{32,36,40,44,48,52,56,60},{64,68,72,76,80,84,88,..., dimensions={0} | all-to-all | bytes 655360 | tf_op jit(solution)/shard_map/all_to_all | solution.py:86
  91.6 3.5 %all-to-all-start.2 = ((bf16[8,80,256]{2,1,0:T(8,128)(2,1)}), bf16[8,80,256]{2,1,0:T(8,128)(2,1)S(1)}, u32[]{:S(2)}, u32[]{:S(2)}) async-start(bf16[8,80,256]{2,1,0:T(8,128)(2,1)} %sum_over_z.1), calls=%async_computation.2 | async-start | bytes 655360 | tf_op jit(solution)/shard_map/all_to_all | solution.py:86
  95.1 10.1 %all-to-all-done.2.pieces = bf16[8,80,256]{2,1,0:T(8,128)(2,1)S(1)} async-done(((bf16[8,80,256]{2,1,0:T(8,128)(2,1)}), bf16[8,80,256]{2,1,0:T(8,128)(2,1)S(1)}, u32[]{:S(2)}, u32[]{:S(2)}) %all-to-all-start.2) | async-done | bytes 327712 | tf_op jit(solution)/shard_map/all_to_all | solution.py:86
  108.3 4.5 %all-to-all-start.3 = ((bf16[4,512,256]{2,1,0:T(8,128)(2,1)}), bf16[4,512,256]{2,1,0:T(8,128)(2,1)}, u32[]{:S(2)}, u32[]{:S(2)}) async-start(bf16[4,512,256]{2,1,0:T(8,128)(2,1)} %get-tuple-element.41), calls=%async_computation.3 | async-start | bytes 2097152 | tf_op jit(solution)/shard_map/all_to_all | solution.py:86
  113.0 7.8 %inverse_factor.1 = f32[256,256]{1,0:T(8,128)S(1)} custom-call(f32[256,256]{1,0:T(8,128)S(1)} %bitcast.58), custom_call_target="tpu_custom_call" | custom-call | flops 8000000000 | bytes 1048576 | tf_op jit(solution)/shard_map/inverse_factor/pallas_call | solution.py:238
  120.8 3.2 %all-to-all-done.3 = bf16[4,512,256]{2,1,0:T(8,128)(2,1)} async-done(((bf16[4,512,256]{2,1,0:T(8,128)(2,1)}), bf16[4,512,256]{2,1,0:T(8,128)(2,1)}, u32[]{:S(2)}, u32[]{:S(2)}) %all-to-all-start.3) | async-done | bytes 1048608 | tf_op jit(solution)/shard_map/all_to_all | solution.py:86
  124.1 1.8 %multiply_reduce_fusion = (f32[256]{0:T(256)S(1)}, bf16[2048,256]{1,0:T(8,128)(2,1)S(1)}) fusion(bf16[2048,256]{1,0:T(8,128)(2,1)} %bitcast.22, f32[256,256]{1,0:T(8,128)S(1)} %inverse_factor.1), kind=kOutput, calls=%fused_computation.16 | convolution fusion | flops 270073600 | bytes 2360320 | tf_op jit(solution)/shard_map/dot_general | solution.py:346
  125.9 5.7 %collective-permute-start.19 = (bf16[2048,256]{1,0:T(8,128)(2,1)S(1)}, bf16[2048,256]{1,0:T(8,128)(2,1)S(1)}, u32[]{:S(2)}, u32[]{:S(2)}) collective-permute-start(bf16[2048,256]{1,0:T(8,128)(2,1)S(1)} %get-tuple-element.51), channel_id=1, source_target_pairs={{0,128},{128,0},{1,129},{129,1},{2,130},{130,2},{3,131},{131,3},{4... | collective-permute-start | bytes 3145736 | tf_op jit(solution)/shard_map/ppermute | solution.py:53
  137.0 1.9 %collective-permute-start.20 = (f32[1,256]{1,0:T(1,128)S(1)}, f32[1,256]{1,0:T(1,128)S(1)}, u32[]{:S(2)}, u32[]{:S(2)}) collective-permute-start(f32[1,256]{1,0:T(1,128)S(1)} %rsqrt_multiply_fusion), channel_id=1, source_target_pairs={{0,128},{128,0},{1,129},{129,1},{2,130},{130,2},{3,131},{131,3},{4... | collective-permute-start | bytes 3080 | tf_op jit(solution)/shard_map/ppermute | solution.py:53
  140.4 1.5 %convolution_convert_fusion = bf16[256,2048]{1,0:T(8,128)(2,1)} fusion(bf16[2048,256]{1,0:T(8,128)(2,1)S(1)} %collective-permute-done.19, bf16[2048,256]{1,0:T(8,128)(2,1)S(1)} %get-tuple-element.51, pred[]{:T(512)S(6)} %eq.20, f32[256]{0:T(256)S(1)} %bitcast.65, f32[256,256]{1,0:T(8,128)S(1)} %collective-permute-done.15, f32[256,256]{1,0:T(8,128)S(1)} %fusion.16), kind=kOutput, calls=%fused_computation.8 | convolution fusion | flops 269680640 | bytes 3671041 | tf_op jit(solution)/shard_map/dot_general | solution.py:365
  (85 shorter events, 23.3 us)
Async XLA Ops:
  0.6 23.6 %collective-permute-start.5 = (bf16[512,256]{1,0:T(8,128)(2,1)}, bf16[512,256]{1,0:T(8,128)(2,1)S(1)}, u32[]{:S(2)}, u32[]{:S(2)}) collective-permute-start(bf16[512,256]{1,0:T(8,128)(2,1)} %refs_0_.1), channel_id=1, source_target_pairs={{0,3},{1,0},{2,1},{3,2},{4,7},{5,4},{6,5},{7,6},{8,11},{9,8},{10,9... | collective-permute-start | bytes 786440 | tf_op jit(solution)/shard_map/ppermute | solution.py:42
  4.0 10.7 %collective-permute-start = (bf16[512,256]{1,0:T(8,128)(2,1)}, bf16[512,256]{1,0:T(8,128)(2,1)S(1)}, u32[]{:S(2)}, u32[]{:S(2)}) collective-permute-start(bf16[512,256]{1,0:T(8,128)(2,1)} %refs_0_.1), channel_id=1, source_target_pairs={{0,1},{1,2},{2,3},{3,0},{4,5},{5,6},{6,7},{7,4},{8,9},{9,10},{10,1... | collective-permute-start | bytes 786440 | tf_op jit(solution)/shard_map/ppermute | solution.py:42
  4.0 20.2 %collective-permute-start.4 = (bf16[512,256]{1,0:T(8,128)(2,1)}, bf16[512,256]{1,0:T(8,128)(2,1)S(1)}, u32[]{:S(2)}, u32[]{:S(2)}) collective-permute-start(bf16[512,256]{1,0:T(8,128)(2,1)} %refs_1_.1), channel_id=1, source_target_pairs={{0,1},{1,2},{2,3},{3,0},{4,5},{5,6},{6,7},{7,4},{8,9},{9,10},{10,1... | collective-permute-start | bytes 786440 | tf_op jit(solution)/shard_map/ppermute | solution.py:42
  4.2 10.7 %collective-permute-start.2 = (bf16[512,256]{1,0:T(8,128)(2,1)}, bf16[512,256]{1,0:T(8,128)(2,1)}, u32[]{:S(2)}, u32[]{:S(2)}) collective-permute-start(bf16[512,256]{1,0:T(8,128)(2,1)} %refs_1_.1), channel_id=1, source_target_pairs={{0,3},{1,0},{2,1},{3,2},{4,7},{5,4},{6,5},{7,6},{8,11},{9,8},{10,9... | collective-permute-start | bytes 786440 | tf_op jit(solution)/shard_map/ppermute | solution.py:42
  14.9 13.1 %collective-permute-start.1 = (bf16[512,256]{1,0:T(8,128)(2,1)S(1)}, bf16[512,256]{1,0:T(8,128)(2,1)S(1)}, u32[]{:S(2)}, u32[]{:S(2)}) collective-permute-start(bf16[512,256]{1,0:T(8,128)(2,1)S(1)} %collective-permute-done.refs_2_), channel_id=1, source_target_pairs={{0,1},{1,2},{2,3},{3,0},{4,5},{5,6},{6,7},{7,4},{8,9},{9,10},{10,1... | collective-permute-start | bytes 786440 | tf_op jit(solution)/shard_map/ppermute | solution.py:42
  15.9 12.1 %collective-permute-start.3 = (bf16[512,256]{1,0:T(8,128)(2,1)}, bf16[512,256]{1,0:T(8,128)(2,1)S(1)}, u32[]{:S(2)}, u32[]{:S(2)}) collective-permute-start(bf16[512,256]{1,0:T(8,128)(2,1)} %collective-permute-done.2.refs_5_), channel_id=1, source_target_pairs={{0,3},{1,0},{2,1},{3,2},{4,7},{5,4},{6,5},{7,6},{8,11},{9,8},{10,9... | collective-permute-start | bytes 786440 | tf_op jit(solution)/shard_map/ppermute | solution.py:42
  18.3 18.6 %slice-start = ((s8[8388608]{0:T(1024)(128)(4,1)}), s8[4194304]{0:T(1024)(128)(4,1)S(1)}, s32[]{:S(2)}) async-start(s8[8388608]{0:T(1024)(128)(4,1)} %bitcast.59), calls=%async_computation.4 | async-start | bytes 8388608
  28.9 3.3 %collective-permute-start.6 = (bf16[256,256]{1,0:T(8,128)(2,1)S(1)}, bf16[256,256]{1,0:T(8,128)(2,1)S(1)}, u32[]{:S(2)}, u32[]{:S(2)}) collective-permute-start(bf16[256,256]{1,0:T(8,128)(2,1)S(1)} %get-tuple-element.31), channel_id=1, source_target_pairs={{0,128},{128,0},{1,129},{129,1},{2,130},{130,2},{3,131},{131,3},{4... | collective-permute-start | bytes 393224 | tf_op jit(solution)/shard_map/ppermute | solution.py:53
  32.2 7.1 %collective-permute-start.9 = (bf16[256,256]{1,0:T(8,128)(2,1)S(1)}, bf16[256,256]{1,0:T(8,128)(2,1)S(1)}, u32[]{:S(2)}, u32[]{:S(2)}) collective-permute-start(bf16[256,256]{1,0:T(8,128)(2,1)S(1)} %add_convert_fusion), channel_id=1, source_target_pairs={{0,3},{1,0},{2,1},{3,2},{4,7},{5,4},{6,5},{7,6},{8,11},{9,8},{10,9... | collective-permute-start | bytes 393224 | tf_op jit(solution)/shard_map/ppermute | solution.py:42
  33.8 6.0 %collective-permute-start.8 = (bf16[256,256]{1,0:T(8,128)(2,1)S(1)}, bf16[256,256]{1,0:T(8,128)(2,1)S(1)}, u32[]{:S(2)}, u32[]{:S(2)}) collective-permute-start(bf16[256,256]{1,0:T(8,128)(2,1)S(1)} %add_convert_fusion), channel_id=1, source_target_pairs={{0,2},{1,3},{2,0},{3,1},{4,6},{5,7},{6,4},{7,5},{8,10},{9,11},{10,... | collective-permute-start | bytes 393224 | tf_op jit(solution)/shard_map/ppermute | solution.py:42
  33.8 9.1 %collective-permute-start.7 = (bf16[256,256]{1,0:T(8,128)(2,1)S(1)}, bf16[256,256]{1,0:T(8,128)(2,1)S(1)}, u32[]{:S(2)}, u32[]{:S(2)}) collective-permute-start(bf16[256,256]{1,0:T(8,128)(2,1)S(1)} %add_convert_fusion), channel_id=1, source_target_pairs={{0,1},{1,2},{2,3},{3,0},{4,5},{5,6},{6,7},{7,4},{8,9},{9,10},{10,1... | collective-permute-start | bytes 393224 | tf_op jit(solution)/shard_map/ppermute | solution.py:42
  43.0 4.5 %collective-permute-start.10 = (bf16[256,256]{1,0:T(8,128)(2,1)S(1)}, bf16[256,256]{1,0:T(8,128)(2,1)S(1)}, u32[]{:S(2)}, u32[]{:S(2)}) collective-permute-start(bf16[256,256]{1,0:T(8,128)(2,1)S(1)} %fusion.17), channel_id=1, source_target_pairs={{0,128},{128,0},{1,129},{129,1},{2,130},{130,2},{3,131},{131,3},{4... | collective-permute-start | bytes 393224 | tf_op jit(solution)/shard_map/ppermute | solution.py:53
  48.5 2.7 %collective-permute-start.11 = (bf16[2048,256]{1,0:T(8,128)(2,1)S(1)}, bf16[2048,256]{1,0:T(8,128)(2,1)S(1)}, u32[]{:S(2)}, u32[]{:S(2)}) collective-permute-start(bf16[2048,256]{1,0:T(8,128)(2,1)S(1)} %get-tuple-element.52), channel_id=1, source_target_pairs={{0,128},{128,0},{1,129},{129,1},{2,130},{130,2},{3,131},{131,3},{4... | collective-permute-start | bytes 3145736 | tf_op jit(solution)/shard_map/ppermute | solution.py:53
  91.6 13.7 %all-to-all-start.2 = ((bf16[8,80,256]{2,1,0:T(8,128)(2,1)}), bf16[8,80,256]{2,1,0:T(8,128)(2,1)S(1)}, u32[]{:S(2)}, u32[]{:S(2)}) async-start(bf16[8,80,256]{2,1,0:T(8,128)(2,1)} %sum_over_z.1), calls=%async_computation.2 | async-start | bytes 655360 | tf_op jit(solution)/shard_map/all_to_all | solution.py:86
  106.3 6.7 %collective-permute-start.14 = (f32[64,256]{1,0:T(8,128)S(1)}, f32[64,256]{1,0:T(8,128)S(1)}, u32[]{:S(2)}, u32[]{:S(2)}) collective-permute-start(f32[64,256]{1,0:T(8,128)S(1)} %get-tuple-element.40), channel_id=1, source_target_pairs={{0,96},{4,100},{8,104},{12,108},{16,112},{20,116},{24,120},{28,124... | collective-permute-start | bytes 196616 | tf_op jit(solution)/shard_map/ppermute | solution.py:49
  107.2 5.7 %collective-permute-start.13 = (f32[64,256]{1,0:T(8,128)S(1)}, f32[64,256]{1,0:T(8,128)S(1)}, u32[]{:S(2)}, u32[]{:S(2)}) collective-permute-start(f32[64,256]{1,0:T(8,128)S(1)} %get-tuple-element.40), channel_id=1, source_target_pairs={{0,64},{4,68},{8,72},{12,76},{16,80},{20,84},{24,88},{28,92},{32,9... | collective-permute-start | bytes 196616 | tf_op jit(solution)/shard_map/ppermute | solution.py:49
  108.3 4.5 %collective-permute-start.12 = (f32[64,256]{1,0:T(8,128)S(1)}, f32[64,256]{1,0:T(8,128)S(1)}, u32[]{:S(2)}, u32[]{:S(2)}) collective-permute-start(f32[64,256]{1,0:T(8,128)S(1)} %get-tuple-element.40), channel_id=1, source_target_pairs={{0,32},{4,36},{8,40},{12,44},{16,48},{20,52},{24,56},{28,60},{32,6... | collective-permute-start | bytes 196616 | tf_op jit(solution)/shard_map/ppermute | solution.py:49
  108.3 15.7 %all-to-all-start.3 = ((bf16[4,512,256]{2,1,0:T(8,128)(2,1)}), bf16[4,512,256]{2,1,0:T(8,128)(2,1)}, u32[]{:S(2)}, u32[]{:S(2)}) async-start(bf16[4,512,256]{2,1,0:T(8,128)(2,1)} %get-tuple-element.41), calls=%async_computation.3 | async-start | bytes 2097152 | tf_op jit(solution)/shard_map/all_to_all | solution.py:86
  125.9 8.3 %collective-permute-start.19 = (bf16[2048,256]{1,0:T(8,128)(2,1)S(1)}, bf16[2048,256]{1,0:T(8,128)(2,1)S(1)}, u32[]{:S(2)}, u32[]{:S(2)}) collective-permute-start(bf16[2048,256]{1,0:T(8,128)(2,1)S(1)} %get-tuple-element.51), channel_id=1, source_target_pairs={{0,128},{128,0},{1,129},{129,1},{2,130},{130,2},{3,131},{131,3},{4... | collective-permute-start | bytes 3145736 | tf_op jit(solution)/shard_map/ppermute | solution.py:53
  132.0 2.2 %collective-permute-start.15 = (f32[256,256]{1,0:T(8,128)S(1)}, f32[256,256]{1,0:T(8,128)S(1)}, u32[]{:S(2)}, u32[]{:S(2)}) collective-permute-start(f32[256,256]{1,0:T(8,128)S(1)} %fusion.16), channel_id=1, source_target_pairs={{0,128},{128,0},{1,129},{129,1},{2,130},{130,2},{3,131},{131,3},{4... | collective-permute-start | bytes 786440 | tf_op jit(solution)/shard_map/ppermute | solution.py:53
  132.1 3.6 %collective-permute-start.18 = (f32[1,256]{1,0:T(1,128)S(1)}, f32[1,256]{1,0:T(1,128)S(1)}, u32[]{:S(2)}, u32[]{:S(2)}) collective-permute-start(f32[1,256]{1,0:T(1,128)S(1)} %bitcast.66), channel_id=1, source_target_pairs={{0,3},{1,0},{2,1},{3,2},{4,7},{5,4},{6,5},{7,6},{8,11},{9,8},{10,9... | collective-permute-start | bytes 3080 | tf_op jit(solution)/shard_map/ppermute | solution.py:42
  132.8 3.9 %collective-permute-start.17 = (f32[1,256]{1,0:T(1,128)S(1)}, f32[1,256]{1,0:T(1,128)S(1)}, u32[]{:S(2)}, u32[]{:S(2)}) collective-permute-start(f32[1,256]{1,0:T(1,128)S(1)} %bitcast.67), channel_id=1, source_target_pairs={{0,2},{1,3},{2,0},{3,1},{4,6},{5,7},{6,4},{7,5},{8,10},{9,11},{10,... | collective-permute-start | bytes 3080 | tf_op jit(solution)/shard_map/ppermute | solution.py:42
  132.8 4.2 %collective-permute-start.16 = (f32[1,256]{1,0:T(1,128)S(1)}, f32[1,256]{1,0:T(1,128)S(1)}, u32[]{:S(2)}, u32[]{:S(2)}) collective-permute-start(f32[1,256]{1,0:T(1,128)S(1)} %bitcast.68), channel_id=1, source_target_pairs={{0,1},{1,2},{2,3},{3,0},{4,5},{5,6},{6,7},{7,4},{8,9},{9,10},{10,1... | collective-permute-start | bytes 3080 | tf_op jit(solution)/shard_map/ppermute | solution.py:42
  137.0 3.4 %collective-permute-start.20 = (f32[1,256]{1,0:T(1,128)S(1)}, f32[1,256]{1,0:T(1,128)S(1)}, u32[]{:S(2)}, u32[]{:S(2)}) collective-permute-start(f32[1,256]{1,0:T(1,128)S(1)} %rsqrt_multiply_fusion), channel_id=1, source_target_pairs={{0,128},{128,0},{1,129},{129,1},{2,130},{130,2},{3,131},{131,3},{4... | collective-permute-start | bytes 3080 | tf_op jit(solution)/shard_map/ppermute | solution.py:53
  (9 other events, 69.9 us)

commit v4 on v3

--- a/solution.py
+++ b/solution.py
@@ -116,6 +116,13 @@
     first = index[N_TP] == 0
     mine[...] = jnp.where(first, query, output)
     other[...] = jnp.where(first, output, query).astype(jnp.bfloat16)
+
+
+def order_kernel(index, *refs):
+    for w in range(2):
+        far, own, up, down, out = refs[w::2]
+        for at, tokens in enumerate((far, own, up, down)):
+            out[pl.ds(index[at], 1)] = tokens[...][None]
 
 
 def indexed_kernel(body, index, operands, results, name):
@@ -300,15 +307,22 @@
         "far_tokens",
     )
     mine = mine + swap_cores(other).astype(jnp.float32)
-    mine, far = lax.optimization_barrier((mine.astype(jnp.bfloat16), far))
+    ordered = indexed_kernel(
+        order_kernel,
+        index,
+        [all_of(a) for a in far + own + up + down],
+        [all_of(shape(jnp.bfloat16, N_TP, count, rows))] * 2,
+        "order_tokens",
+    )
+    mine, ordered = lax.optimization_barrier((mine.astype(jnp.bfloat16), ordered))
     buffers = [
         (
             moments[w][0].astype(jnp.float32)
-            + contract_rows(in_order([own[w], up[w], far[w], down[w]], tp), grads[w])
+            + contract_rows(ordered[w].reshape(N_TP * count, rows), grads[w])
         ).astype(jnp.bfloat16)
         for w in range(2)
     ]
-    parts, buffers[0] = lax.optimization_barrier((from_all(mine, shift_tp), buffers[0]))
+    parts, buffers = lax.optimization_barrier((from_all(mine, shift_tp), buffers))
     power = total(parts)
     power_b = power.astype(jnp.bfloat16)
     powers_b = split([power_b, swap_cores(power_b)])

time: 144 us -> 139 us (0.965)
  local copies, waits for them, and re-layouts: 5.24 us -> 0.87 us
  waiting for transfers between devices: 22 us -> 23.9 us
    dynamic_update_slice x11 -> x4, local copies, waits for them, and re-layouts: 3.97 us -> 0.05 us  [in_order(): whole = lax.dynamic_update_index_in_dim(whole, parts[by], (me - by) % n, 0)]
    ppermute x12, waiting for transfers between devices: 5.09 us -> 6.86 us  [shift_tp(): return lax.ppermute(x, 'tp', [(i, (i + by) % N_TP) for i in range(N_TP)])]
    pallas_call x2 -> x3, Pallas kernels: 3.86 us -> 3.29 us  [indexed_kernel(): pl.pallas_call(body, grid_spec=pltpu.PrefetchScalarGridSpec(num_scalar_pr...]
  transfers between devices with their start and end apart: 23 -> 23, of which waited for: 10 -> 11; matrix products, arithmetic and copies ran while one was open for 19% -> 15% of each run, Pallas kernels for 8% -> 7%
where the time goes in v4:
time: 139 us
  blocking collectives  38 us (27%)
  starting transfers between devices  34.8 us (25%)
  matrix products  26.4 us (19%)
  waiting for transfers between devices  23.9 us (17%)
  Pallas kernels  13.3 us (10%)
    all_to_all x2, blocking collectives, exchange(): return lax.all_to_all(x, 'fsdp', 0, 0, axis_index_groups=groups)  38 us
    ppermute x12, starting transfers between devices, shift_tp(): return lax.ppermute(x, 'tp', [(i, (i + by) % N_TP) for i in range(N_TP)])  13.6 us
    all_to_all x2, waiting for transfers between devices, exchange(): return lax.all_to_all(x, 'fsdp', 0, 0, axis_index_groups=groups)  13.5 us
    dot_general x2, matrix products, per_device(): product = jnp.dot(grad, bases[w], preferred_element_type=jnp.float32)  11.8 us
    ppermute x6, starting transfers between devices, swap_cores(): return lax.ppermute(x, 'rep', [(0, 1), (1, 0)])  11.2 us
    all_to_all x2, starting transfers between devices, exchange(): return lax.all_to_all(x, 'fsdp', 0, 0, axis_index_groups=groups)  7.91 us
    pallas_call x1, Pallas kernels, inverse_factor(): pl.pallas_call(inverse_kernel, out_shape=jax.ShapeDtypeStruct((RANK, RANK...  7.84 us
    ppermute x12, waiting for transfers between devices, shift_tp(): return lax.ppermute(x, 'tp', [(i, (i + by) % N_TP) for i in range(N_TP)])  6.86 us
  transfers between devices with their start and end apart: 23, of which 11 were waited for; matrix products, arithmetic and copies ran while one was open for 15% of the time, Pallas kernels for 7%

profile of v4, /device:TPU:1, one launch (start us, length us, event | category | flops | bytes accessed | tf_op | source)
XLA Modules:
  0.0 138.5 jit_solution(13996105365962450547)
XLA Ops:
  0.6 3.4 %collective-permute-start.5 = (bf16[512,256]{1,0:T(8,128)(2,1)}, bf16[512,256]{1,0:T(8,128)(2,1)S(1)}, u32[]{:S(2)}, u32[]{:S(2)}) collective-permute-start(bf16[512,256]{1,0:T(8,128)(2,1)} %refs_2_.1), channel_id=1, source_target_pairs={{0,3},{1,0},{2,1},{3,2},{4,7},{5,4},{6,5},{7,6},{8,11},{9,8},{10,9... | collective-permute-start | bytes 786440 | tf_op jit(solution)/shard_map/ppermute | solution.py:42
  4.2 2.5 %collective-permute-start.2 = (bf16[512,256]{1,0:T(8,128)(2,1)}, bf16[512,256]{1,0:T(8,128)(2,1)S(1)}, u32[]{:S(2)}, u32[]{:S(2)}) collective-permute-start(bf16[512,256]{1,0:T(8,128)(2,1)} %refs_3_.1), channel_id=1, source_target_pairs={{0,3},{1,0},{2,1},{3,2},{4,7},{5,4},{6,5},{7,6},{8,11},{9,8},{10,9... | collective-permute-start | bytes 786440 | tf_op jit(solution)/shard_map/ppermute | solution.py:42
  6.7 6.0 %convolution_convert_fusion.5.refs_6_.refs_8_.refs_10_.refs_2_ = bf16[2048,256]{1,0:T(8,128)(2,1)S(1)} fusion(bf16[2048,2048]{1,0:T(8,128)(2,1)} %param.9, bf16[2048,256]{1,0:T(8,128)(2,1)} %refs_14_.1), kind=kOutput, calls=%fused_computation.11 | convolution fusion | flops 2148007936 | bytes 10485760 | tf_op jit(solution)/shard_map/dot_general | solution.py:290
  12.9 2.0 %collective-permute-done.2.refs_5_.refs_7_ = bf16[512,256]{1,0:T(8,128)(2,1)S(1)} collective-permute-done((bf16[512,256]{1,0:T(8,128)(2,1)}, bf16[512,256]{1,0:T(8,128)(2,1)S(1)}, u32[]{:S(2)}, u32[]{:S(2)}) %collective-permute-start.2) | collective-permute-done | bytes 262176 | tf_op jit(solution)/shard_map/ppermute | solution.py:42
  15.8 2.5 %collective-permute-start.3 = (bf16[512,256]{1,0:T(8,128)(2,1)S(1)}, bf16[512,256]{1,0:T(8,128)(2,1)S(1)}, u32[]{:S(2)}, u32[]{:S(2)}) collective-permute-start(bf16[512,256]{1,0:T(8,128)(2,1)S(1)} %collective-permute-done.2.refs_5_.refs_7_), channel_id=1, source_target_pairs={{0,3},{1,0},{2,1},{3,2},{4,7},{5,4},{6,5},{7,6},{8,11},{9,8},{10,9... | collective-permute-start | bytes 786440 | tf_op jit(solution)/shard_map/ppermute | solution.py:42
  18.2 5.9 %convolution_convert_fusion.4.refs_7_.refs_9_.refs_11_.refs_3_ = bf16[2048,256]{1,0:T(8,128)(2,1)S(1)} fusion(bf16[2048,2048]{1,0:T(8,128)(2,1)} %param.11, bf16[2048,256]{1,0:T(8,128)(2,1)S(1)} %copy-done.3), kind=kOutput, calls=%fused_computation.10 | convolution fusion | flops 2148007936 | bytes 10485760 | tf_op jit(solution)/shard_map/dot_general | solution.py:290
  24.2 1.7 %near_tokens.1 = (f32[256,256]{1,0:T(8,128)S(1)}, f32[256,256]{1,0:T(8,128)S(1)}) custom-call(s32[5]{0:T(128)S(1)} %stack.23.index, bf16[512,256]{1,0:T(8,128)(2,1)S(1)} %copy-done.4, bf16[512,256]{1,0:T(8,128)(2,1)S(1)} %copy-done.5, bf16[512,256]{1,0:T(8,128)(2,1)S(1)} %collective-permute-done.refs_2_.refs_4_, ...), custom_call_target="tpu_custom_call" | custom-call | flops 1048576 | bytes 1048576 | tf_op jit(solution)/shard_map/near_tokens/pallas_call | solution.py:130
  26.9 1.9 %collective-permute-start.6 = (bf16[256,256]{1,0:T(8,128)(2,1)S(1)}, bf16[256,256]{1,0:T(8,128)(2,1)S(1)}, u32[]{:S(2)}, u32[]{:S(2)}) collective-permute-start(bf16[256,256]{1,0:T(8,128)(2,1)S(1)} %get-tuple-element.34), channel_id=1, source_target_pairs={{0,128},{128,0},{1,129},{129,1},{2,130},{130,2},{3,131},{131,3},{4... | collective-permute-start | bytes 393224 | tf_op jit(solution)/shard_map/ppermute | solution.py:53
  29.8 1.8 %collective-permute-start.9 = (bf16[256,256]{1,0:T(8,128)(2,1)S(1)}, bf16[256,256]{1,0:T(8,128)(2,1)S(1)}, u32[]{:S(2)}, u32[]{:S(2)}) collective-permute-start(bf16[256,256]{1,0:T(8,128)(2,1)S(1)} %add_convert_fusion), channel_id=1, source_target_pairs={{0,3},{1,0},{2,1},{3,2},{4,7},{5,4},{6,5},{7,6},{8,11},{9,8},{10,9... | collective-permute-start | bytes 393224 | tf_op jit(solution)/shard_map/ppermute | solution.py:42
  32.5 2.3 %fusion = bf16[256,2048]{1,0:T(8,128)(2,1)S(1)} fusion(bf16[2048,256]{1,0:T(8,128)(2,1)S(1)} %bitcast.43, bf16[2048,2048]{1,0:T(8,128)(2,1)S(1)} %bitcast.46, bf16[1,256,2048]{2,1,0:T(8,128)(2,1)S(1)} %copy-done), kind=kOutput, calls=%fused_computation.4 | convolution fusion | flops 2149056512 | bytes 11534336 | tf_op jit(solution)/shard_map/dot_general | solution.py:27
  34.9 2.3 %fusion.1 = bf16[256,2048]{1,0:T(8,128)(2,1)S(1)} fusion(bf16[2048,256]{1,0:T(8,128)(2,1)S(1)} %bitcast.42, bf16[2048,2048]{1,0:T(8,128)(2,1)S(1)} %bitcast.48, bf16[1,256,2048]{2,1,0:T(8,128)(2,1)S(1)} %copy-done.1), kind=kOutput, calls=%fused_computation.5 | convolution fusion | flops 2149056512 | bytes 11534336 | tf_op jit(solution)/shard_map/dot_general | solution.py:27
  37.6 3.1 %collective-permute-done.7 = bf16[256,256]{1,0:T(8,128)(2,1)S(1)} collective-permute-done((bf16[256,256]{1,0:T(8,128)(2,1)S(1)}, bf16[256,256]{1,0:T(8,128)(2,1)S(1)}, u32[]{:S(2)}, u32[]{:S(2)}) %collective-permute-start.7) | collective-permute-done | bytes 131104 | tf_op jit(solution)/shard_map/ppermute | solution.py:42
  45.4 1.7 %collective-permute-done.11.other = bf16[2048,256]{1,0:T(8,128)(2,1)S(1)} collective-permute-done((bf16[2048,256]{1,0:T(8,128)(2,1)S(1)}, bf16[2048,256]{1,0:T(8,128)(2,1)S(1)}, u32[]{:S(2)}, u32[]{:S(2)}) %collective-permute-start.11) | collective-permute-done | bytes 1048608 | tf_op jit(solution)/shard_map/ppermute | solution.py:53
  47.3 19.6 %all_to_all.20.pieces = bf16[4,576,256]{2,1,0:T(8,128)(2,1)S(1)} all-to-all(bf16[4,576,256]{2,1,0:T(8,128)(2,1)S(1)} %pack_quarters.1), channel_id=1, replica_groups={{0,32,64,96},{4,36,68,100},{8,40,72,104},{12,44,76,108},{16,48,80,112},..., dimensions={0} | all-to-all | bytes 2359296 | tf_op jit(solution)/shard_map/all_to_all | solution.py:86
  67.1 18.3 %all_to_all.21.pieces = bf16[8,80,256]{2,1,0:T(8,128)(2,1)S(1)} all-to-all(bf16[8,80,256]{2,1,0:T(8,128)(2,1)S(1)} %sum_over_y.1), channel_id=1, replica_groups={{0,4,8,12,16,20,24,28},{32,36,40,44,48,52,56,60},{64,68,72,76,80,84,88,..., dimensions={0} | all-to-all | bytes 655360 | tf_op jit(solution)/shard_map/all_to_all | solution.py:86
  86.3 3.4 %all-to-all-start.2 = ((bf16[8,80,256]{2,1,0:T(8,128)(2,1)}), bf16[8,80,256]{2,1,0:T(8,128)(2,1)S(1)}, u32[]{:S(2)}, u32[]{:S(2)}) async-start(bf16[8,80,256]{2,1,0:T(8,128)(2,1)} %sum_over_z.1), calls=%async_computation.2 | async-start | bytes 655360 | tf_op jit(solution)/shard_map/all_to_all | solution.py:86
  89.8 10.0 %all-to-all-done.2.pieces = bf16[8,80,256]{2,1,0:T(8,128)(2,1)S(1)} async-done(((bf16[8,80,256]{2,1,0:T(8,128)(2,1)}), bf16[8,80,256]{2,1,0:T(8,128)(2,1)S(1)}, u32[]{:S(2)}, u32[]{:S(2)}) %all-to-all-start.2) | async-done | bytes 327712 | tf_op jit(solution)/shard_map/all_to_all | solution.py:86
  102.9 4.5 %all-to-all-start.3 = ((bf16[4,512,256]{2,1,0:T(8,128)(2,1)}), bf16[4,512,256]{2,1,0:T(8,128)(2,1)}, u32[]{:S(2)}, u32[]{:S(2)}) async-start(bf16[4,512,256]{2,1,0:T(8,128)(2,1)} %get-tuple-element.47), calls=%async_computation.3 | async-start | bytes 2097152 | tf_op jit(solution)/shard_map/all_to_all | solution.py:86
  107.5 7.8 %inverse_factor.1 = f32[256,256]{1,0:T(8,128)S(1)} custom-call(f32[256,256]{1,0:T(8,128)S(1)} %bitcast.44), custom_call_target="tpu_custom_call" | custom-call | flops 8000000000 | bytes 1048576 | tf_op jit(solution)/shard_map/inverse_factor/pallas_call | solution.py:245
  115.3 3.5 %all-to-all-done.3 = bf16[4,512,256]{2,1,0:T(8,128)(2,1)} async-done(((bf16[4,512,256]{2,1,0:T(8,128)(2,1)}), bf16[4,512,256]{2,1,0:T(8,128)(2,1)}, u32[]{:S(2)}, u32[]{:S(2)}) %all-to-all-start.3) | async-done | bytes 1048608 | tf_op jit(solution)/shard_map/all_to_all | solution.py:86
  118.9 1.8 %multiply_reduce_fusion = (f32[256]{0:T(256)S(1)}, bf16[2048,256]{1,0:T(8,128)(2,1)S(1)}) fusion(bf16[2048,256]{1,0:T(8,128)(2,1)} %bitcast.14, f32[256,256]{1,0:T(8,128)S(1)} %inverse_factor.1), kind=kOutput, calls=%fused_computation.14 | convolution fusion | flops 270073600 | bytes 2360320 | tf_op jit(solution)/shard_map/dot_general | solution.py:360
  120.7 5.9 %collective-permute-start.19 = (bf16[2048,256]{1,0:T(8,128)(2,1)S(1)}, bf16[2048,256]{1,0:T(8,128)(2,1)S(1)}, u32[]{:S(2)}, u32[]{:S(2)}) collective-permute-start(bf16[2048,256]{1,0:T(8,128)(2,1)S(1)} %get-tuple-element.57), channel_id=1, source_target_pairs={{0,128},{128,0},{1,129},{129,1},{2,130},{130,2},{3,131},{131,3},{4... | collective-permute-start | bytes 3145736 | tf_op jit(solution)/shard_map/ppermute | solution.py:53
  132.1 1.9 %collective-permute-start.20 = (f32[1,256]{1,0:T(1,128)S(1)}, f32[1,256]{1,0:T(1,128)S(1)}, u32[]{:S(2)}, u32[]{:S(2)}) collective-permute-start(f32[1,256]{1,0:T(1,128)S(1)} %rsqrt_multiply_fusion), channel_id=1, source_target_pairs={{0,128},{128,0},{1,129},{129,1},{2,130},{130,2},{3,131},{131,3},{4... | collective-permute-start | bytes 3080 | tf_op jit(solution)/shard_map/ppermute | solution.py:53
  137.0 1.5 %convolution_convert_fusion.1 = bf16[256,2048]{1,0:T(8,128)(2,1)} fusion(bf16[2048,256]{1,0:T(8,128)(2,1)S(1)} %get-tuple-element.57, bf16[2048,256]{1,0:T(8,128)(2,1)S(1)} %collective-permute-done.19, pred[]{:T(512)S(6)} %eq.12, f32[256]{0:T(256)S(1)} %bitcast.49, f32[256,256]{1,0:T(8,128)S(1)} %fusion.14, f32[256,256]{1,0:T(8,128)S(1)} %collective-permute-done.15), kind=kOutput, calls=%fused_computation.7 | convolution fusion | flops 269680640 | bytes 3671041 | tf_op jit(solution)/shard_map/dot_general | solution.py:379
  (85 shorter events, 21.7 us)
Async XLA Ops:
  0.6 17.6 %copy-start.3 = (bf16[2048,256]{1,0:T(8,128)(2,1)S(1)}, bf16[2048,256]{1,0:T(8,128)(2,1)}, u32[]{:S(2)}) copy-start(bf16[2048,256]{1,0:T(8,128)(2,1)} %refs_15_.1) | copy-start | bytes 3145732
  0.6 23.5 %collective-permute-start.5 = (bf16[512,256]{1,0:T(8,128)(2,1)}, bf16[512,256]{1,0:T(8,128)(2,1)S(1)}, u32[]{:S(2)}, u32[]{:S(2)}) collective-permute-start(bf16[512,256]{1,0:T(8,128)(2,1)} %refs_2_.1), channel_id=1, source_target_pairs={{0,3},{1,0},{2,1},{3,2},{4,7},{5,4},{6,5},{7,6},{8,11},{9,8},{10,9... | collective-permute-start | bytes 786440 | tf_op jit(solution)/shard_map/ppermute | solution.py:42
  4.0 8.8 %collective-permute-start = (bf16[512,256]{1,0:T(8,128)(2,1)}, bf16[512,256]{1,0:T(8,128)(2,1)S(1)}, u32[]{:S(2)}, u32[]{:S(2)}) collective-permute-start(bf16[512,256]{1,0:T(8,128)(2,1)} %refs_2_.1), channel_id=1, source_target_pairs={{0,1},{1,2},{2,3},{3,0},{4,5},{5,6},{6,7},{7,4},{8,9},{9,10},{10,1... | collective-permute-start | bytes 786440 | tf_op jit(solution)/shard_map/ppermute | solution.py:42
  4.0 20.1 %collective-permute-start.4 = (bf16[512,256]{1,0:T(8,128)(2,1)}, bf16[512,256]{1,0:T(8,128)(2,1)S(1)}, u32[]{:S(2)}, u32[]{:S(2)}) collective-permute-start(bf16[512,256]{1,0:T(8,128)(2,1)} %refs_3_.1), channel_id=1, source_target_pairs={{0,1},{1,2},{2,3},{3,0},{4,5},{5,6},{6,7},{7,4},{8,9},{9,10},{10,1... | collective-permute-start | bytes 786440 | tf_op jit(solution)/shard_map/ppermute | solution.py:42
  4.2 10.7 %collective-permute-start.2 = (bf16[512,256]{1,0:T(8,128)(2,1)}, bf16[512,256]{1,0:T(8,128)(2,1)S(1)}, u32[]{:S(2)}, u32[]{:S(2)}) collective-permute-start(bf16[512,256]{1,0:T(8,128)(2,1)} %refs_3_.1), channel_id=1, source_target_pairs={{0,3},{1,0},{2,1},{3,2},{4,7},{5,4},{6,5},{7,6},{8,11},{9,8},{10,9... | collective-permute-start | bytes 786440 | tf_op jit(solution)/shard_map/ppermute | solution.py:42
  14.9 11.0 %collective-permute-start.1 = (bf16[512,256]{1,0:T(8,128)(2,1)S(1)}, bf16[512,256]{1,0:T(8,128)(2,1)S(1)}, u32[]{:S(2)}, u32[]{:S(2)}) collective-permute-start(bf16[512,256]{1,0:T(8,128)(2,1)S(1)} %collective-permute-done.refs_2_.refs_4_), channel_id=1, source_target_pairs={{0,1},{1,2},{2,3},{3,0},{4,5},{5,6},{6,7},{7,4},{8,9},{9,10},{10,1... | collective-permute-start | bytes 786440 | tf_op jit(solution)/shard_map/ppermute | solution.py:42
  15.8 10.2 %collective-permute-start.3 = (bf16[512,256]{1,0:T(8,128)(2,1)S(1)}, bf16[512,256]{1,0:T(8,128)(2,1)S(1)}, u32[]{:S(2)}, u32[]{:S(2)}) collective-permute-start(bf16[512,256]{1,0:T(8,128)(2,1)S(1)} %collective-permute-done.2.refs_5_.refs_7_), channel_id=1, source_target_pairs={{0,3},{1,0},{2,1},{3,2},{4,7},{5,4},{6,5},{7,6},{8,11},{9,8},{10,9... | collective-permute-start | bytes 786440 | tf_op jit(solution)/shard_map/ppermute | solution.py:42
  26.9 2.9 %collective-permute-start.6 = (bf16[256,256]{1,0:T(8,128)(2,1)S(1)}, bf16[256,256]{1,0:T(8,128)(2,1)S(1)}, u32[]{:S(2)}, u32[]{:S(2)}) collective-permute-start(bf16[256,256]{1,0:T(8,128)(2,1)S(1)} %get-tuple-element.34), channel_id=1, source_target_pairs={{0,128},{128,0},{1,129},{129,1},{2,130},{130,2},{3,131},{131,3},{4... | collective-permute-start | bytes 393224 | tf_op jit(solution)/shard_map/ppermute | solution.py:53
  29.8 7.4 %collective-permute-start.9 = (bf16[256,256]{1,0:T(8,128)(2,1)S(1)}, bf16[256,256]{1,0:T(8,128)(2,1)S(1)}, u32[]{:S(2)}, u32[]{:S(2)}) collective-permute-start(bf16[256,256]{1,0:T(8,128)(2,1)S(1)} %add_convert_fusion), channel_id=1, source_target_pairs={{0,3},{1,0},{2,1},{3,2},{4,7},{5,4},{6,5},{7,6},{8,11},{9,8},{10,9... | collective-permute-start | bytes 393224 | tf_op jit(solution)/shard_map/ppermute | solution.py:42
  31.6 6.0 %collective-permute-start.8 = (bf16[256,256]{1,0:T(8,128)(2,1)S(1)}, bf16[256,256]{1,0:T(8,128)(2,1)S(1)}, u32[]{:S(2)}, u32[]{:S(2)}) collective-permute-start(bf16[256,256]{1,0:T(8,128)(2,1)S(1)} %add_convert_fusion), channel_id=1, source_target_pairs={{0,2},{1,3},{2,0},{3,1},{4,6},{5,7},{6,4},{7,5},{8,10},{9,11},{10,... | collective-permute-start | bytes 393224 | tf_op jit(solution)/shard_map/ppermute | solution.py:42
  31.6 9.1 %collective-permute-start.7 = (bf16[256,256]{1,0:T(8,128)(2,1)S(1)}, bf16[256,256]{1,0:T(8,128)(2,1)S(1)}, u32[]{:S(2)}, u32[]{:S(2)}) collective-permute-start(bf16[256,256]{1,0:T(8,128)(2,1)S(1)} %add_convert_fusion), channel_id=1, source_target_pairs={{0,1},{1,2},{2,3},{3,0},{4,5},{5,6},{6,7},{7,4},{8,9},{9,10},{10,1... | collective-permute-start | bytes 393224 | tf_op jit(solution)/shard_map/ppermute | solution.py:42
  41.5 1.9 %collective-permute-start.10 = (bf16[256,256]{1,0:T(8,128)(2,1)S(1)}, bf16[256,256]{1,0:T(8,128)(2,1)S(1)}, u32[]{:S(2)}, u32[]{:S(2)}) collective-permute-start(bf16[256,256]{1,0:T(8,128)(2,1)S(1)} %fusion.15), channel_id=1, source_target_pairs={{0,128},{128,0},{1,129},{129,1},{2,130},{130,2},{3,131},{131,3},{4... | collective-permute-start | bytes 393224 | tf_op jit(solution)/shard_map/ppermute | solution.py:53
  44.3 2.7 %collective-permute-start.11 = (bf16[2048,256]{1,0:T(8,128)(2,1)S(1)}, bf16[2048,256]{1,0:T(8,128)(2,1)S(1)}, u32[]{:S(2)}, u32[]{:S(2)}) collective-permute-start(bf16[2048,256]{1,0:T(8,128)(2,1)S(1)} %get-tuple-element.58), channel_id=1, source_target_pairs={{0,128},{128,0},{1,129},{129,1},{2,130},{130,2},{3,131},{131,3},{4... | collective-permute-start | bytes 3145736 | tf_op jit(solution)/shard_map/ppermute | solution.py:53
  86.3 13.5 %all-to-all-start.2 = ((bf16[8,80,256]{2,1,0:T(8,128)(2,1)}), bf16[8,80,256]{2,1,0:T(8,128)(2,1)S(1)}, u32[]{:S(2)}, u32[]{:S(2)}) async-start(bf16[8,80,256]{2,1,0:T(8,128)(2,1)} %sum_over_z.1), calls=%async_computation.2 | async-start | bytes 655360 | tf_op jit(solution)/shard_map/all_to_all | solution.py:86
  100.8 6.7 %collective-permute-start.14 = (f32[64,256]{1,0:T(8,128)S(1)}, f32[64,256]{1,0:T(8,128)S(1)}, u32[]{:S(2)}, u32[]{:S(2)}) collective-permute-start(f32[64,256]{1,0:T(8,128)S(1)} %get-tuple-element.46), channel_id=1, source_target_pairs={{0,96},{4,100},{8,104},{12,108},{16,112},{20,116},{24,120},{28,124... | collective-permute-start | bytes 196616 | tf_op jit(solution)/shard_map/ppermute | solution.py:49
  101.7 5.8 %collective-permute-start.13 = (f32[64,256]{1,0:T(8,128)S(1)}, f32[64,256]{1,0:T(8,128)S(1)}, u32[]{:S(2)}, u32[]{:S(2)}) collective-permute-start(f32[64,256]{1,0:T(8,128)S(1)} %get-tuple-element.46), channel_id=1, source_target_pairs={{0,64},{4,68},{8,72},{12,76},{16,80},{20,84},{24,88},{28,92},{32,9... | collective-permute-start | bytes 196616 | tf_op jit(solution)/shard_map/ppermute | solution.py:49
  102.9 4.5 %collective-permute-start.12 = (f32[64,256]{1,0:T(8,128)S(1)}, f32[64,256]{1,0:T(8,128)S(1)}, u32[]{:S(2)}, u32[]{:S(2)}) collective-permute-start(f32[64,256]{1,0:T(8,128)S(1)} %get-tuple-element.46), channel_id=1, source_target_pairs={{0,32},{4,36},{8,40},{12,44},{16,48},{20,52},{24,56},{28,60},{32,6... | collective-permute-start | bytes 196616 | tf_op jit(solution)/shard_map/ppermute | solution.py:49
  102.9 16.0 %all-to-all-start.3 = ((bf16[4,512,256]{2,1,0:T(8,128)(2,1)}), bf16[4,512,256]{2,1,0:T(8,128)(2,1)}, u32[]{:S(2)}, u32[]{:S(2)}) async-start(bf16[4,512,256]{2,1,0:T(8,128)(2,1)} %get-tuple-element.47), calls=%async_computation.3 | async-start | bytes 2097152 | tf_op jit(solution)/shard_map/all_to_all | solution.py:86
  120.7 8.6 %collective-permute-start.19 = (bf16[2048,256]{1,0:T(8,128)(2,1)S(1)}, bf16[2048,256]{1,0:T(8,128)(2,1)S(1)}, u32[]{:S(2)}, u32[]{:S(2)}) collective-permute-start(bf16[2048,256]{1,0:T(8,128)(2,1)S(1)} %get-tuple-element.57), channel_id=1, source_target_pairs={{0,128},{128,0},{1,129},{129,1},{2,130},{130,2},{3,131},{131,3},{4... | collective-permute-start | bytes 3145736 | tf_op jit(solution)/shard_map/ppermute | solution.py:53
  127.1 2.2 %collective-permute-start.15 = (f32[256,256]{1,0:T(8,128)S(1)}, f32[256,256]{1,0:T(8,128)S(1)}, u32[]{:S(2)}, u32[]{:S(2)}) collective-permute-start(f32[256,256]{1,0:T(8,128)S(1)} %fusion.14), channel_id=1, source_target_pairs={{0,128},{128,0},{1,129},{129,1},{2,130},{130,2},{3,131},{131,3},{4... | collective-permute-start | bytes 786440 | tf_op jit(solution)/shard_map/ppermute | solution.py:53
  127.2 3.6 %collective-permute-start.18 = (f32[1,256]{1,0:T(1,128)S(1)}, f32[1,256]{1,0:T(1,128)S(1)}, u32[]{:S(2)}, u32[]{:S(2)}) collective-permute-start(f32[1,256]{1,0:T(1,128)S(1)} %bitcast.51), channel_id=1, source_target_pairs={{0,3},{1,0},{2,1},{3,2},{4,7},{5,4},{6,5},{7,6},{8,11},{9,8},{10,9... | collective-permute-start | bytes 3080 | tf_op jit(solution)/shard_map/ppermute | solution.py:42
  127.9 3.9 %collective-permute-start.17 = (f32[1,256]{1,0:T(1,128)S(1)}, f32[1,256]{1,0:T(1,128)S(1)}, u32[]{:S(2)}, u32[]{:S(2)}) collective-permute-start(f32[1,256]{1,0:T(1,128)S(1)} %bitcast.52), channel_id=1, source_target_pairs={{0,2},{1,3},{2,0},{3,1},{4,6},{5,7},{6,4},{7,5},{8,10},{9,11},{10,... | collective-permute-start | bytes 3080 | tf_op jit(solution)/shard_map/ppermute | solution.py:42
  127.9 4.2 %collective-permute-start.16 = (f32[1,256]{1,0:T(1,128)S(1)}, f32[1,256]{1,0:T(1,128)S(1)}, u32[]{:S(2)}, u32[]{:S(2)}) collective-permute-start(f32[1,256]{1,0:T(1,128)S(1)} %bitcast.53), channel_id=1, source_target_pairs={{0,1},{1,2},{2,3},{3,0},{4,5},{5,6},{6,7},{7,4},{8,9},{9,10},{10,1... | collective-permute-start | bytes 3080 | tf_op jit(solution)/shard_map/ppermute | solution.py:42
  132.1 3.4 %collective-permute-start.20 = (f32[1,256]{1,0:T(1,128)S(1)}, f32[1,256]{1,0:T(1,128)S(1)}, u32[]{:S(2)}, u32[]{:S(2)}) collective-permute-start(f32[1,256]{1,0:T(1,128)S(1)} %rsqrt_multiply_fusion), channel_id=1, source_target_pairs={{0,128},{128,0},{1,129},{129,1},{2,130},{130,2},{3,131},{131,3},{4... | collective-permute-start | bytes 3080 | tf_op jit(solution)/shard_map/ppermute | solution.py:53
  (13 other events, 111.8 us)

commit v5 on v4

--- a/solution.py
+++ b/solution.py
@@ -148,12 +148,10 @@
     return (a, a.shape, lambda s, i: (0,) * len(a.shape))
 
 
-def pack_kernel(mine, other, gram, out):
-    many, few = mine.shape[0] // N_Y, gram.shape[0] // N_Y
+def pack_kernel(term, gram, out):
+    many, few = term.shape[0] // N_Y, gram.shape[0] // N_Y
     for j in range(N_Y):
-        rows = slice(j * many, (j + 1) * many)
-        term = mine[rows].astype(jnp.float32) + other[rows].astype(jnp.float32)
-        out[j, :many] = term.astype(jnp.bfloat16)
+        out[j, :many] = term[j * many : (j + 1) * many]
         out[j, many:] = gram[j * few : (j + 1) * few]
 
 
@@ -322,21 +320,19 @@
         ).astype(jnp.bfloat16)
         for w in range(2)
     ]
-    parts, buffers = lax.optimization_barrier((from_all(mine, shift_tp), buffers))
+    taken, given = split(buffers)
+    parts, taken, given = lax.optimization_barrier((from_all(mine, shift_tp), taken, given))
+    given = swap_cores(given)
     power = total(parts)
     power_b = power.astype(jnp.bfloat16)
-    powers_b = split([power_b, swap_cores(power_b)])
-    mine, other = split(
-        [contract_rows(buffers[w], powers_b[w]).astype(jnp.bfloat16) for w in range(2)]
-    )
-    other = swap_cores(other)
-
-    width = mine.shape[1]
-    many, few = mine.shape[0] // N_Y, RANK // N_Y
+    term = (contract_rows(taken, power_b) + contract_rows(given, power_b)).astype(jnp.bfloat16)
+
+    width = term.shape[1]
+    many, few = term.shape[0] // N_Y, RANK // N_Y
     gram = contract_rows(power, power, lax.Precision.HIGHEST).astype(jnp.bfloat16)
     half = lambda *dims: shape(jnp.bfloat16, *dims)
     packed = local_kernel(
-        pack_kernel, [mine, other, gram], half(N_Y, many + few, width), "pack_quarters"
+        pack_kernel, [term, gram], half(N_Y, many + few, width), "pack_quarters"
     )
     packed = exchange(packed, Y_GROUPS)
     sent = half(N_Z, (many + 2 * few) // N_Z, width)

time: 139 us -> 146 us (1.050)
  waiting for transfers between devices: 23.9 us -> 18.3 us
  matrix products: 26.4 us -> 30.2 us
  starting transfers between devices: 34.8 us -> 38.4 us
  local copies, waits for them, and re-layouts: 0.87 us -> 3.76 us
  Pallas kernels: 13.3 us -> 15.8 us
    dot_general x5, matrix products: 6.28 us -> 10.1 us  [contract_rows(): lax.dot_general(left, right, (((0,), (0,)), ((), ())), precision=precisio...]
    unnamed x28 -> x34, local copies, waits for them, and re-layouts: 0.72 us -> 3.61 us
    ppermute x12, starting transfers between devices: 13.6 us -> 16.3 us  [shift_tp(): return lax.ppermute(x, 'tp', [(i, (i + by) % N_TP) for i in range(N_TP)])]
    pallas_call x3, Pallas kernels: 3.29 us -> 5.96 us  [indexed_kernel(): pl.pallas_call(body, grid_spec=pltpu.PrefetchScalarGridSpec(num_scalar_pr...]
    all_to_all x2, waiting for transfers between devices: 13.5 us -> 11.5 us  [exchange(): return lax.all_to_all(x, 'fsdp', 0, 0, axis_index_groups=groups)]
    ppermute x6 -> x5, waiting for transfers between devices: 3.55 us -> 1.63 us  [swap_cores(): return lax.ppermute(x, 'rep', [(0, 1), (1, 0)])]
    ppermute x12, waiting for transfers between devices: 6.86 us -> 5.17 us  [shift_tp(): return lax.ppermute(x, 'tp', [(i, (i + by) % N_TP) for i in range(N_TP)])]
    ppermute x6 -> x5, starting transfers between devices: 11.2 us -> 11.3 us  [swap_cores(): return lax.ppermute(x, 'rep', [(0, 1), (1, 0)])]
  transfers between devices with their start and end apart: 23 -> 22, of which waited for: 11 -> 4; matrix products, arithmetic and copies ran while one was open for 15% -> 17% of each run, Pallas kernels for 7% -> 9%
where the time goes in v5:
time: 146 us
  starting transfers between devices  38.4 us (26%)
  blocking collectives  37.9 us (26%)
  matrix products  30.2 us (21%)
  waiting for transfers between devices  18.3 us (13%)
  Pallas kernels  15.8 us (11%)
  local copies, waits for them, and re-layouts  3.76 us (3%)
    all_to_all x2, blocking collectives, exchange(): return lax.all_to_all(x, 'fsdp', 0, 0, axis_index_groups=groups)  37.9 us
    ppermute x12, starting transfers between devices, shift_tp(): return lax.ppermute(x, 'tp', [(i, (i + by) % N_TP) for i in range(N_TP)])  16.3 us
    dot_general x2, matrix products, per_device(): product = jnp.dot(grad, bases[w], preferred_element_type=jnp.float32)  11.9 us
    all_to_all x2, waiting for transfers between devices, exchange(): return lax.all_to_all(x, 'fsdp', 0, 0, axis_index_groups=groups)  11.5 us
    ppermute x5, starting transfers between devices, swap_cores(): return lax.ppermute(x, 'rep', [(0, 1), (1, 0)])  11.3 us
    dot_general x5, matrix products, contract_rows(): lax.dot_general(left, right, (((0,), (0,)), ((), ())), precision=precisio...  10.1 us
    all_to_all x2, starting transfers between devices, exchange(): return lax.all_to_all(x, 'fsdp', 0, 0, axis_index_groups=groups)  7.91 us
    pallas_call x1, Pallas kernels, inverse_factor(): pl.pallas_call(inverse_kernel, out_shape=jax.ShapeDtypeStruct((RANK, RANK...  7.84 us
  transfers between devices with their start and end apart: 22, of which 4 were waited for; matrix products, arithmetic and copies ran while one was open for 17% of the time, Pallas kernels for 9%

profile of v5, /device:TPU:1, one launch (start us, length us, event | category | flops | bytes accessed | tf_op | source)
XLA Modules:
  0.0 145.9 jit_solution(16672799475228086513)
XLA Ops:
  0.6 3.4 %collective-permute-start.2 = (bf16[512,256]{1,0:T(8,128)(2,1)}, bf16[512,256]{1,0:T(8,128)(2,1)}, u32[]{:S(2)}, u32[]{:S(2)}) collective-permute-start(bf16[512,256]{1,0:T(8,128)(2,1)} %refs_3_.1), channel_id=1, source_target_pairs={{0,3},{1,0},{2,1},{3,2},{4,7},{5,4},{6,5},{7,6},{8,11},{9,8},{10,9... | collective-permute-start | bytes 786440 | tf_op jit(solution)/shard_map/ppermute | solution.py:42
  4.2 2.5 %collective-permute-start.5 = (bf16[512,256]{1,0:T(8,128)(2,1)}, bf16[512,256]{1,0:T(8,128)(2,1)}, u32[]{:S(2)}, u32[]{:S(2)}) collective-permute-start(bf16[512,256]{1,0:T(8,128)(2,1)} %refs_2_.1), channel_id=1, source_target_pairs={{0,3},{1,0},{2,1},{3,2},{4,7},{5,4},{6,5},{7,6},{8,11},{9,8},{10,9... | collective-permute-start | bytes 786440 | tf_op jit(solution)/shard_map/ppermute | solution.py:42
  6.7 6.0 %convolution_convert_fusion.3.refs_6_.refs_8_.refs_10_.refs_2_ = bf16[2048,256]{1,0:T(8,128)(2,1)S(1)} fusion(bf16[2048,2048]{1,0:T(8,128)(2,1)} %param.9, bf16[2048,256]{1,0:T(8,128)(2,1)} %refs_14_.1), kind=kOutput, calls=%fused_computation.15 | convolution fusion | flops 2148007936 | bytes 10485760 | tf_op jit(solution)/shard_map/dot_general | solution.py:288
  12.9 5.1 %collective-permute-done.refs_2_.refs_4_ = bf16[512,256]{1,0:T(8,128)(2,1)} collective-permute-done((bf16[512,256]{1,0:T(8,128)(2,1)}, bf16[512,256]{1,0:T(8,128)(2,1)}, u32[]{:S(2)}, u32[]{:S(2)}) %collective-permute-start) | collective-permute-done | bytes 262176 | tf_op jit(solution)/shard_map/ppermute | solution.py:42
  18.0 2.7 %collective-permute-start.3 = (bf16[512,256]{1,0:T(8,128)(2,1)}, bf16[512,256]{1,0:T(8,128)(2,1)S(1)}, u32[]{:S(2)}, u32[]{:S(2)}) collective-permute-start(bf16[512,256]{1,0:T(8,128)(2,1)} %collective-permute-done.2.refs_5_.refs_7_), channel_id=1, source_target_pairs={{0,3},{1,0},{2,1},{3,2},{4,7},{5,4},{6,5},{7,6},{8,11},{9,8},{10,9... | collective-permute-start | bytes 786440 | tf_op jit(solution)/shard_map/ppermute | solution.py:42
  20.7 6.0 %convolution_convert_fusion.2.refs_7_.refs_9_.refs_11_.refs_3_ = bf16[2048,256]{1,0:T(8,128)(2,1)S(1)} fusion(bf16[2048,2048]{1,0:T(8,128)(2,1)} %param.11, bf16[2048,256]{1,0:T(8,128)(2,1)} %refs_15_.1), kind=kOutput, calls=%fused_computation.14 | convolution fusion | flops 2148007936 | bytes 10485760 | tf_op jit(solution)/shard_map/dot_general | solution.py:288
  26.7 2.9 %near_tokens.1 = (f32[256,256]{1,0:T(8,128)S(1)}, f32[256,256]{1,0:T(8,128)S(1)}) custom-call(s32[5]{0:T(128)S(1)} %stack.23.index, bf16[512,256]{1,0:T(8,128)(2,1)S(1)} %copy-done.4, bf16[512,256]{1,0:T(8,128)(2,1)S(1)} %copy-done.5, bf16[512,256]{1,0:T(8,128)(2,1)} %collective-permute-done.refs_2_.refs_4_, ...), custom_call_target="tpu_custom_call" | custom-call | flops 1048576 | bytes 1048576 | tf_op jit(solution)/shard_map/near_tokens/pallas_call | solution.py:130
  31.3 2.4 %collective-permute-start.6 = (bf16[256,256]{1,0:T(8,128)(2,1)S(1)}, bf16[256,256]{1,0:T(8,128)(2,1)S(1)}, u32[]{:S(2)}, u32[]{:S(2)}) collective-permute-start(bf16[256,256]{1,0:T(8,128)(2,1)S(1)} %get-tuple-element.34), channel_id=1, source_target_pairs={{0,128},{128,0},{1,129},{129,1},{2,130},{130,2},{3,131},{131,3},{4... | collective-permute-start | bytes 393224 | tf_op jit(solution)/shard_map/ppermute | solution.py:53
  36.6 2.1 %order_tokens.1 = (bf16[4,512,256]{2,1,0:T(8,128)(2,1)S(1)}, bf16[4,512,256]{2,1,0:T(8,128)(2,1)S(1)}) custom-call(s32[5]{0:T(128)S(1)} %stack.23.index, bf16[512,256]{1,0:T(8,128)(2,1)S(1)} %copy-done.8, bf16[512,256]{1,0:T(8,128)(2,1)S(1)} %copy-done.10, bf16[512,256]{1,0:T(8,128)(2,1)S(1)} %copy-done.4, bf16[512,256]{1,0:T(8,128)(2,1)S(1)} %copy-done.6, ...), custom_call_target="tpu_custom_call" | custom-call | flops 1048576 | bytes 1048576 | tf_op jit(solution)/shard_map/order_tokens/pallas_call | solution.py:130
  39.8 1.8 %collective-permute-start.9 = (bf16[256,256]{1,0:T(8,128)(2,1)S(1)}, bf16[256,256]{1,0:T(8,128)(2,1)S(1)}, u32[]{:S(2)}, u32[]{:S(2)}) collective-permute-start(bf16[256,256]{1,0:T(8,128)(2,1)S(1)} %add_convert_fusion), channel_id=1, source_target_pairs={{0,3},{1,0},{2,1},{3,2},{4,7},{5,4},{6,5},{7,6},{8,11},{9,8},{10,9... | collective-permute-start | bytes 393224 | tf_op jit(solution)/shard_map/ppermute | solution.py:42
  41.6 5.9 %fusion.2 = bf16[256,2048]{1,0:T(8,128)(2,1)S(1)} fusion(bf16[2048,256]{1,0:T(8,128)(2,1)S(1)} %bitcast.45, bf16[2048,2048]{1,0:T(8,128)(2,1)} %param.9, bf16[1,256,2048]{2,1,0:T(8,128)(2,1)S(1)} %copy-done), kind=kOutput, calls=%fused_computation.7 | convolution fusion | flops 2149056512 | bytes 11534336 | tf_op jit(solution)/shard_map/dot_general | solution.py:27
  47.5 2.6 %broadcast_select_fusion.2 = (bf16[256,2048]{1,0:T(8,128)(2,1)S(1)}, bf16[256,2048]{1,0:T(8,128)(2,1)S(1)}, bf16[256,2048]{1,0:T(8,128)(2,1)S(1)}) fusion(bf16[256,2048]{1,0:T(8,128)(2,1)S(1)} %fusion.2, pred[]{:T(512)S(6)} %eq.12, bf16[2048,256]{1,0:T(8,128)(2,1)S(1)} %bitcast.46, bf16[2048,2048]{1,0:T(8,128)(2,1)S(1)} %bitcast.49, ...), kind=kOutput, calls=%fused_computation.22 | convolution fusion | flops 2150105088 | bytes 14680065 | tf_op jit(solution)/shard_map/dot_general | solution.py:27
  51.5 1.6 %collective-permute-done.10 = bf16[256,2048]{1,0:T(8,128)(2,1)S(1)} collective-permute-done((bf16[256,2048]{1,0:T(8,128)(2,1)S(1)}, bf16[256,2048]{1,0:T(8,128)(2,1)S(1)}, u32[]{:S(2)}, u32[]{:S(2)}) %collective-permute-start.10) | collective-permute-done | bytes 1048608 | tf_op jit(solution)/shard_map/ppermute | solution.py:53
  54.2 19.6 %all_to_all.20.pieces = bf16[4,576,256]{2,1,0:T(8,128)(2,1)S(1)} all-to-all(bf16[4,576,256]{2,1,0:T(8,128)(2,1)S(1)} %pack_quarters.1), channel_id=1, replica_groups={{0,32,64,96},{4,36,68,100},{8,40,72,104},{12,44,76,108},{16,48,80,112},..., dimensions={0} | all-to-all | bytes 2359296 | tf_op jit(solution)/shard_map/all_to_all | solution.py:86
  74.0 18.3 %all_to_all.21.pieces = bf16[8,80,256]{2,1,0:T(8,128)(2,1)S(1)} all-to-all(bf16[8,80,256]{2,1,0:T(8,128)(2,1)S(1)} %sum_over_y.1), channel_id=1, replica_groups={{0,4,8,12,16,20,24,28},{32,36,40,44,48,52,56,60},{64,68,72,76,80,84,88,..., dimensions={0} | all-to-all | bytes 655360 | tf_op jit(solution)/shard_map/all_to_all | solution.py:86
  93.1 3.4 %all-to-all-start.2 = ((bf16[8,80,256]{2,1,0:T(8,128)(2,1)}), bf16[8,80,256]{2,1,0:T(8,128)(2,1)S(1)}, u32[]{:S(2)}, u32[]{:S(2)}) async-start(bf16[8,80,256]{2,1,0:T(8,128)(2,1)} %sum_over_z.1), calls=%async_computation.2 | async-start | bytes 655360 | tf_op jit(solution)/shard_map/all_to_all | solution.py:86
  96.6 10.0 %all-to-all-done.2.pieces = bf16[8,80,256]{2,1,0:T(8,128)(2,1)S(1)} async-done(((bf16[8,80,256]{2,1,0:T(8,128)(2,1)}), bf16[8,80,256]{2,1,0:T(8,128)(2,1)S(1)}, u32[]{:S(2)}, u32[]{:S(2)}) %all-to-all-start.2) | async-done | bytes 327712 | tf_op jit(solution)/shard_map/all_to_all | solution.py:86
  107.9 1.8 %collective-permute-start.12 = (f32[64,256]{1,0:T(8,128)S(1)}, f32[64,256]{1,0:T(8,128)S(1)}, u32[]{:S(2)}, u32[]{:S(2)}) collective-permute-start(f32[64,256]{1,0:T(8,128)S(1)} %get-tuple-element.46), channel_id=1, source_target_pairs={{0,64},{4,68},{8,72},{12,76},{16,80},{20,84},{24,88},{28,92},{32,9... | collective-permute-start | bytes 196616 | tf_op jit(solution)/shard_map/ppermute | solution.py:49
  110.6 4.5 %all-to-all-start.3 = ((bf16[4,512,256]{2,1,0:T(8,128)(2,1)}), bf16[4,512,256]{2,1,0:T(8,128)(2,1)}, u32[]{:S(2)}, u32[]{:S(2)}) async-start(bf16[4,512,256]{2,1,0:T(8,128)(2,1)} %get-tuple-element.47), calls=%async_computation.3 | async-start | bytes 2097152 | tf_op jit(solution)/shard_map/all_to_all | solution.py:86
  115.2 7.8 %inverse_factor.1 = f32[256,256]{1,0:T(8,128)S(1)} custom-call(f32[256,256]{1,0:T(8,128)S(1)} %bitcast.47), custom_call_target="tpu_custom_call" | custom-call | flops 8000000000 | bytes 1048576 | tf_op jit(solution)/shard_map/inverse_factor/pallas_call | solution.py:243
  124.6 1.8 %multiply_reduce_fusion = (f32[256]{0:T(256)S(1)}, bf16[2048,256]{1,0:T(8,128)(2,1)S(1)}) fusion(bf16[2048,256]{1,0:T(8,128)(2,1)} %bitcast.14, f32[256,256]{1,0:T(8,128)S(1)} %inverse_factor.1), kind=kOutput, calls=%fused_computation.18 | convolution fusion | flops 270073600 | bytes 2360320 | tf_op jit(solution)/shard_map/dot_general | solution.py:356
  126.5 6.8 %collective-permute-start.18 = (bf16[2048,256]{1,0:T(8,128)(2,1)S(1)}, bf16[2048,256]{1,0:T(8,128)(2,1)S(1)}, u32[]{:S(2)}, u32[]{:S(2)}) collective-permute-start(bf16[2048,256]{1,0:T(8,128)(2,1)S(1)} %get-tuple-element.57), channel_id=1, source_target_pairs={{0,128},{128,0},{1,129},{129,1},{2,130},{130,2},{3,131},{131,3},{4... | collective-permute-start | bytes 3145736 | tf_op jit(solution)/shard_map/ppermute | solution.py:53
  134.4 2.1 %collective-permute-start.16 = (f32[1,256]{1,0:T(1,128)S(1)}, f32[1,256]{1,0:T(1,128)S(1)}, u32[]{:S(2)}, u32[]{:S(2)}) collective-permute-start(f32[1,256]{1,0:T(1,128)S(1)} %bitcast.53), channel_id=1, source_target_pairs={{0,2},{1,3},{2,0},{3,1},{4,6},{5,7},{6,4},{7,5},{8,10},{9,11},{10,... | collective-permute-start | bytes 3080 | tf_op jit(solution)/shard_map/ppermute | solution.py:42
  136.6 2.0 %collective-permute-start.17 = (f32[1,256]{1,0:T(1,128)S(1)}, f32[1,256]{1,0:T(1,128)S(1)}, u32[]{:S(2)}, u32[]{:S(2)}) collective-permute-start(f32[1,256]{1,0:T(1,128)S(1)} %bitcast.54), channel_id=1, source_target_pairs={{0,3},{1,0},{2,1},{3,2},{4,7},{5,4},{6,5},{7,6},{8,11},{9,8},{10,9... | collective-permute-start | bytes 3080 | tf_op jit(solution)/shard_map/ppermute | solution.py:42
  (88 shorter events, 21.5 us)
Async XLA Ops:
  0.6 17.4 %collective-permute-start.2 = (bf16[512,256]{1,0:T(8,128)(2,1)}, bf16[512,256]{1,0:T(8,128)(2,1)}, u32[]{:S(2)}, u32[]{:S(2)}) collective-permute-start(bf16[512,256]{1,0:T(8,128)(2,1)} %refs_3_.1), channel_id=1, source_target_pairs={{0,3},{1,0},{2,1},{3,2},{4,7},{5,4},{6,5},{7,6},{8,11},{9,8},{10,9... | collective-permute-start | bytes 786440 | tf_op jit(solution)/shard_map/ppermute | solution.py:42
  4.0 22.6 %collective-permute-start.4 = (bf16[512,256]{1,0:T(8,128)(2,1)}, bf16[512,256]{1,0:T(8,128)(2,1)}, u32[]{:S(2)}, u32[]{:S(2)}) collective-permute-start(bf16[512,256]{1,0:T(8,128)(2,1)} %refs_3_.1), channel_id=1, source_target_pairs={{0,1},{1,2},{2,3},{3,0},{4,5},{5,6},{6,7},{7,4},{8,9},{9,10},{10,1... | collective-permute-start | bytes 786440 | tf_op jit(solution)/shard_map/ppermute | solution.py:42
  4.0 14.0 %collective-permute-start = (bf16[512,256]{1,0:T(8,128)(2,1)}, bf16[512,256]{1,0:T(8,128)(2,1)}, u32[]{:S(2)}, u32[]{:S(2)}) collective-permute-start(bf16[512,256]{1,0:T(8,128)(2,1)} %refs_2_.1), channel_id=1, source_target_pairs={{0,1},{1,2},{2,3},{3,0},{4,5},{5,6},{6,7},{7,4},{8,9},{9,10},{10,1... | collective-permute-start | bytes 786440 | tf_op jit(solution)/shard_map/ppermute | solution.py:42
  4.2 22.5 %collective-permute-start.5 = (bf16[512,256]{1,0:T(8,128)(2,1)}, bf16[512,256]{1,0:T(8,128)(2,1)}, u32[]{:S(2)}, u32[]{:S(2)}) collective-permute-start(bf16[512,256]{1,0:T(8,128)(2,1)} %refs_2_.1), channel_id=1, source_target_pairs={{0,3},{1,0},{2,1},{3,2},{4,7},{5,4},{6,5},{7,6},{8,11},{9,8},{10,9... | collective-permute-start | bytes 786440 | tf_op jit(solution)/shard_map/ppermute | solution.py:42
  12.8 13.9 %copy-start.3 = (bf16[2048,256]{1,0:T(8,128)(2,1)S(1)}, bf16[2048,256]{1,0:T(8,128)(2,1)}, u32[]{:S(2)}) copy-start(bf16[2048,256]{1,0:T(8,128)(2,1)} %refs_15_.1) | copy-start | bytes 3145732
  18.0 11.7 %collective-permute-start.1 = (bf16[512,256]{1,0:T(8,128)(2,1)}, bf16[512,256]{1,0:T(8,128)(2,1)S(1)}, u32[]{:S(2)}, u32[]{:S(2)}) collective-permute-start(bf16[512,256]{1,0:T(8,128)(2,1)} %collective-permute-done.refs_2_.refs_4_), channel_id=1, source_target_pairs={{0,1},{1,2},{2,3},{3,0},{4,5},{5,6},{6,7},{7,4},{8,9},{9,10},{10,1... | collective-permute-start | bytes 786440 | tf_op jit(solution)/shard_map/ppermute | solution.py:42
  18.0 11.7 %collective-permute-start.3 = (bf16[512,256]{1,0:T(8,128)(2,1)}, bf16[512,256]{1,0:T(8,128)(2,1)S(1)}, u32[]{:S(2)}, u32[]{:S(2)}) collective-permute-start(bf16[512,256]{1,0:T(8,128)(2,1)} %collective-permute-done.2.refs_5_.refs_7_), channel_id=1, source_target_pairs={{0,3},{1,0},{2,1},{3,2},{4,7},{5,4},{6,5},{7,6},{8,11},{9,8},{10,9... | collective-permute-start | bytes 786440 | tf_op jit(solution)/shard_map/ppermute | solution.py:42
  31.3 7.4 %collective-permute-start.6 = (bf16[256,256]{1,0:T(8,128)(2,1)S(1)}, bf16[256,256]{1,0:T(8,128)(2,1)S(1)}, u32[]{:S(2)}, u32[]{:S(2)}) collective-permute-start(bf16[256,256]{1,0:T(8,128)(2,1)S(1)} %get-tuple-element.34), channel_id=1, source_target_pairs={{0,128},{128,0},{1,129},{129,1},{2,130},{130,2},{3,131},{131,3},{4... | collective-permute-start | bytes 393224 | tf_op jit(solution)/shard_map/ppermute | solution.py:53
  38.8 11.3 %collective-permute-start.7 = (bf16[256,256]{1,0:T(8,128)(2,1)S(1)}, bf16[256,256]{1,0:T(8,128)(2,1)S(1)}, u32[]{:S(2)}, u32[]{:S(2)}) collective-permute-start(bf16[256,256]{1,0:T(8,128)(2,1)S(1)} %add_convert_fusion), channel_id=1, source_target_pairs={{0,1},{1,2},{2,3},{3,0},{4,5},{5,6},{6,7},{7,4},{8,9},{9,10},{10,1... | collective-permute-start | bytes 393224 | tf_op jit(solution)/shard_map/ppermute | solution.py:42
  38.9 11.2 %collective-permute-start.8 = (bf16[256,256]{1,0:T(8,128)(2,1)S(1)}, bf16[256,256]{1,0:T(8,128)(2,1)S(1)}, u32[]{:S(2)}, u32[]{:S(2)}) collective-permute-start(bf16[256,256]{1,0:T(8,128)(2,1)S(1)} %add_convert_fusion), channel_id=1, source_target_pairs={{0,2},{1,3},{2,0},{3,1},{4,6},{5,7},{6,4},{7,5},{8,10},{9,11},{10,... | collective-permute-start | bytes 393224 | tf_op jit(solution)/shard_map/ppermute | solution.py:42
  39.8 10.4 %collective-permute-start.9 = (bf16[256,256]{1,0:T(8,128)(2,1)S(1)}, bf16[256,256]{1,0:T(8,128)(2,1)S(1)}, u32[]{:S(2)}, u32[]{:S(2)}) collective-permute-start(bf16[256,256]{1,0:T(8,128)(2,1)S(1)} %add_convert_fusion), channel_id=1, source_target_pairs={{0,3},{1,0},{2,1},{3,2},{4,7},{5,4},{6,5},{7,6},{8,11},{9,8},{10,9... | collective-permute-start | bytes 393224 | tf_op jit(solution)/shard_map/ppermute | solution.py:42
  50.2 2.9 %collective-permute-start.10 = (bf16[256,2048]{1,0:T(8,128)(2,1)S(1)}, bf16[256,2048]{1,0:T(8,128)(2,1)S(1)}, u32[]{:S(2)}, u32[]{:S(2)}) collective-permute-start(bf16[256,2048]{1,0:T(8,128)(2,1)S(1)} %get-tuple-element.45), channel_id=1, source_target_pairs={{0,128},{128,0},{1,129},{129,1},{2,130},{130,2},{3,131},{131,3},{4... | collective-permute-start | bytes 3145736 | tf_op jit(solution)/shard_map/ppermute | solution.py:53
  93.1 13.5 %all-to-all-start.2 = ((bf16[8,80,256]{2,1,0:T(8,128)(2,1)}), bf16[8,80,256]{2,1,0:T(8,128)(2,1)S(1)}, u32[]{:S(2)}, u32[]{:S(2)}) async-start(bf16[8,80,256]{2,1,0:T(8,128)(2,1)} %sum_over_z.1), calls=%async_computation.2 | async-start | bytes 655360 | tf_op jit(solution)/shard_map/all_to_all | solution.py:86
  107.6 7.5 %collective-permute-start.11 = (f32[64,256]{1,0:T(8,128)S(1)}, f32[64,256]{1,0:T(8,128)S(1)}, u32[]{:S(2)}, u32[]{:S(2)}) collective-permute-start(f32[64,256]{1,0:T(8,128)S(1)} %get-tuple-element.46), channel_id=1, source_target_pairs={{0,32},{4,36},{8,40},{12,44},{16,48},{20,52},{24,56},{28,60},{32,6... | collective-permute-start | bytes 196616 | tf_op jit(solution)/shard_map/ppermute | solution.py:49
  107.9 7.2 %collective-permute-start.12 = (f32[64,256]{1,0:T(8,128)S(1)}, f32[64,256]{1,0:T(8,128)S(1)}, u32[]{:S(2)}, u32[]{:S(2)}) collective-permute-start(f32[64,256]{1,0:T(8,128)S(1)} %get-tuple-element.46), channel_id=1, source_target_pairs={{0,64},{4,68},{8,72},{12,76},{16,80},{20,84},{24,88},{28,92},{32,9... | collective-permute-start | bytes 196616 | tf_op jit(solution)/shard_map/ppermute | solution.py:49
  109.7 5.5 %collective-permute-start.13 = (f32[64,256]{1,0:T(8,128)S(1)}, f32[64,256]{1,0:T(8,128)S(1)}, u32[]{:S(2)}, u32[]{:S(2)}) collective-permute-start(f32[64,256]{1,0:T(8,128)S(1)} %get-tuple-element.46), channel_id=1, source_target_pairs={{0,96},{4,100},{8,104},{12,108},{16,112},{20,116},{24,120},{28,124... | collective-permute-start | bytes 196616 | tf_op jit(solution)/shard_map/ppermute | solution.py:49
  110.6 14.1 %all-to-all-start.3 = ((bf16[4,512,256]{2,1,0:T(8,128)(2,1)}), bf16[4,512,256]{2,1,0:T(8,128)(2,1)}, u32[]{:S(2)}, u32[]{:S(2)}) async-start(bf16[4,512,256]{2,1,0:T(8,128)(2,1)} %get-tuple-element.47), calls=%async_computation.3 | async-start | bytes 2097152 | tf_op jit(solution)/shard_map/all_to_all | solution.py:86
  123.0 15.5 %copy-start.14 = (bf16[256,2048]{1,0:T(8,128)(2,1)S(1)}, bf16[256,2048]{1,0:T(8,128)(2,1)}, u32[]{:S(2)}) copy-start(bf16[256,2048]{1,0:T(8,128)(2,1)} %copy-done.13) | copy-start | bytes 3145732
  126.5 12.1 %collective-permute-start.18 = (bf16[2048,256]{1,0:T(8,128)(2,1)S(1)}, bf16[2048,256]{1,0:T(8,128)(2,1)S(1)}, u32[]{:S(2)}, u32[]{:S(2)}) collective-permute-start(bf16[2048,256]{1,0:T(8,128)(2,1)S(1)} %get-tuple-element.57), channel_id=1, source_target_pairs={{0,128},{128,0},{1,129},{129,1},{2,130},{130,2},{3,131},{131,3},{4... | collective-permute-start | bytes 3145736 | tf_op jit(solution)/shard_map/ppermute | solution.py:53
  133.7 4.9 %collective-permute-start.14 = (f32[256,256]{1,0:T(8,128)S(1)}, f32[256,256]{1,0:T(8,128)S(1)}, u32[]{:S(2)}, u32[]{:S(2)}) collective-permute-start(f32[256,256]{1,0:T(8,128)S(1)} %fusion.18), channel_id=1, source_target_pairs={{0,128},{128,0},{1,129},{129,1},{2,130},{130,2},{3,131},{131,3},{4... | collective-permute-start | bytes 786440 | tf_op jit(solution)/shard_map/ppermute | solution.py:53
  133.8 6.3 %collective-permute-start.15 = (f32[1,256]{1,0:T(1,128)S(1)}, f32[1,256]{1,0:T(1,128)S(1)}, u32[]{:S(2)}, u32[]{:S(2)}) collective-permute-start(f32[1,256]{1,0:T(1,128)S(1)} %bitcast.52), channel_id=1, source_target_pairs={{0,1},{1,2},{2,3},{3,0},{4,5},{5,6},{6,7},{7,4},{8,9},{9,10},{10,1... | collective-permute-start | bytes 3080 | tf_op jit(solution)/shard_map/ppermute | solution.py:42
  134.4 5.6 %collective-permute-start.16 = (f32[1,256]{1,0:T(1,128)S(1)}, f32[1,256]{1,0:T(1,128)S(1)}, u32[]{:S(2)}, u32[]{:S(2)}) collective-permute-start(f32[1,256]{1,0:T(1,128)S(1)} %bitcast.53), channel_id=1, source_target_pairs={{0,2},{1,3},{2,0},{3,1},{4,6},{5,7},{6,4},{7,5},{8,10},{9,11},{10,... | collective-permute-start | bytes 3080 | tf_op jit(solution)/shard_map/ppermute | solution.py:42
  136.6 3.5 %collective-permute-start.17 = (f32[1,256]{1,0:T(1,128)S(1)}, f32[1,256]{1,0:T(1,128)S(1)}, u32[]{:S(2)}, u32[]{:S(2)}) collective-permute-start(f32[1,256]{1,0:T(1,128)S(1)} %bitcast.54), channel_id=1, source_target_pairs={{0,3},{1,0},{2,1},{3,2},{4,7},{5,4},{6,5},{7,6},{8,11},{9,8},{10,9... | collective-permute-start | bytes 3080 | tf_op jit(solution)/shard_map/ppermute | solution.py:42
  140.1 2.8 %collective-permute-start.19 = (f32[1,256]{1,0:T(1,128)S(1)}, f32[1,256]{1,0:T(1,128)S(1)}, u32[]{:S(2)}, u32[]{:S(2)}) collective-permute-start(f32[1,256]{1,0:T(1,128)S(1)} %rsqrt_multiply_fusion), channel_id=1, source_target_pairs={{0,128},{128,0},{1,129},{129,1},{2,130},{130,2},{3,131},{131,3},{4... | collective-permute-start | bytes 3080 | tf_op jit(solution)/shard_map/ppermute | solution.py:53
  (15 other events, 97.0 us)

commit v6 on v5

--- a/solution.py
+++ b/solution.py
@@ -118,6 +118,12 @@
     other[...] = jnp.where(first, output, query).astype(jnp.bfloat16)
 
 
+def choose_kernel(index, query, output, taken, given):
+    first = index[N_TP] == 0
+    taken[...] = jnp.where(first, query[...], output[...])
+    given[...] = jnp.where(first, output[...], query[...])
+
+
 def order_kernel(index, *refs):
     for w in range(2):
         far, own, up, down, out = refs[w::2]
@@ -125,8 +131,9 @@
             out[pl.ds(index[at], 1)] = tokens[...][None]
 
 
-def indexed_kernel(body, index, operands, results, name):
-    spec = lambda block, place: pl.BlockSpec(block, place)
+def indexed_kernel(body, index, operands, results, name, limit=6):
+    spec = lambda block, place: pl.BlockSpec(block, place, pipeline_mode=pl.Buffered(1))
+    results = [(jax.ShapeDtypeStruct(a.shape, a.dtype), block, place) for a, block, place in results]
     return pl.pallas_call(
         body,
         grid_spec=pltpu.PrefetchScalarGridSpec(
@@ -137,7 +144,7 @@
         ),
         out_shape=[shape for shape, _, _ in results],
         compiler_params=pltpu.CompilerParams(
-            dimension_semantics=("arbitrary",), vmem_limit_bytes=24 << 20
+            dimension_semantics=("arbitrary",), vmem_limit_bytes=limit << 20
         ),
         cost_estimate=pl.CostEstimate(flops=1 << 20, bytes_accessed=1 << 20, transcendentals=0),
         name=name,
@@ -296,6 +303,7 @@
         + [all_of(a) for a in moments + bases],
         [all_of(square)] * 2,
         "near_tokens",
+        limit=12,
     )
     mine, other = indexed_kernel(
         far_kernel,
@@ -320,7 +328,13 @@
         ).astype(jnp.bfloat16)
         for w in range(2)
     ]
-    taken, given = split(buffers)
+    taken, given = indexed_kernel(
+        choose_kernel,
+        index,
+        [all_of(a) for a in buffers],
+        [all_of(a) for a in buffers],
+        "choose_buffers",
+    )
     parts, taken, given = lax.optimization_barrier((from_all(mine, shift_tp), taken, given))
     given = swap_cores(given)
     power = total(parts)

time: 146 us -> 143 us (0.979)
  local copies, waits for them, and re-layouts: 3.76 us -> 0.21 us
  Pallas kernels: 15.8 us -> 13.9 us
    dot_general x5, matrix products: 10.1 us -> 6.29 us  [contract_rows(): lax.dot_general(left, right, (((0,), (0,)), ((), ())), precision=precisio...]
    unnamed x34 -> x24, local copies, waits for them, and re-layouts: 3.61 us -> 0.05 us
    dot_general x2, matrix products: 3.01 us -> 5.2 us  [per_device(): jnp.dot((orthos[w] * scales[w]).astype(jnp.bfloat16), rights[w].T, prefer...]
    dot_general x2, matrix products: 2.98 us -> 5.14 us  [per_device(): jnp.dot(orthos[w].astype(jnp.bfloat16), rights[w].T, preferred_element_ty...]
    pallas_call x3 -> x4, Pallas kernels: 5.96 us -> 4.05 us  [indexed_kernel(): pl.pallas_call(body, grid_spec=pltpu.PrefetchScalarGridSpec(num_scalar_pr...]
  transfers between devices with their start and end apart: 22 -> 22, of which waited for: 4 -> 7; matrix products, arithmetic and copies ran while one was open for 17% -> 17% of each run, Pallas kernels for 9% -> 8%
where the time goes in v6:
time: 143 us
  starting transfers between devices  38.3 us (27%)
  blocking collectives  38 us (27%)
  matrix products  31.5 us (22%)
  waiting for transfers between devices  19.4 us (14%)
  Pallas kernels  13.9 us (10%)
    all_to_all x2, blocking collectives, exchange(): return lax.all_to_all(x, 'fsdp', 0, 0, axis_index_groups=groups)  38 us
    ppermute x12, starting transfers between devices, shift_tp(): return lax.ppermute(x, 'tp', [(i, (i + by) % N_TP) for i in range(N_TP)])  14.9 us
    ppermute x5, starting transfers between devices, swap_cores(): return lax.ppermute(x, 'rep', [(0, 1), (1, 0)])  12.6 us
    dot_general x2, matrix products, per_device(): product = jnp.dot(grad, bases[w], preferred_element_type=jnp.float32)  11.8 us
    all_to_all x2, waiting for transfers between devices, exchange(): return lax.all_to_all(x, 'fsdp', 0, 0, axis_index_groups=groups)  11.6 us
    all_to_all x2, starting transfers between devices, exchange(): return lax.all_to_all(x, 'fsdp', 0, 0, axis_index_groups=groups)  7.89 us
    pallas_call x1, Pallas kernels, inverse_factor(): pl.pallas_call(inverse_kernel, out_shape=jax.ShapeDtypeStruct((RANK, RANK...  7.84 us
    dot_general x5, matrix products, contract_rows(): lax.dot_general(left, right, (((0,), (0,)), ((), ())), precision=precisio...  6.29 us
  transfers between devices with their start and end apart: 22, of which 7 were waited for; matrix products, arithmetic and copies ran while one was open for 17% of the time, Pallas kernels for 8%

profile of v6, /device:TPU:1, one launch (start us, length us, event | category | flops | bytes accessed | tf_op | source)
XLA Modules:
  0.0 142.6 jit_solution(2808956158306910366)
XLA Ops:
  0.6 3.4 %collective-permute-start.2 = (bf16[512,256]{1,0:T(8,128)(2,1)}, bf16[512,256]{1,0:T(8,128)(2,1)S(1)}, u32[]{:S(2)}, u32[]{:S(2)}) collective-permute-start(bf16[512,256]{1,0:T(8,128)(2,1)} %refs_3_.1), channel_id=1, source_target_pairs={{0,3},{1,0},{2,1},{3,2},{4,7},{5,4},{6,5},{7,6},{8,11},{9,8},{10,9... | collective-permute-start | bytes 786440 | tf_op jit(solution)/shard_map/ppermute | solution.py:42
  4.2 2.5 %collective-permute-start.5 = (bf16[512,256]{1,0:T(8,128)(2,1)}, bf16[512,256]{1,0:T(8,128)(2,1)S(1)}, u32[]{:S(2)}, u32[]{:S(2)}) collective-permute-start(bf16[512,256]{1,0:T(8,128)(2,1)} %refs_2_.1), channel_id=1, source_target_pairs={{0,3},{1,0},{2,1},{3,2},{4,7},{5,4},{6,5},{7,6},{8,11},{9,8},{10,9... | collective-permute-start | bytes 786440 | tf_op jit(solution)/shard_map/ppermute | solution.py:42
  6.7 6.0 %convolution_convert_fusion.3.refs_6_.refs_8_.refs_10_.refs_2_ = bf16[2048,256]{1,0:T(8,128)(2,1)S(1)} fusion(bf16[2048,2048]{1,0:T(8,128)(2,1)} %param.9, bf16[2048,256]{1,0:T(8,128)(2,1)} %refs_14_.1), kind=kOutput, calls=%fused_computation.15 | convolution fusion | flops 2148007936 | bytes 10485760 | tf_op jit(solution)/shard_map/dot_general | solution.py:295
  12.9 5.0 %collective-permute-done.refs_2_.refs_4_ = bf16[512,256]{1,0:T(8,128)(2,1)S(1)} collective-permute-done((bf16[512,256]{1,0:T(8,128)(2,1)}, bf16[512,256]{1,0:T(8,128)(2,1)S(1)}, u32[]{:S(2)}, u32[]{:S(2)}) %collective-permute-start) | collective-permute-done | bytes 262176 | tf_op jit(solution)/shard_map/ppermute | solution.py:42
  17.9 2.7 %collective-permute-start.3 = (bf16[512,256]{1,0:T(8,128)(2,1)S(1)}, bf16[512,256]{1,0:T(8,128)(2,1)S(1)}, u32[]{:S(2)}, u32[]{:S(2)}) collective-permute-start(bf16[512,256]{1,0:T(8,128)(2,1)S(1)} %collective-permute-done.2.refs_5_.refs_7_), channel_id=1, source_target_pairs={{0,3},{1,0},{2,1},{3,2},{4,7},{5,4},{6,5},{7,6},{8,11},{9,8},{10,9... | collective-permute-start | bytes 786440 | tf_op jit(solution)/shard_map/ppermute | solution.py:42
  20.6 5.9 %convolution_convert_fusion.2.refs_7_.refs_9_.refs_11_.refs_3_ = bf16[2048,256]{1,0:T(8,128)(2,1)S(1)} fusion(bf16[2048,2048]{1,0:T(8,128)(2,1)} %param.11, bf16[2048,256]{1,0:T(8,128)(2,1)S(1)} %copy-done.3), kind=kOutput, calls=%fused_computation.14 | convolution fusion | flops 2148007936 | bytes 10485760 | tf_op jit(solution)/shard_map/dot_general | solution.py:295
  29.2 2.5 %collective-permute-start.6 = (bf16[256,256]{1,0:T(8,128)(2,1)S(1)}, bf16[256,256]{1,0:T(8,128)(2,1)S(1)}, u32[]{:S(2)}, u32[]{:S(2)}) collective-permute-start(bf16[256,256]{1,0:T(8,128)(2,1)S(1)} %get-tuple-element.36), channel_id=1, source_target_pairs={{0,128},{128,0},{1,129},{129,1},{2,130},{130,2},{3,131},{131,3},{4... | collective-permute-start | bytes 393224 | tf_op jit(solution)/shard_map/ppermute | solution.py:53
  35.5 2.3 %fusion.2.query = bf16[256,2048]{1,0:T(8,128)(2,1)S(1)} fusion(bf16[2048,256]{1,0:T(8,128)(2,1)S(1)} %bitcast.46, bf16[2048,2048]{1,0:T(8,128)(2,1)S(1)} %bitcast.49, bf16[1,256,2048]{2,1,0:T(8,128)(2,1)S(1)} %copy-done), kind=kOutput, calls=%fused_computation.7 | convolution fusion | flops 2149056512 | bytes 11534336 | tf_op jit(solution)/shard_map/dot_general | solution.py:27
  37.9 2.3 %fusion.3.output = bf16[256,2048]{1,0:T(8,128)(2,1)S(1)} fusion(bf16[2048,256]{1,0:T(8,128)(2,1)S(1)} %bitcast.45, bf16[2048,2048]{1,0:T(8,128)(2,1)S(1)} %bitcast.51, bf16[1,256,2048]{2,1,0:T(8,128)(2,1)S(1)} %copy-done.1), kind=kOutput, calls=%fused_computation.8 | convolution fusion | flops 2149056512 | bytes 11534336 | tf_op jit(solution)/shard_map/dot_general | solution.py:27
  46.8 19.6 %all_to_all.20.pieces = bf16[4,576,256]{2,1,0:T(8,128)(2,1)S(1)} all-to-all(bf16[4,576,256]{2,1,0:T(8,128)(2,1)S(1)} %pack_quarters.1), channel_id=1, replica_groups={{0,32,64,96},{4,36,68,100},{8,40,72,104},{12,44,76,108},{16,48,80,112},..., dimensions={0} | all-to-all | bytes 2359296 | tf_op jit(solution)/shard_map/all_to_all | solution.py:86
  66.6 18.3 %all_to_all.21.pieces = bf16[8,80,256]{2,1,0:T(8,128)(2,1)S(1)} all-to-all(bf16[8,80,256]{2,1,0:T(8,128)(2,1)S(1)} %sum_over_y.1), channel_id=1, replica_groups={{0,4,8,12,16,20,24,28},{32,36,40,44,48,52,56,60},{64,68,72,76,80,84,88,..., dimensions={0} | all-to-all | bytes 655360 | tf_op jit(solution)/shard_map/all_to_all | solution.py:86
  85.7 3.4 %all-to-all-start.2 = ((bf16[8,80,256]{2,1,0:T(8,128)(2,1)}), bf16[8,80,256]{2,1,0:T(8,128)(2,1)S(1)}, u32[]{:S(2)}, u32[]{:S(2)}) async-start(bf16[8,80,256]{2,1,0:T(8,128)(2,1)} %sum_over_z.1), calls=%async_computation.2 | async-start | bytes 655360 | tf_op jit(solution)/shard_map/all_to_all | solution.py:86
  89.2 10.0 %all-to-all-done.2.pieces = bf16[8,80,256]{2,1,0:T(8,128)(2,1)S(1)} async-done(((bf16[8,80,256]{2,1,0:T(8,128)(2,1)}), bf16[8,80,256]{2,1,0:T(8,128)(2,1)S(1)}, u32[]{:S(2)}, u32[]{:S(2)}) %all-to-all-start.2) | async-done | bytes 327712 | tf_op jit(solution)/shard_map/all_to_all | solution.py:86
  100.5 1.8 %collective-permute-start.12 = (f32[64,256]{1,0:T(8,128)S(1)}, f32[64,256]{1,0:T(8,128)S(1)}, u32[]{:S(2)}, u32[]{:S(2)}) collective-permute-start(f32[64,256]{1,0:T(8,128)S(1)} %get-tuple-element.50), channel_id=1, source_target_pairs={{0,64},{4,68},{8,72},{12,76},{16,80},{20,84},{24,88},{28,92},{32,9... | collective-permute-start | bytes 196616 | tf_op jit(solution)/shard_map/ppermute | solution.py:49
  103.1 4.5 %all-to-all-start.3 = ((bf16[4,512,256]{2,1,0:T(8,128)(2,1)}), bf16[4,512,256]{2,1,0:T(8,128)(2,1)}, u32[]{:S(2)}, u32[]{:S(2)}) async-start(bf16[4,512,256]{2,1,0:T(8,128)(2,1)} %get-tuple-element.51), calls=%async_computation.3 | async-start | bytes 2097152 | tf_op jit(solution)/shard_map/all_to_all | solution.py:86
  107.7 7.8 %inverse_factor.1 = f32[256,256]{1,0:T(8,128)S(1)} custom-call(f32[256,256]{1,0:T(8,128)S(1)} %bitcast.47), custom_call_target="tpu_custom_call" | custom-call | flops 8000000000 | bytes 1048576 | tf_op jit(solution)/shard_map/inverse_factor/pallas_call | solution.py:250
  117.2 1.9 %multiply_reduce_fusion = (f32[256]{0:T(256)S(1)}, bf16[2048,256]{1,0:T(8,128)(2,1)S(1)}) fusion(bf16[2048,256]{1,0:T(8,128)(2,1)} %bitcast.14, f32[256,256]{1,0:T(8,128)S(1)} %inverse_factor.1), kind=kOutput, calls=%fused_computation.18 | convolution fusion | flops 270073600 | bytes 2360320 | tf_op jit(solution)/shard_map/dot_general | solution.py:370
  119.1 6.7 %collective-permute-start.18 = (bf16[2048,256]{1,0:T(8,128)(2,1)S(1)}, bf16[2048,256]{1,0:T(8,128)(2,1)}, u32[]{:S(2)}, u32[]{:S(2)}) collective-permute-start(bf16[2048,256]{1,0:T(8,128)(2,1)S(1)} %get-tuple-element.61), channel_id=1, source_target_pairs={{0,128},{128,0},{1,129},{129,1},{2,130},{130,2},{3,131},{131,3},{4... | collective-permute-start | bytes 3145736 | tf_op jit(solution)/shard_map/ppermute | solution.py:53
  127.0 3.2 %collective-permute-start.16 = (f32[1,256]{1,0:T(1,128)S(1)}, f32[1,256]{1,0:T(1,128)S(1)}, u32[]{:S(2)}, u32[]{:S(2)}) collective-permute-start(f32[1,256]{1,0:T(1,128)S(1)} %bitcast.55), channel_id=1, source_target_pairs={{0,2},{1,3},{2,0},{3,1},{4,6},{5,7},{6,4},{7,5},{8,10},{9,11},{10,... | collective-permute-start | bytes 3080 | tf_op jit(solution)/shard_map/ppermute | solution.py:42
  130.3 2.7 %fusion.8 = bf16[1,256,2048]{2,1,0:T(8,128)(2,1)} fusion(bf16[256,2048]{1,0:T(8,128)(2,1)S(1)} %fusion.2.query, bf16[2048,256]{1,0:T(8,128)(2,1)S(1)} %get-tuple-element.61, bf16[2048,256]{1,0:T(8,128)(2,1)} %collective-permute-done.18, pred[]{:T(512)S(6)} %eq.12, f32[256,256]{1,0:T(8,128)} %fusion.18, f32[256,256]{1,0:T(8,128)S(1)} %collective-permute-done.14), kind=kOutput, calls=%fused_computation.17 | convolution fusion | flops 271122432 | bytes 4718593 | tf_op jit(solution)/shard_map/dot_general | solution.py:376
  133.1 1.9 %collective-permute-start.19 = (f32[1,256]{1,0:T(1,128)S(1)}, f32[1,256]{1,0:T(1,128)S(1)}, u32[]{:S(2)}, u32[]{:S(2)}) collective-permute-start(f32[1,256]{1,0:T(1,128)S(1)} %rsqrt_multiply_fusion), channel_id=1, source_target_pairs={{0,128},{128,0},{1,129},{129,1},{2,130},{130,2},{3,131},{131,3},{4... | collective-permute-start | bytes 3080 | tf_op jit(solution)/shard_map/ppermute | solution.py:53
  134.9 2.4 %fusion.7 = bf16[1,256,2048]{2,1,0:T(8,128)(2,1)} fusion(bf16[256,2048]{1,0:T(8,128)(2,1)S(1)} %fusion.3.output, bf16[2048,256]{1,0:T(8,128)(2,1)} %collective-permute-done.18, bf16[2048,256]{1,0:T(8,128)(2,1)S(1)} %get-tuple-element.61, pred[]{:T(512)S(6)} %eq.12, f32[256,256]{1,0:T(8,128)S(1)} %collective-permute-done.14, f32[256,256]{1,0:T(8,128)} %fusion.18), kind=kOutput, calls=%fused_computation.16 | convolution fusion | flops 271122432 | bytes 4718593 | tf_op jit(solution)/shard_map/dot_general | solution.py:376
  137.4 2.5 %convolution_convert_fusion = bf16[256,2048]{1,0:T(8,128)(2,1)} fusion(bf16[2048,256]{1,0:T(8,128)(2,1)} %collective-permute-done.18, bf16[2048,256]{1,0:T(8,128)(2,1)S(1)} %get-tuple-element.61, pred[]{:T(512)S(6)} %eq.12, f32[256]{0:T(256)S(1)} %bitcast.53, f32[256,256]{1,0:T(8,128)S(1)} %collective-permute-done.14, f32[256,256]{1,0:T(8,128)} %fusion.18), kind=kOutput, calls=%fused_computation.12 | convolution fusion | flops 269680640 | bytes 3671041 | tf_op jit(solution)/shard_map/dot_general | solution.py:389
  139.8 2.7 %convolution_convert_fusion.1 = bf16[256,2048]{1,0:T(8,128)(2,1)} fusion(bf16[2048,256]{1,0:T(8,128)(2,1)S(1)} %get-tuple-element.61, bf16[2048,256]{1,0:T(8,128)(2,1)} %collective-permute-done.18, pred[]{:T(512)S(6)} %eq.12, f32[256]{0:T(256)S(1)} %bitcast.52, f32[256,256]{1,0:T(8,128)} %fusion.18, f32[256,256]{1,0:T(8,128)S(1)} %collective-permute-done.14), kind=kOutput, calls=%fused_computation.13 | convolution fusion | flops 269680640 | bytes 3671041 | tf_op jit(solution)/shard_map/dot_general | solution.py:389
  (80 shorter events, 19.3 us)
Async XLA Ops:
  0.6 20.0 %copy-start.3 = (bf16[2048,256]{1,0:T(8,128)(2,1)S(1)}, bf16[2048,256]{1,0:T(8,128)(2,1)}, u32[]{:S(2)}) copy-start(bf16[2048,256]{1,0:T(8,128)(2,1)} %refs_15_.1) | copy-start | bytes 3145732
  0.6 17.3 %collective-permute-start.2 = (bf16[512,256]{1,0:T(8,128)(2,1)}, bf16[512,256]{1,0:T(8,128)(2,1)S(1)}, u32[]{:S(2)}, u32[]{:S(2)}) collective-permute-start(bf16[512,256]{1,0:T(8,128)(2,1)} %refs_3_.1), channel_id=1, source_target_pairs={{0,3},{1,0},{2,1},{3,2},{4,7},{5,4},{6,5},{7,6},{8,11},{9,8},{10,9... | collective-permute-start | bytes 786440 | tf_op jit(solution)/shard_map/ppermute | solution.py:42
  4.0 22.5 %collective-permute-start.4 = (bf16[512,256]{1,0:T(8,128)(2,1)}, bf16[512,256]{1,0:T(8,128)(2,1)S(1)}, u32[]{:S(2)}, u32[]{:S(2)}) collective-permute-start(bf16[512,256]{1,0:T(8,128)(2,1)} %refs_3_.1), channel_id=1, source_target_pairs={{0,1},{1,2},{2,3},{3,0},{4,5},{5,6},{6,7},{7,4},{8,9},{9,10},{10,1... | collective-permute-start | bytes 786440 | tf_op jit(solution)/shard_map/ppermute | solution.py:42
  4.0 13.9 %collective-permute-start = (bf16[512,256]{1,0:T(8,128)(2,1)}, bf16[512,256]{1,0:T(8,128)(2,1)S(1)}, u32[]{:S(2)}, u32[]{:S(2)}) collective-permute-start(bf16[512,256]{1,0:T(8,128)(2,1)} %refs_2_.1), channel_id=1, source_target_pairs={{0,1},{1,2},{2,3},{3,0},{4,5},{5,6},{6,7},{7,4},{8,9},{9,10},{10,1... | collective-permute-start | bytes 786440 | tf_op jit(solution)/shard_map/ppermute | solution.py:42
  4.2 22.3 %collective-permute-start.5 = (bf16[512,256]{1,0:T(8,128)(2,1)}, bf16[512,256]{1,0:T(8,128)(2,1)S(1)}, u32[]{:S(2)}, u32[]{:S(2)}) collective-permute-start(bf16[512,256]{1,0:T(8,128)(2,1)} %refs_2_.1), channel_id=1, source_target_pairs={{0,3},{1,0},{2,1},{3,2},{4,7},{5,4},{6,5},{7,6},{8,11},{9,8},{10,9... | collective-permute-start | bytes 786440 | tf_op jit(solution)/shard_map/ppermute | solution.py:42
  17.9 10.4 %collective-permute-start.1 = (bf16[512,256]{1,0:T(8,128)(2,1)S(1)}, bf16[512,256]{1,0:T(8,128)(2,1)S(1)}, u32[]{:S(2)}, u32[]{:S(2)}) collective-permute-start(bf16[512,256]{1,0:T(8,128)(2,1)S(1)} %collective-permute-done.refs_2_.refs_4_), channel_id=1, source_target_pairs={{0,1},{1,2},{2,3},{3,0},{4,5},{5,6},{6,7},{7,4},{8,9},{9,10},{10,1... | collective-permute-start | bytes 786440 | tf_op jit(solution)/shard_map/ppermute | solution.py:42
  17.9 10.4 %collective-permute-start.3 = (bf16[512,256]{1,0:T(8,128)(2,1)S(1)}, bf16[512,256]{1,0:T(8,128)(2,1)S(1)}, u32[]{:S(2)}, u32[]{:S(2)}) collective-permute-start(bf16[512,256]{1,0:T(8,128)(2,1)S(1)} %collective-permute-done.2.refs_5_.refs_7_), channel_id=1, source_target_pairs={{0,3},{1,0},{2,1},{3,2},{4,7},{5,4},{6,5},{7,6},{8,11},{9,8},{10,9... | collective-permute-start | bytes 786440 | tf_op jit(solution)/shard_map/ppermute | solution.py:42
  20.6 14.9 %slice-start = ((s8[8388608]{0:T(1024)(128)(4,1)}), s8[4194304]{0:T(1024)(128)(4,1)S(1)}, s32[]{:S(2)}) async-start(s8[8388608]{0:T(1024)(128)(4,1)} %bitcast.48), calls=%async_computation.4 | async-start | bytes 8388608
  29.2 3.5 %collective-permute-start.6 = (bf16[256,256]{1,0:T(8,128)(2,1)S(1)}, bf16[256,256]{1,0:T(8,128)(2,1)S(1)}, u32[]{:S(2)}, u32[]{:S(2)}) collective-permute-start(bf16[256,256]{1,0:T(8,128)(2,1)S(1)} %get-tuple-element.36), channel_id=1, source_target_pairs={{0,128},{128,0},{1,129},{129,1},{2,130},{130,2},{3,131},{131,3},{4... | collective-permute-start | bytes 393224 | tf_op jit(solution)/shard_map/ppermute | solution.py:53
  32.7 8.9 %collective-permute-start.7 = (bf16[256,256]{1,0:T(8,128)(2,1)S(1)}, bf16[256,256]{1,0:T(8,128)(2,1)S(1)}, u32[]{:S(2)}, u32[]{:S(2)}) collective-permute-start(bf16[256,256]{1,0:T(8,128)(2,1)S(1)} %add_convert_fusion), channel_id=1, source_target_pairs={{0,1},{1,2},{2,3},{3,0},{4,5},{5,6},{6,7},{7,4},{8,9},{9,10},{10,1... | collective-permute-start | bytes 393224 | tf_op jit(solution)/shard_map/ppermute | solution.py:42
  32.8 8.8 %collective-permute-start.8 = (bf16[256,256]{1,0:T(8,128)(2,1)S(1)}, bf16[256,256]{1,0:T(8,128)(2,1)S(1)}, u32[]{:S(2)}, u32[]{:S(2)}) collective-permute-start(bf16[256,256]{1,0:T(8,128)(2,1)S(1)} %add_convert_fusion), channel_id=1, source_target_pairs={{0,2},{1,3},{2,0},{3,1},{4,6},{5,7},{6,4},{7,5},{8,10},{9,11},{10,... | collective-permute-start | bytes 393224 | tf_op jit(solution)/shard_map/ppermute | solution.py:42
  33.8 8.1 %collective-permute-start.9 = (bf16[256,256]{1,0:T(8,128)(2,1)S(1)}, bf16[256,256]{1,0:T(8,128)(2,1)S(1)}, u32[]{:S(2)}, u32[]{:S(2)}) collective-permute-start(bf16[256,256]{1,0:T(8,128)(2,1)S(1)} %add_convert_fusion), channel_id=1, source_target_pairs={{0,3},{1,0},{2,1},{3,2},{4,7},{5,4},{6,5},{7,6},{8,11},{9,8},{10,9... | collective-permute-start | bytes 393224 | tf_op jit(solution)/shard_map/ppermute | solution.py:42
  41.9 3.8 %collective-permute-start.10 = (bf16[256,2048]{1,0:T(8,128)(2,1)S(1)}, bf16[256,2048]{1,0:T(8,128)(2,1)S(1)}, u32[]{:S(2)}, u32[]{:S(2)}) collective-permute-start(bf16[256,2048]{1,0:T(8,128)(2,1)S(1)} %get-tuple-element.49), channel_id=1, source_target_pairs={{0,128},{128,0},{1,129},{129,1},{2,130},{130,2},{3,131},{131,3},{4... | collective-permute-start | bytes 3145736 | tf_op jit(solution)/shard_map/ppermute | solution.py:53
  85.7 13.5 %all-to-all-start.2 = ((bf16[8,80,256]{2,1,0:T(8,128)(2,1)}), bf16[8,80,256]{2,1,0:T(8,128)(2,1)S(1)}, u32[]{:S(2)}, u32[]{:S(2)}) async-start(bf16[8,80,256]{2,1,0:T(8,128)(2,1)} %sum_over_z.1), calls=%async_computation.2 | async-start | bytes 655360 | tf_op jit(solution)/shard_map/all_to_all | solution.py:86
  100.2 7.5 %collective-permute-start.11 = (f32[64,256]{1,0:T(8,128)S(1)}, f32[64,256]{1,0:T(8,128)S(1)}, u32[]{:S(2)}, u32[]{:S(2)}) collective-permute-start(f32[64,256]{1,0:T(8,128)S(1)} %get-tuple-element.50), channel_id=1, source_target_pairs={{0,32},{4,36},{8,40},{12,44},{16,48},{20,52},{24,56},{28,60},{32,6... | collective-permute-start | bytes 196616 | tf_op jit(solution)/shard_map/ppermute | solution.py:49
  100.5 7.2 %collective-permute-start.12 = (f32[64,256]{1,0:T(8,128)S(1)}, f32[64,256]{1,0:T(8,128)S(1)}, u32[]{:S(2)}, u32[]{:S(2)}) collective-permute-start(f32[64,256]{1,0:T(8,128)S(1)} %get-tuple-element.50), channel_id=1, source_target_pairs={{0,64},{4,68},{8,72},{12,76},{16,80},{20,84},{24,88},{28,92},{32,9... | collective-permute-start | bytes 196616 | tf_op jit(solution)/shard_map/ppermute | solution.py:49
  102.3 5.4 %collective-permute-start.13 = (f32[64,256]{1,0:T(8,128)S(1)}, f32[64,256]{1,0:T(8,128)S(1)}, u32[]{:S(2)}, u32[]{:S(2)}) collective-permute-start(f32[64,256]{1,0:T(8,128)S(1)} %get-tuple-element.50), channel_id=1, source_target_pairs={{0,96},{4,100},{8,104},{12,108},{16,112},{20,116},{24,120},{28,124... | collective-permute-start | bytes 196616 | tf_op jit(solution)/shard_map/ppermute | solution.py:49
  103.1 14.0 %all-to-all-start.3 = ((bf16[4,512,256]{2,1,0:T(8,128)(2,1)}), bf16[4,512,256]{2,1,0:T(8,128)(2,1)}, u32[]{:S(2)}, u32[]{:S(2)}) async-start(bf16[4,512,256]{2,1,0:T(8,128)(2,1)} %get-tuple-element.51), calls=%async_computation.3 | async-start | bytes 2097152 | tf_op jit(solution)/shard_map/all_to_all | solution.py:86
  119.1 11.3 %collective-permute-start.18 = (bf16[2048,256]{1,0:T(8,128)(2,1)S(1)}, bf16[2048,256]{1,0:T(8,128)(2,1)}, u32[]{:S(2)}, u32[]{:S(2)}) collective-permute-start(bf16[2048,256]{1,0:T(8,128)(2,1)S(1)} %get-tuple-element.61), channel_id=1, source_target_pairs={{0,128},{128,0},{1,129},{129,1},{2,130},{130,2},{3,131},{131,3},{4... | collective-permute-start | bytes 3145736 | tf_op jit(solution)/shard_map/ppermute | solution.py:53
  127.0 3.4 %collective-permute-start.14 = (f32[256,256]{1,0:T(8,128)}, f32[256,256]{1,0:T(8,128)S(1)}, u32[]{:S(2)}, u32[]{:S(2)}) collective-permute-start(f32[256,256]{1,0:T(8,128)} %fusion.18), channel_id=1, source_target_pairs={{0,128},{128,0},{1,129},{129,1},{2,130},{130,2},{3,131},{131,3},{4... | collective-permute-start | bytes 786440 | tf_op jit(solution)/shard_map/ppermute | solution.py:53
  127.0 6.1 %collective-permute-start.15 = (f32[1,256]{1,0:T(1,128)S(1)}, f32[1,256]{1,0:T(1,128)S(1)}, u32[]{:S(2)}, u32[]{:S(2)}) collective-permute-start(f32[1,256]{1,0:T(1,128)S(1)} %bitcast.54), channel_id=1, source_target_pairs={{0,1},{1,2},{2,3},{3,0},{4,5},{5,6},{6,7},{7,4},{8,9},{9,10},{10,1... | collective-permute-start | bytes 3080 | tf_op jit(solution)/shard_map/ppermute | solution.py:42
  127.0 6.1 %collective-permute-start.16 = (f32[1,256]{1,0:T(1,128)S(1)}, f32[1,256]{1,0:T(1,128)S(1)}, u32[]{:S(2)}, u32[]{:S(2)}) collective-permute-start(f32[1,256]{1,0:T(1,128)S(1)} %bitcast.55), channel_id=1, source_target_pairs={{0,2},{1,3},{2,0},{3,1},{4,6},{5,7},{6,4},{7,5},{8,10},{9,11},{10,... | collective-permute-start | bytes 3080 | tf_op jit(solution)/shard_map/ppermute | solution.py:42
  130.2 2.8 %collective-permute-start.17 = (f32[1,256]{1,0:T(1,128)S(1)}, f32[1,256]{1,0:T(1,128)S(1)}, u32[]{:S(2)}, u32[]{:S(2)}) collective-permute-start(f32[1,256]{1,0:T(1,128)S(1)} %bitcast.56), channel_id=1, source_target_pairs={{0,3},{1,0},{2,1},{3,2},{4,7},{5,4},{6,5},{7,6},{8,11},{9,8},{10,9... | collective-permute-start | bytes 3080 | tf_op jit(solution)/shard_map/ppermute | solution.py:42
  133.1 4.3 %collective-permute-start.19 = (f32[1,256]{1,0:T(1,128)S(1)}, f32[1,256]{1,0:T(1,128)S(1)}, u32[]{:S(2)}, u32[]{:S(2)}) collective-permute-start(f32[1,256]{1,0:T(1,128)S(1)} %rsqrt_multiply_fusion), channel_id=1, source_target_pairs={{0,128},{128,0},{1,129},{129,1},{2,130},{130,2},{3,131},{131,3},{4... | collective-permute-start | bytes 3080 | tf_op jit(solution)/shard_map/ppermute | solution.py:53
  (10 other events, 97.9 us)

commit v7 on v4

--- a/solution.py
+++ b/solution.py
@@ -324,11 +324,10 @@
     ]
     parts, buffers = lax.optimization_barrier((from_all(mine, shift_tp), buffers))
     power = total(parts)
-    power_b = power.astype(jnp.bfloat16)
-    powers_b = split([power_b, swap_cores(power_b)])
-    mine, other = split(
-        [contract_rows(buffers[w], powers_b[w]).astype(jnp.bfloat16) for w in range(2)]
-    )
+    power, power_b = lax.optimization_barrier((power, power.astype(jnp.bfloat16)))
+    taken, given = split(buffers)
+    mine = contract_rows(taken, power_b).astype(jnp.bfloat16)
+    other = contract_rows(given, swap_cores(power_b)).astype(jnp.bfloat16)
     other = swap_cores(other)
 
     width = mine.shape[1]

time: 139 us -> 138 us (level)
  no operation moved by 1% of the time
where the time goes in v7:
time: 138 us; the launch traced here: 137 us
  blocking collectives  38 us (28%)
  starting transfers between devices  34.8 us (25%)
  matrix products  26.4 us (19%)
  waiting for transfers between devices  23.3 us (17%)
  Pallas kernels  13.3 us (10%)
    all_to_all x2, blocking collectives, exchange(): return lax.all_to_all(x, 'fsdp', 0, 0, axis_index_groups=groups)  38 us
    ppermute x12, starting transfers between devices, shift_tp(): return lax.ppermute(x, 'tp', [(i, (i + by) % N_TP) for i in range(N_TP)])  13.6 us
    all_to_all x2, waiting for transfers between devices, exchange(): return lax.all_to_all(x, 'fsdp', 0, 0, axis_index_groups=groups)  13.5 us
    dot_general x2, matrix products, per_device(): product = jnp.dot(grad, bases[w], preferred_element_type=jnp.float32)  11.8 us
    ppermute x6, starting transfers between devices, swap_cores(): return lax.ppermute(x, 'rep', [(0, 1), (1, 0)])  11.2 us
    all_to_all x2, starting transfers between devices, exchange(): return lax.all_to_all(x, 'fsdp', 0, 0, axis_index_groups=groups)  7.9 us
    pallas_call x1, Pallas kernels, inverse_factor(): pl.pallas_call(inverse_kernel, out_shape=jax.ShapeDtypeStruct((RANK, RANK...  7.84 us
    ppermute x12, waiting for transfers between devices, shift_tp(): return lax.ppermute(x, 'tp', [(i, (i + by) % N_TP) for i in range(N_TP)])  6.82 us
  transfers between devices with their start and end apart: 23, of which 11 were waited for; matrix products, arithmetic and copies ran while one was open for 15% of the time, Pallas kernels for 7%

profile of v7, /device:TPU:1, one launch (start us, length us, event | category | flops | bytes accessed | tf_op | source)
XLA Modules:
  0.0 137.4 jit_solution(11269030216381328746)
XLA Ops:
  0.6 3.4 %collective-permute-start.5 = (bf16[512,256]{1,0:T(8,128)(2,1)}, bf16[512,256]{1,0:T(8,128)(2,1)S(1)}, u32[]{:S(2)}, u32[]{:S(2)}) collective-permute-start(bf16[512,256]{1,0:T(8,128)(2,1)} %refs_2_.1), channel_id=1, source_target_pairs={{0,3},{1,0},{2,1},{3,2},{4,7},{5,4},{6,5},{7,6},{8,11},{9,8},{10,9... | collective-permute-start | bytes 786440 | tf_op jit(solution)/shard_map/ppermute | solution.py:42
  4.2 2.5 %collective-permute-start.2 = (bf16[512,256]{1,0:T(8,128)(2,1)}, bf16[512,256]{1,0:T(8,128)(2,1)S(1)}, u32[]{:S(2)}, u32[]{:S(2)}) collective-permute-start(bf16[512,256]{1,0:T(8,128)(2,1)} %refs_3_.1), channel_id=1, source_target_pairs={{0,3},{1,0},{2,1},{3,2},{4,7},{5,4},{6,5},{7,6},{8,11},{9,8},{10,9... | collective-permute-start | bytes 786440 | tf_op jit(solution)/shard_map/ppermute | solution.py:42
  6.7 6.0 %convolution_convert_fusion.5.refs_6_.refs_8_.refs_10_.refs_2_ = bf16[2048,256]{1,0:T(8,128)(2,1)S(1)} fusion(bf16[2048,2048]{1,0:T(8,128)(2,1)} %param.9, bf16[2048,256]{1,0:T(8,128)(2,1)} %refs_14_.1), kind=kOutput, calls=%fused_computation.11 | convolution fusion | flops 2148007936 | bytes 10485760 | tf_op jit(solution)/shard_map/dot_general | solution.py:290
  12.9 2.0 %collective-permute-done.2.refs_5_.refs_7_ = bf16[512,256]{1,0:T(8,128)(2,1)S(1)} collective-permute-done((bf16[512,256]{1,0:T(8,128)(2,1)}, bf16[512,256]{1,0:T(8,128)(2,1)S(1)}, u32[]{:S(2)}, u32[]{:S(2)}) %collective-permute-start.2) | collective-permute-done | bytes 262176 | tf_op jit(solution)/shard_map/ppermute | solution.py:42
  15.8 2.5 %collective-permute-start.3 = (bf16[512,256]{1,0:T(8,128)(2,1)S(1)}, bf16[512,256]{1,0:T(8,128)(2,1)S(1)}, u32[]{:S(2)}, u32[]{:S(2)}) collective-permute-start(bf16[512,256]{1,0:T(8,128)(2,1)S(1)} %collective-permute-done.2.refs_5_.refs_7_), channel_id=1, source_target_pairs={{0,3},{1,0},{2,1},{3,2},{4,7},{5,4},{6,5},{7,6},{8,11},{9,8},{10,9... | collective-permute-start | bytes 786440 | tf_op jit(solution)/shard_map/ppermute | solution.py:42
  18.2 5.9 %convolution_convert_fusion.4.refs_7_.refs_9_.refs_11_.refs_3_ = bf16[2048,256]{1,0:T(8,128)(2,1)S(1)} fusion(bf16[2048,2048]{1,0:T(8,128)(2,1)} %param.11, bf16[2048,256]{1,0:T(8,128)(2,1)S(1)} %copy-done.3), kind=kOutput, calls=%fused_computation.10 | convolution fusion | flops 2148007936 | bytes 10485760 | tf_op jit(solution)/shard_map/dot_general | solution.py:290
  24.2 1.7 %near_tokens.1 = (f32[256,256]{1,0:T(8,128)S(1)}, f32[256,256]{1,0:T(8,128)S(1)}) custom-call(s32[5]{0:T(128)S(1)} %stack.23.index, bf16[512,256]{1,0:T(8,128)(2,1)S(1)} %copy-done.4, bf16[512,256]{1,0:T(8,128)(2,1)S(1)} %copy-done.5, bf16[512,256]{1,0:T(8,128)(2,1)S(1)} %collective-permute-done.refs_2_.refs_4_, ...), custom_call_target="tpu_custom_call" | custom-call | flops 1048576 | bytes 1048576 | tf_op jit(solution)/shard_map/near_tokens/pallas_call | solution.py:130
  26.9 1.9 %collective-permute-start.6 = (bf16[256,256]{1,0:T(8,128)(2,1)S(1)}, bf16[256,256]{1,0:T(8,128)(2,1)S(1)}, u32[]{:S(2)}, u32[]{:S(2)}) collective-permute-start(bf16[256,256]{1,0:T(8,128)(2,1)S(1)} %get-tuple-element.36), channel_id=1, source_target_pairs={{0,128},{128,0},{1,129},{129,1},{2,130},{130,2},{3,131},{131,3},{4... | collective-permute-start | bytes 393224 | tf_op jit(solution)/shard_map/ppermute | solution.py:53
  29.8 1.8 %collective-permute-start.9 = (bf16[256,256]{1,0:T(8,128)(2,1)S(1)}, bf16[256,256]{1,0:T(8,128)(2,1)S(1)}, u32[]{:S(2)}, u32[]{:S(2)}) collective-permute-start(bf16[256,256]{1,0:T(8,128)(2,1)S(1)} %add_convert_fusion), channel_id=1, source_target_pairs={{0,3},{1,0},{2,1},{3,2},{4,7},{5,4},{6,5},{7,6},{8,11},{9,8},{10,9... | collective-permute-start | bytes 393224 | tf_op jit(solution)/shard_map/ppermute | solution.py:42
  32.5 2.3 %fusion = bf16[256,2048]{1,0:T(8,128)(2,1)S(1)} fusion(bf16[2048,256]{1,0:T(8,128)(2,1)S(1)} %bitcast.46, bf16[2048,2048]{1,0:T(8,128)(2,1)S(1)} %bitcast.49, bf16[1,256,2048]{2,1,0:T(8,128)(2,1)S(1)} %copy-done), kind=kOutput, calls=%fused_computation.4 | convolution fusion | flops 2149056512 | bytes 11534336 | tf_op jit(solution)/shard_map/dot_general | solution.py:27
  34.9 2.3 %fusion.1 = bf16[256,2048]{1,0:T(8,128)(2,1)S(1)} fusion(bf16[2048,256]{1,0:T(8,128)(2,1)S(1)} %bitcast.45, bf16[2048,2048]{1,0:T(8,128)(2,1)S(1)} %bitcast.51, bf16[1,256,2048]{2,1,0:T(8,128)(2,1)S(1)} %copy-done.1), kind=kOutput, calls=%fused_computation.5 | convolution fusion | flops 2149056512 | bytes 11534336 | tf_op jit(solution)/shard_map/dot_general | solution.py:27
  37.6 3.1 %collective-permute-done.7 = bf16[256,256]{1,0:T(8,128)(2,1)S(1)} collective-permute-done((bf16[256,256]{1,0:T(8,128)(2,1)S(1)}, bf16[256,256]{1,0:T(8,128)(2,1)S(1)}, u32[]{:S(2)}, u32[]{:S(2)}) %collective-permute-start.7) | collective-permute-done | bytes 131104 | tf_op jit(solution)/shard_map/ppermute | solution.py:42
  46.2 19.6 %all_to_all.20.pieces = bf16[4,576,256]{2,1,0:T(8,128)(2,1)S(1)} all-to-all(bf16[4,576,256]{2,1,0:T(8,128)(2,1)S(1)} %pack_quarters.1), channel_id=1, replica_groups={{0,32,64,96},{4,36,68,100},{8,40,72,104},{12,44,76,108},{16,48,80,112},..., dimensions={0} | all-to-all | bytes 2359296 | tf_op jit(solution)/shard_map/all_to_all | solution.py:86
  66.0 18.3 %all_to_all.21.pieces = bf16[8,80,256]{2,1,0:T(8,128)(2,1)S(1)} all-to-all(bf16[8,80,256]{2,1,0:T(8,128)(2,1)S(1)} %sum_over_y.1), channel_id=1, replica_groups={{0,4,8,12,16,20,24,28},{32,36,40,44,48,52,56,60},{64,68,72,76,80,84,88,..., dimensions={0} | all-to-all | bytes 655360 | tf_op jit(solution)/shard_map/all_to_all | solution.py:86
  85.1 3.4 %all-to-all-start.2 = ((bf16[8,80,256]{2,1,0:T(8,128)(2,1)}), bf16[8,80,256]{2,1,0:T(8,128)(2,1)S(1)}, u32[]{:S(2)}, u32[]{:S(2)}) async-start(bf16[8,80,256]{2,1,0:T(8,128)(2,1)} %sum_over_z.1), calls=%async_computation.2 | async-start | bytes 655360 | tf_op jit(solution)/shard_map/all_to_all | solution.py:86
  88.7 10.0 %all-to-all-done.2.pieces = bf16[8,80,256]{2,1,0:T(8,128)(2,1)S(1)} async-done(((bf16[8,80,256]{2,1,0:T(8,128)(2,1)}), bf16[8,80,256]{2,1,0:T(8,128)(2,1)S(1)}, u32[]{:S(2)}, u32[]{:S(2)}) %all-to-all-start.2) | async-done | bytes 327712 | tf_op jit(solution)/shard_map/all_to_all | solution.py:86
  101.7 4.5 %all-to-all-start.3 = ((bf16[4,512,256]{2,1,0:T(8,128)(2,1)}), bf16[4,512,256]{2,1,0:T(8,128)(2,1)}, u32[]{:S(2)}, u32[]{:S(2)}) async-start(bf16[4,512,256]{2,1,0:T(8,128)(2,1)} %get-tuple-element.51), calls=%async_computation.3 | async-start | bytes 2097152 | tf_op jit(solution)/shard_map/all_to_all | solution.py:86
  106.4 7.8 %inverse_factor.1 = f32[256,256]{1,0:T(8,128)S(1)} custom-call(f32[256,256]{1,0:T(8,128)S(1)} %bitcast.47), custom_call_target="tpu_custom_call" | custom-call | flops 8000000000 | bytes 1048576 | tf_op jit(solution)/shard_map/inverse_factor/pallas_call | solution.py:245
  114.2 3.5 %all-to-all-done.3 = bf16[4,512,256]{2,1,0:T(8,128)(2,1)} async-done(((bf16[4,512,256]{2,1,0:T(8,128)(2,1)}), bf16[4,512,256]{2,1,0:T(8,128)(2,1)}, u32[]{:S(2)}, u32[]{:S(2)}) %all-to-all-start.3) | async-done | bytes 1048608 | tf_op jit(solution)/shard_map/all_to_all | solution.py:86
  117.7 1.8 %multiply_reduce_fusion = (f32[256]{0:T(256)S(1)}, bf16[2048,256]{1,0:T(8,128)(2,1)S(1)}) fusion(bf16[2048,256]{1,0:T(8,128)(2,1)} %bitcast.14, f32[256,256]{1,0:T(8,128)S(1)} %inverse_factor.1), kind=kOutput, calls=%fused_computation.14 | convolution fusion | flops 270073600 | bytes 2360320 | tf_op jit(solution)/shard_map/dot_general | solution.py:359
  119.6 5.9 %collective-permute-start.19 = (bf16[2048,256]{1,0:T(8,128)(2,1)S(1)}, bf16[2048,256]{1,0:T(8,128)(2,1)S(1)}, u32[]{:S(2)}, u32[]{:S(2)}) collective-permute-start(bf16[2048,256]{1,0:T(8,128)(2,1)S(1)} %get-tuple-element.63), channel_id=1, source_target_pairs={{0,128},{128,0},{1,129},{129,1},{2,130},{130,2},{3,131},{131,3},{4... | collective-permute-start | bytes 3145736 | tf_op jit(solution)/shard_map/ppermute | solution.py:53
  130.9 1.9 %collective-permute-start.20 = (f32[1,256]{1,0:T(1,128)S(1)}, f32[1,256]{1,0:T(1,128)S(1)}, u32[]{:S(2)}, u32[]{:S(2)}) collective-permute-start(f32[1,256]{1,0:T(1,128)S(1)} %rsqrt_multiply_fusion), channel_id=1, source_target_pairs={{0,128},{128,0},{1,129},{129,1},{2,130},{130,2},{3,131},{131,3},{4... | collective-permute-start | bytes 3080 | tf_op jit(solution)/shard_map/ppermute | solution.py:53
  134.4 1.5 %convolution_convert_fusion = bf16[256,2048]{1,0:T(8,128)(2,1)} fusion(bf16[2048,256]{1,0:T(8,128)(2,1)S(1)} %collective-permute-done.19, bf16[2048,256]{1,0:T(8,128)(2,1)S(1)} %get-tuple-element.63, pred[]{:T(512)S(6)} %eq.12, f32[256]{0:T(256)S(1)} %bitcast.53, f32[256,256]{1,0:T(8,128)S(1)} %collective-permute-done.15, f32[256,256]{1,0:T(8,128)S(1)} %fusion.15), kind=kOutput, calls=%fused_computation.6 | convolution fusion | flops 269680640 | bytes 3671041 | tf_op jit(solution)/shard_map/dot_general | solution.py:378
  135.9 1.5 %convolution_convert_fusion.1 = bf16[256,2048]{1,0:T(8,128)(2,1)} fusion(bf16[2048,256]{1,0:T(8,128)(2,1)S(1)} %get-tuple-element.63, bf16[2048,256]{1,0:T(8,128)(2,1)S(1)} %collective-permute-done.19, pred[]{:T(512)S(6)} %eq.12, f32[256]{0:T(256)S(1)} %bitcast.52, f32[256,256]{1,0:T(8,128)S(1)} %fusion.15, f32[256,256]{1,0:T(8,128)S(1)} %collective-permute-done.15), kind=kOutput, calls=%fused_computation.7 | convolution fusion | flops 269680640 | bytes 3671041 | tf_op jit(solution)/shard_map/dot_general | solution.py:378
  (81 shorter events, 20.8 us)
Async XLA Ops:
  0.6 17.6 %copy-start.3 = (bf16[2048,256]{1,0:T(8,128)(2,1)S(1)}, bf16[2048,256]{1,0:T(8,128)(2,1)}, u32[]{:S(2)}) copy-start(bf16[2048,256]{1,0:T(8,128)(2,1)} %refs_15_.1) | copy-start | bytes 3145732
  0.6 23.5 %collective-permute-start.5 = (bf16[512,256]{1,0:T(8,128)(2,1)}, bf16[512,256]{1,0:T(8,128)(2,1)S(1)}, u32[]{:S(2)}, u32[]{:S(2)}) collective-permute-start(bf16[512,256]{1,0:T(8,128)(2,1)} %refs_2_.1), channel_id=1, source_target_pairs={{0,3},{1,0},{2,1},{3,2},{4,7},{5,4},{6,5},{7,6},{8,11},{9,8},{10,9... | collective-permute-start | bytes 786440 | tf_op jit(solution)/shard_map/ppermute | solution.py:42
  4.0 8.8 %collective-permute-start = (bf16[512,256]{1,0:T(8,128)(2,1)}, bf16[512,256]{1,0:T(8,128)(2,1)S(1)}, u32[]{:S(2)}, u32[]{:S(2)}) collective-permute-start(bf16[512,256]{1,0:T(8,128)(2,1)} %refs_2_.1), channel_id=1, source_target_pairs={{0,1},{1,2},{2,3},{3,0},{4,5},{5,6},{6,7},{7,4},{8,9},{9,10},{10,1... | collective-permute-start | bytes 786440 | tf_op jit(solution)/shard_map/ppermute | solution.py:42
  4.0 20.1 %collective-permute-start.4 = (bf16[512,256]{1,0:T(8,128)(2,1)}, bf16[512,256]{1,0:T(8,128)(2,1)S(1)}, u32[]{:S(2)}, u32[]{:S(2)}) collective-permute-start(bf16[512,256]{1,0:T(8,128)(2,1)} %refs_3_.1), channel_id=1, source_target_pairs={{0,1},{1,2},{2,3},{3,0},{4,5},{5,6},{6,7},{7,4},{8,9},{9,10},{10,1... | collective-permute-start | bytes 786440 | tf_op jit(solution)/shard_map/ppermute | solution.py:42
  4.2 10.7 %collective-permute-start.2 = (bf16[512,256]{1,0:T(8,128)(2,1)}, bf16[512,256]{1,0:T(8,128)(2,1)S(1)}, u32[]{:S(2)}, u32[]{:S(2)}) collective-permute-start(bf16[512,256]{1,0:T(8,128)(2,1)} %refs_3_.1), channel_id=1, source_target_pairs={{0,3},{1,0},{2,1},{3,2},{4,7},{5,4},{6,5},{7,6},{8,11},{9,8},{10,9... | collective-permute-start | bytes 786440 | tf_op jit(solution)/shard_map/ppermute | solution.py:42
  14.9 11.0 %collective-permute-start.1 = (bf16[512,256]{1,0:T(8,128)(2,1)S(1)}, bf16[512,256]{1,0:T(8,128)(2,1)S(1)}, u32[]{:S(2)}, u32[]{:S(2)}) collective-permute-start(bf16[512,256]{1,0:T(8,128)(2,1)S(1)} %collective-permute-done.refs_2_.refs_4_), channel_id=1, source_target_pairs={{0,1},{1,2},{2,3},{3,0},{4,5},{5,6},{6,7},{7,4},{8,9},{9,10},{10,1... | collective-permute-start | bytes 786440 | tf_op jit(solution)/shard_map/ppermute | solution.py:42
  15.8 10.2 %collective-permute-start.3 = (bf16[512,256]{1,0:T(8,128)(2,1)S(1)}, bf16[512,256]{1,0:T(8,128)(2,1)S(1)}, u32[]{:S(2)}, u32[]{:S(2)}) collective-permute-start(bf16[512,256]{1,0:T(8,128)(2,1)S(1)} %collective-permute-done.2.refs_5_.refs_7_), channel_id=1, source_target_pairs={{0,3},{1,0},{2,1},{3,2},{4,7},{5,4},{6,5},{7,6},{8,11},{9,8},{10,9... | collective-permute-start | bytes 786440 | tf_op jit(solution)/shard_map/ppermute | solution.py:42
  26.9 2.9 %collective-permute-start.6 = (bf16[256,256]{1,0:T(8,128)(2,1)S(1)}, bf16[256,256]{1,0:T(8,128)(2,1)S(1)}, u32[]{:S(2)}, u32[]{:S(2)}) collective-permute-start(bf16[256,256]{1,0:T(8,128)(2,1)S(1)} %get-tuple-element.36), channel_id=1, source_target_pairs={{0,128},{128,0},{1,129},{129,1},{2,130},{130,2},{3,131},{131,3},{4... | collective-permute-start | bytes 393224 | tf_op jit(solution)/shard_map/ppermute | solution.py:53
  29.8 7.4 %collective-permute-start.9 = (bf16[256,256]{1,0:T(8,128)(2,1)S(1)}, bf16[256,256]{1,0:T(8,128)(2,1)S(1)}, u32[]{:S(2)}, u32[]{:S(2)}) collective-permute-start(bf16[256,256]{1,0:T(8,128)(2,1)S(1)} %add_convert_fusion), channel_id=1, source_target_pairs={{0,3},{1,0},{2,1},{3,2},{4,7},{5,4},{6,5},{7,6},{8,11},{9,8},{10,9... | collective-permute-start | bytes 393224 | tf_op jit(solution)/shard_map/ppermute | solution.py:42
  31.6 6.0 %collective-permute-start.8 = (bf16[256,256]{1,0:T(8,128)(2,1)S(1)}, bf16[256,256]{1,0:T(8,128)(2,1)S(1)}, u32[]{:S(2)}, u32[]{:S(2)}) collective-permute-start(bf16[256,256]{1,0:T(8,128)(2,1)S(1)} %add_convert_fusion), channel_id=1, source_target_pairs={{0,2},{1,3},{2,0},{3,1},{4,6},{5,7},{6,4},{7,5},{8,10},{9,11},{10,... | collective-permute-start | bytes 393224 | tf_op jit(solution)/shard_map/ppermute | solution.py:42
  31.6 9.1 %collective-permute-start.7 = (bf16[256,256]{1,0:T(8,128)(2,1)S(1)}, bf16[256,256]{1,0:T(8,128)(2,1)S(1)}, u32[]{:S(2)}, u32[]{:S(2)}) collective-permute-start(bf16[256,256]{1,0:T(8,128)(2,1)S(1)} %add_convert_fusion), channel_id=1, source_target_pairs={{0,1},{1,2},{2,3},{3,0},{4,5},{5,6},{6,7},{7,4},{8,9},{9,10},{10,1... | collective-permute-start | bytes 393224 | tf_op jit(solution)/shard_map/ppermute | solution.py:42
  40.8 1.9 %collective-permute-start.10 = (bf16[256,256]{1,0:T(8,128)(2,1)S(1)}, bf16[256,256]{1,0:T(8,128)(2,1)S(1)}, u32[]{:S(2)}, u32[]{:S(2)}) collective-permute-start(bf16[256,256]{1,0:T(8,128)(2,1)S(1)} %get-tuple-element.49), channel_id=1, source_target_pairs={{0,128},{128,0},{1,129},{129,1},{2,130},{130,2},{3,131},{131,3},{4... | collective-permute-start | bytes 393224 | tf_op jit(solution)/shard_map/ppermute | solution.py:53
  43.2 2.7 %collective-permute-start.11 = (bf16[2048,256]{1,0:T(8,128)(2,1)S(1)}, bf16[2048,256]{1,0:T(8,128)(2,1)S(1)}, u32[]{:S(2)}, u32[]{:S(2)}) collective-permute-start(bf16[2048,256]{1,0:T(8,128)(2,1)S(1)} %convolution_convert_fusion.2), channel_id=1, source_target_pairs={{0,128},{128,0},{1,129},{129,1},{2,130},{130,2},{3,131},{131,3},{4... | collective-permute-start | bytes 3145736 | tf_op jit(solution)/shard_map/ppermute | solution.py:53
  85.1 13.5 %all-to-all-start.2 = ((bf16[8,80,256]{2,1,0:T(8,128)(2,1)}), bf16[8,80,256]{2,1,0:T(8,128)(2,1)S(1)}, u32[]{:S(2)}, u32[]{:S(2)}) async-start(bf16[8,80,256]{2,1,0:T(8,128)(2,1)} %sum_over_z.1), calls=%async_computation.2 | async-start | bytes 655360 | tf_op jit(solution)/shard_map/all_to_all | solution.py:86
  99.7 6.7 %collective-permute-start.14 = (f32[64,256]{1,0:T(8,128)S(1)}, f32[64,256]{1,0:T(8,128)S(1)}, u32[]{:S(2)}, u32[]{:S(2)}) collective-permute-start(f32[64,256]{1,0:T(8,128)S(1)} %get-tuple-element.50), channel_id=1, source_target_pairs={{0,96},{4,100},{8,104},{12,108},{16,112},{20,116},{24,120},{28,124... | collective-permute-start | bytes 196616 | tf_op jit(solution)/shard_map/ppermute | solution.py:49
  100.6 5.7 %collective-permute-start.13 = (f32[64,256]{1,0:T(8,128)S(1)}, f32[64,256]{1,0:T(8,128)S(1)}, u32[]{:S(2)}, u32[]{:S(2)}) collective-permute-start(f32[64,256]{1,0:T(8,128)S(1)} %get-tuple-element.50), channel_id=1, source_target_pairs={{0,64},{4,68},{8,72},{12,76},{16,80},{20,84},{24,88},{28,92},{32,9... | collective-permute-start | bytes 196616 | tf_op jit(solution)/shard_map/ppermute | solution.py:49
  101.7 4.5 %collective-permute-start.12 = (f32[64,256]{1,0:T(8,128)S(1)}, f32[64,256]{1,0:T(8,128)S(1)}, u32[]{:S(2)}, u32[]{:S(2)}) collective-permute-start(f32[64,256]{1,0:T(8,128)S(1)} %get-tuple-element.50), channel_id=1, source_target_pairs={{0,32},{4,36},{8,40},{12,44},{16,48},{20,52},{24,56},{28,60},{32,6... | collective-permute-start | bytes 196616 | tf_op jit(solution)/shard_map/ppermute | solution.py:49
  101.7 16.0 %all-to-all-start.3 = ((bf16[4,512,256]{2,1,0:T(8,128)(2,1)}), bf16[4,512,256]{2,1,0:T(8,128)(2,1)}, u32[]{:S(2)}, u32[]{:S(2)}) async-start(bf16[4,512,256]{2,1,0:T(8,128)(2,1)} %get-tuple-element.51), calls=%async_computation.3 | async-start | bytes 2097152 | tf_op jit(solution)/shard_map/all_to_all | solution.py:86
  119.6 8.6 %collective-permute-start.19 = (bf16[2048,256]{1,0:T(8,128)(2,1)S(1)}, bf16[2048,256]{1,0:T(8,128)(2,1)S(1)}, u32[]{:S(2)}, u32[]{:S(2)}) collective-permute-start(bf16[2048,256]{1,0:T(8,128)(2,1)S(1)} %get-tuple-element.63), channel_id=1, source_target_pairs={{0,128},{128,0},{1,129},{129,1},{2,130},{130,2},{3,131},{131,3},{4... | collective-permute-start | bytes 3145736 | tf_op jit(solution)/shard_map/ppermute | solution.py:53
  125.9 2.2 %collective-permute-start.15 = (f32[256,256]{1,0:T(8,128)S(1)}, f32[256,256]{1,0:T(8,128)S(1)}, u32[]{:S(2)}, u32[]{:S(2)}) collective-permute-start(f32[256,256]{1,0:T(8,128)S(1)} %fusion.15), channel_id=1, source_target_pairs={{0,128},{128,0},{1,129},{129,1},{2,130},{130,2},{3,131},{131,3},{4... | collective-permute-start | bytes 786440 | tf_op jit(solution)/shard_map/ppermute | solution.py:53
  126.0 3.6 %collective-permute-start.18 = (f32[1,256]{1,0:T(1,128)S(1)}, f32[1,256]{1,0:T(1,128)S(1)}, u32[]{:S(2)}, u32[]{:S(2)}) collective-permute-start(f32[1,256]{1,0:T(1,128)S(1)} %bitcast.54), channel_id=1, source_target_pairs={{0,3},{1,0},{2,1},{3,2},{4,7},{5,4},{6,5},{7,6},{8,11},{9,8},{10,9... | collective-permute-start | bytes 3080 | tf_op jit(solution)/shard_map/ppermute | solution.py:42
  126.7 3.9 %collective-permute-start.17 = (f32[1,256]{1,0:T(1,128)S(1)}, f32[1,256]{1,0:T(1,128)S(1)}, u32[]{:S(2)}, u32[]{:S(2)}) collective-permute-start(f32[1,256]{1,0:T(1,128)S(1)} %bitcast.55), channel_id=1, source_target_pairs={{0,2},{1,3},{2,0},{3,1},{4,6},{5,7},{6,4},{7,5},{8,10},{9,11},{10,... | collective-permute-start | bytes 3080 | tf_op jit(solution)/shard_map/ppermute | solution.py:42
  126.7 4.2 %collective-permute-start.16 = (f32[1,256]{1,0:T(1,128)S(1)}, f32[1,256]{1,0:T(1,128)S(1)}, u32[]{:S(2)}, u32[]{:S(2)}) collective-permute-start(f32[1,256]{1,0:T(1,128)S(1)} %bitcast.56), channel_id=1, source_target_pairs={{0,1},{1,2},{2,3},{3,0},{4,5},{5,6},{6,7},{7,4},{8,9},{9,10},{10,1... | collective-permute-start | bytes 3080 | tf_op jit(solution)/shard_map/ppermute | solution.py:42
  130.9 3.4 %collective-permute-start.20 = (f32[1,256]{1,0:T(1,128)S(1)}, f32[1,256]{1,0:T(1,128)S(1)}, u32[]{:S(2)}, u32[]{:S(2)}) collective-permute-start(f32[1,256]{1,0:T(1,128)S(1)} %rsqrt_multiply_fusion), channel_id=1, source_target_pairs={{0,128},{128,0},{1,129},{129,1},{2,130},{130,2},{3,131},{131,3},{4... | collective-permute-start | bytes 3080 | tf_op jit(solution)/shard_map/ppermute | solution.py:53
  (11 other events, 111.1 us)

commit v8 on v7

--- a/solution.py
+++ b/solution.py
@@ -353,6 +353,7 @@
     gram = in_order(from_all(gram, shift_y), y)
     inverse = inverse_factor(gram)
     ortho = jnp.dot(power, inverse.T, precision=lax.Precision.HIGHEST)
+    inverse, ortho = lax.optimization_barrier((inverse, ortho))
     orthos = split([ortho, swap_cores(ortho)])
     raw = exchange(raw, Y_GROUPS).reshape(-1, width)
 

time: 138 us -> 137 us (level)
  no operation moved by 1% of the time
where the time goes in v8:
time: 137 us
  blocking collectives  38 us (28%)
  starting transfers between devices  34.7 us (25%)
  matrix products  26.5 us (19%)
  waiting for transfers between devices  22.9 us (17%)
  Pallas kernels  13.3 us (10%)
    all_to_all x2, blocking collectives, exchange(): return lax.all_to_all(x, 'fsdp', 0, 0, axis_index_groups=groups)  38 us
    ppermute x12, starting transfers between devices, shift_tp(): return lax.ppermute(x, 'tp', [(i, (i + by) % N_TP) for i in range(N_TP)])  13.5 us
    all_to_all x2, waiting for transfers between devices, exchange(): return lax.all_to_all(x, 'fsdp', 0, 0, axis_index_groups=groups)  13.1 us
    dot_general x2, matrix products, per_device(): product = jnp.dot(grad, bases[w], preferred_element_type=jnp.float32)  11.8 us
    ppermute x6, starting transfers between devices, swap_cores(): return lax.ppermute(x, 'rep', [(0, 1), (1, 0)])  11.2 us
    all_to_all x2, starting transfers between devices, exchange(): return lax.all_to_all(x, 'fsdp', 0, 0, axis_index_groups=groups)  7.9 us
    pallas_call x1, Pallas kernels, inverse_factor(): pl.pallas_call(inverse_kernel, out_shape=jax.ShapeDtypeStruct((RANK, RANK...  7.84 us
    dot_general x5, matrix products, contract_rows(): lax.dot_general(left, right, (((0,), (0,)), ((), ())), precision=precisio...  6.38 us
  transfers between devices with their start and end apart: 23, of which 11 were waited for; matrix products, arithmetic and copies ran while one was open for 15% of the time, Pallas kernels for 7%

profile of v8, /device:TPU:1, one launch (start us, length us, event | category | flops | bytes accessed | tf_op | source)
XLA Modules:
  0.0 136.9 jit_solution(6603729482381164331)
XLA Ops:
  0.6 3.4 %collective-permute-start.5 = (bf16[512,256]{1,0:T(8,128)(2,1)}, bf16[512,256]{1,0:T(8,128)(2,1)S(1)}, u32[]{:S(2)}, u32[]{:S(2)}) collective-permute-start(bf16[512,256]{1,0:T(8,128)(2,1)} %refs_2_.1), channel_id=1, source_target_pairs={{0,3},{1,0},{2,1},{3,2},{4,7},{5,4},{6,5},{7,6},{8,11},{9,8},{10,9... | collective-permute-start | bytes 786440 | tf_op jit(solution)/shard_map/ppermute | solution.py:42
  4.2 2.5 %collective-permute-start.2 = (bf16[512,256]{1,0:T(8,128)(2,1)}, bf16[512,256]{1,0:T(8,128)(2,1)S(1)}, u32[]{:S(2)}, u32[]{:S(2)}) collective-permute-start(bf16[512,256]{1,0:T(8,128)(2,1)} %refs_3_.1), channel_id=1, source_target_pairs={{0,3},{1,0},{2,1},{3,2},{4,7},{5,4},{6,5},{7,6},{8,11},{9,8},{10,9... | collective-permute-start | bytes 786440 | tf_op jit(solution)/shard_map/ppermute | solution.py:42
  6.7 6.0 %convolution_convert_fusion.5.refs_6_.refs_8_.refs_10_.refs_2_ = bf16[2048,256]{1,0:T(8,128)(2,1)S(1)} fusion(bf16[2048,2048]{1,0:T(8,128)(2,1)} %param.9, bf16[2048,256]{1,0:T(8,128)(2,1)} %refs_14_.1), kind=kOutput, calls=%fused_computation.11 | convolution fusion | flops 2148007936 | bytes 10485760 | tf_op jit(solution)/shard_map/dot_general | solution.py:290
  12.9 2.0 %collective-permute-done.2.refs_5_.refs_7_ = bf16[512,256]{1,0:T(8,128)(2,1)S(1)} collective-permute-done((bf16[512,256]{1,0:T(8,128)(2,1)}, bf16[512,256]{1,0:T(8,128)(2,1)S(1)}, u32[]{:S(2)}, u32[]{:S(2)}) %collective-permute-start.2) | collective-permute-done | bytes 262176 | tf_op jit(solution)/shard_map/ppermute | solution.py:42
  15.8 2.5 %collective-permute-start.3 = (bf16[512,256]{1,0:T(8,128)(2,1)S(1)}, bf16[512,256]{1,0:T(8,128)(2,1)S(1)}, u32[]{:S(2)}, u32[]{:S(2)}) collective-permute-start(bf16[512,256]{1,0:T(8,128)(2,1)S(1)} %collective-permute-done.2.refs_5_.refs_7_), channel_id=1, source_target_pairs={{0,3},{1,0},{2,1},{3,2},{4,7},{5,4},{6,5},{7,6},{8,11},{9,8},{10,9... | collective-permute-start | bytes 786440 | tf_op jit(solution)/shard_map/ppermute | solution.py:42
  18.2 5.9 %convolution_convert_fusion.4.refs_7_.refs_9_.refs_11_.refs_3_ = bf16[2048,256]{1,0:T(8,128)(2,1)S(1)} fusion(bf16[2048,2048]{1,0:T(8,128)(2,1)} %param.11, bf16[2048,256]{1,0:T(8,128)(2,1)S(1)} %copy-done.3), kind=kOutput, calls=%fused_computation.10 | convolution fusion | flops 2148007936 | bytes 10485760 | tf_op jit(solution)/shard_map/dot_general | solution.py:290
  24.2 1.7 %near_tokens.1 = (f32[256,256]{1,0:T(8,128)S(1)}, f32[256,256]{1,0:T(8,128)S(1)}) custom-call(s32[5]{0:T(128)S(1)} %stack.23.index, bf16[512,256]{1,0:T(8,128)(2,1)S(1)} %copy-done.4, bf16[512,256]{1,0:T(8,128)(2,1)S(1)} %copy-done.5, bf16[512,256]{1,0:T(8,128)(2,1)S(1)} %collective-permute-done.refs_2_.refs_4_, ...), custom_call_target="tpu_custom_call" | custom-call | flops 1048576 | bytes 1048576 | tf_op jit(solution)/shard_map/near_tokens/pallas_call | solution.py:130
  26.9 1.9 %collective-permute-start.6 = (bf16[256,256]{1,0:T(8,128)(2,1)S(1)}, bf16[256,256]{1,0:T(8,128)(2,1)S(1)}, u32[]{:S(2)}, u32[]{:S(2)}) collective-permute-start(bf16[256,256]{1,0:T(8,128)(2,1)S(1)} %get-tuple-element.38), channel_id=1, source_target_pairs={{0,128},{128,0},{1,129},{129,1},{2,130},{130,2},{3,131},{131,3},{4... | collective-permute-start | bytes 393224 | tf_op jit(solution)/shard_map/ppermute | solution.py:53
  29.8 1.8 %collective-permute-start.9 = (bf16[256,256]{1,0:T(8,128)(2,1)S(1)}, bf16[256,256]{1,0:T(8,128)(2,1)S(1)}, u32[]{:S(2)}, u32[]{:S(2)}) collective-permute-start(bf16[256,256]{1,0:T(8,128)(2,1)S(1)} %add_convert_fusion), channel_id=1, source_target_pairs={{0,3},{1,0},{2,1},{3,2},{4,7},{5,4},{6,5},{7,6},{8,11},{9,8},{10,9... | collective-permute-start | bytes 393224 | tf_op jit(solution)/shard_map/ppermute | solution.py:42
  32.5 2.3 %fusion = bf16[256,2048]{1,0:T(8,128)(2,1)S(1)} fusion(bf16[2048,256]{1,0:T(8,128)(2,1)S(1)} %bitcast.46, bf16[2048,2048]{1,0:T(8,128)(2,1)S(1)} %bitcast.49, bf16[1,256,2048]{2,1,0:T(8,128)(2,1)S(1)} %copy-done), kind=kOutput, calls=%fused_computation.4 | convolution fusion | flops 2149056512 | bytes 11534336 | tf_op jit(solution)/shard_map/dot_general | solution.py:27
  34.9 2.3 %fusion.1 = bf16[256,2048]{1,0:T(8,128)(2,1)S(1)} fusion(bf16[2048,256]{1,0:T(8,128)(2,1)S(1)} %bitcast.45, bf16[2048,2048]{1,0:T(8,128)(2,1)S(1)} %bitcast.51, bf16[1,256,2048]{2,1,0:T(8,128)(2,1)S(1)} %copy-done.1), kind=kOutput, calls=%fused_computation.5 | convolution fusion | flops 2149056512 | bytes 11534336 | tf_op jit(solution)/shard_map/dot_general | solution.py:27
  37.6 3.1 %collective-permute-done.7 = bf16[256,256]{1,0:T(8,128)(2,1)S(1)} collective-permute-done((bf16[256,256]{1,0:T(8,128)(2,1)S(1)}, bf16[256,256]{1,0:T(8,128)(2,1)S(1)}, u32[]{:S(2)}, u32[]{:S(2)}) %collective-permute-start.7) | collective-permute-done | bytes 131104 | tf_op jit(solution)/shard_map/ppermute | solution.py:42
  46.2 19.6 %all_to_all.20.pieces = bf16[4,576,256]{2,1,0:T(8,128)(2,1)S(1)} all-to-all(bf16[4,576,256]{2,1,0:T(8,128)(2,1)S(1)} %pack_quarters.1), channel_id=1, replica_groups={{0,32,64,96},{4,36,68,100},{8,40,72,104},{12,44,76,108},{16,48,80,112},..., dimensions={0} | all-to-all | bytes 2359296 | tf_op jit(solution)/shard_map/all_to_all | solution.py:86
  66.0 18.3 %all_to_all.21.pieces = bf16[8,80,256]{2,1,0:T(8,128)(2,1)S(1)} all-to-all(bf16[8,80,256]{2,1,0:T(8,128)(2,1)S(1)} %sum_over_y.1), channel_id=1, replica_groups={{0,4,8,12,16,20,24,28},{32,36,40,44,48,52,56,60},{64,68,72,76,80,84,88,..., dimensions={0} | all-to-all | bytes 655360 | tf_op jit(solution)/shard_map/all_to_all | solution.py:86
  85.1 3.4 %all-to-all-start.2 = ((bf16[8,80,256]{2,1,0:T(8,128)(2,1)}), bf16[8,80,256]{2,1,0:T(8,128)(2,1)S(1)}, u32[]{:S(2)}, u32[]{:S(2)}) async-start(bf16[8,80,256]{2,1,0:T(8,128)(2,1)} %sum_over_z.1), calls=%async_computation.2 | async-start | bytes 655360 | tf_op jit(solution)/shard_map/all_to_all | solution.py:86
  88.7 10.0 %all-to-all-done.2.pieces = bf16[8,80,256]{2,1,0:T(8,128)(2,1)S(1)} async-done(((bf16[8,80,256]{2,1,0:T(8,128)(2,1)}), bf16[8,80,256]{2,1,0:T(8,128)(2,1)S(1)}, u32[]{:S(2)}, u32[]{:S(2)}) %all-to-all-start.2) | async-done | bytes 327712 | tf_op jit(solution)/shard_map/all_to_all | solution.py:86
  101.7 4.5 %all-to-all-start.3 = ((bf16[4,512,256]{2,1,0:T(8,128)(2,1)}), bf16[4,512,256]{2,1,0:T(8,128)(2,1)}, u32[]{:S(2)}, u32[]{:S(2)}) async-start(bf16[4,512,256]{2,1,0:T(8,128)(2,1)} %get-tuple-element.54), calls=%async_computation.3 | async-start | bytes 2097152 | tf_op jit(solution)/shard_map/all_to_all | solution.py:86
  106.4 7.8 %inverse_factor.1 = f32[256,256]{1,0:T(8,128)S(1)} custom-call(f32[256,256]{1,0:T(8,128)S(1)} %bitcast.47), custom_call_target="tpu_custom_call" | custom-call | flops 8000000000 | bytes 1048576 | tf_op jit(solution)/shard_map/inverse_factor/pallas_call | solution.py:245
  114.6 3.1 %all-to-all-done.3 = bf16[4,512,256]{2,1,0:T(8,128)(2,1)} async-done(((bf16[4,512,256]{2,1,0:T(8,128)(2,1)}), bf16[4,512,256]{2,1,0:T(8,128)(2,1)}, u32[]{:S(2)}, u32[]{:S(2)}) %all-to-all-start.3) | async-done | bytes 1048608 | tf_op jit(solution)/shard_map/all_to_all | solution.py:86
  117.7 1.8 %multiply_reduce_fusion = (f32[256]{0:T(256)S(1)}, bf16[2048,256]{1,0:T(8,128)(2,1)S(1)}) fusion(bf16[2048,256]{1,0:T(8,128)(2,1)} %bitcast.14, f32[256,256]{1,0:T(8,128)S(1)} %inverse_factor.1), kind=kOutput, calls=%fused_computation.14 | convolution fusion | flops 270073600 | bytes 2360320 | tf_op jit(solution)/shard_map/dot_general | solution.py:360
  119.6 5.9 %collective-permute-start.19 = (bf16[2048,256]{1,0:T(8,128)(2,1)S(1)}, bf16[2048,256]{1,0:T(8,128)(2,1)S(1)}, u32[]{:S(2)}, u32[]{:S(2)}) collective-permute-start(bf16[2048,256]{1,0:T(8,128)(2,1)S(1)} %get-tuple-element.67), channel_id=1, source_target_pairs={{0,128},{128,0},{1,129},{129,1},{2,130},{130,2},{3,131},{131,3},{4... | collective-permute-start | bytes 3145736 | tf_op jit(solution)/shard_map/ppermute | solution.py:53
  130.4 1.9 %collective-permute-start.20 = (f32[1,256]{1,0:T(1,128)S(1)}, f32[1,256]{1,0:T(1,128)S(1)}, u32[]{:S(2)}, u32[]{:S(2)}) collective-permute-start(f32[1,256]{1,0:T(1,128)S(1)} %rsqrt_multiply_fusion), channel_id=1, source_target_pairs={{0,128},{128,0},{1,129},{129,1},{2,130},{130,2},{3,131},{131,3},{4... | collective-permute-start | bytes 3080 | tf_op jit(solution)/shard_map/ppermute | solution.py:53
  133.9 1.5 %convolution_convert_fusion = bf16[256,2048]{1,0:T(8,128)(2,1)} fusion(bf16[2048,256]{1,0:T(8,128)(2,1)S(1)} %collective-permute-done.19, bf16[2048,256]{1,0:T(8,128)(2,1)S(1)} %get-tuple-element.67, pred[]{:T(512)S(6)} %eq.12, f32[256]{0:T(256)S(1)} %bitcast.53, f32[256,256]{1,0:T(8,128)S(1)} %collective-permute-done.15, f32[256,256]{1,0:T(8,128)S(1)} %fusion.15), kind=kOutput, calls=%fused_computation.6 | convolution fusion | flops 269680640 | bytes 3671041 | tf_op jit(solution)/shard_map/dot_general | solution.py:379
  135.4 1.5 %convolution_convert_fusion.1 = bf16[256,2048]{1,0:T(8,128)(2,1)} fusion(bf16[2048,256]{1,0:T(8,128)(2,1)S(1)} %get-tuple-element.67, bf16[2048,256]{1,0:T(8,128)(2,1)S(1)} %collective-permute-done.19, pred[]{:T(512)S(6)} %eq.12, f32[256]{0:T(256)S(1)} %bitcast.52, f32[256,256]{1,0:T(8,128)S(1)} %fusion.15, f32[256,256]{1,0:T(8,128)S(1)} %collective-permute-done.15), kind=kOutput, calls=%fused_computation.7 | convolution fusion | flops 269680640 | bytes 3671041 | tf_op jit(solution)/shard_map/dot_general | solution.py:379
  (81 shorter events, 20.7 us)
Async XLA Ops:
  0.6 17.6 %copy-start.3 = (bf16[2048,256]{1,0:T(8,128)(2,1)S(1)}, bf16[2048,256]{1,0:T(8,128)(2,1)}, u32[]{:S(2)}) copy-start(bf16[2048,256]{1,0:T(8,128)(2,1)} %refs_15_.1) | copy-start | bytes 3145732
  0.6 23.5 %collective-permute-start.5 = (bf16[512,256]{1,0:T(8,128)(2,1)}, bf16[512,256]{1,0:T(8,128)(2,1)S(1)}, u32[]{:S(2)}, u32[]{:S(2)}) collective-permute-start(bf16[512,256]{1,0:T(8,128)(2,1)} %refs_2_.1), channel_id=1, source_target_pairs={{0,3},{1,0},{2,1},{3,2},{4,7},{5,4},{6,5},{7,6},{8,11},{9,8},{10,9... | collective-permute-start | bytes 786440 | tf_op jit(solution)/shard_map/ppermute | solution.py:42
  4.0 8.8 %collective-permute-start = (bf16[512,256]{1,0:T(8,128)(2,1)}, bf16[512,256]{1,0:T(8,128)(2,1)S(1)}, u32[]{:S(2)}, u32[]{:S(2)}) collective-permute-start(bf16[512,256]{1,0:T(8,128)(2,1)} %refs_2_.1), channel_id=1, source_target_pairs={{0,1},{1,2},{2,3},{3,0},{4,5},{5,6},{6,7},{7,4},{8,9},{9,10},{10,1... | collective-permute-start | bytes 786440 | tf_op jit(solution)/shard_map/ppermute | solution.py:42
  4.0 20.1 %collective-permute-start.4 = (bf16[512,256]{1,0:T(8,128)(2,1)}, bf16[512,256]{1,0:T(8,128)(2,1)S(1)}, u32[]{:S(2)}, u32[]{:S(2)}) collective-permute-start(bf16[512,256]{1,0:T(8,128)(2,1)} %refs_3_.1), channel_id=1, source_target_pairs={{0,1},{1,2},{2,3},{3,0},{4,5},{5,6},{6,7},{7,4},{8,9},{9,10},{10,1... | collective-permute-start | bytes 786440 | tf_op jit(solution)/shard_map/ppermute | solution.py:42
  4.2 10.7 %collective-permute-start.2 = (bf16[512,256]{1,0:T(8,128)(2,1)}, bf16[512,256]{1,0:T(8,128)(2,1)S(1)}, u32[]{:S(2)}, u32[]{:S(2)}) collective-permute-start(bf16[512,256]{1,0:T(8,128)(2,1)} %refs_3_.1), channel_id=1, source_target_pairs={{0,3},{1,0},{2,1},{3,2},{4,7},{5,4},{6,5},{7,6},{8,11},{9,8},{10,9... | collective-permute-start | bytes 786440 | tf_op jit(solution)/shard_map/ppermute | solution.py:42
  14.9 11.0 %collective-permute-start.1 = (bf16[512,256]{1,0:T(8,128)(2,1)S(1)}, bf16[512,256]{1,0:T(8,128)(2,1)S(1)}, u32[]{:S(2)}, u32[]{:S(2)}) collective-permute-start(bf16[512,256]{1,0:T(8,128)(2,1)S(1)} %collective-permute-done.refs_2_.refs_4_), channel_id=1, source_target_pairs={{0,1},{1,2},{2,3},{3,0},{4,5},{5,6},{6,7},{7,4},{8,9},{9,10},{10,1... | collective-permute-start | bytes 786440 | tf_op jit(solution)/shard_map/ppermute | solution.py:42
  15.8 10.2 %collective-permute-start.3 = (bf16[512,256]{1,0:T(8,128)(2,1)S(1)}, bf16[512,256]{1,0:T(8,128)(2,1)S(1)}, u32[]{:S(2)}, u32[]{:S(2)}) collective-permute-start(bf16[512,256]{1,0:T(8,128)(2,1)S(1)} %collective-permute-done.2.refs_5_.refs_7_), channel_id=1, source_target_pairs={{0,3},{1,0},{2,1},{3,2},{4,7},{5,4},{6,5},{7,6},{8,11},{9,8},{10,9... | collective-permute-start | bytes 786440 | tf_op jit(solution)/shard_map/ppermute | solution.py:42
  26.9 2.9 %collective-permute-start.6 = (bf16[256,256]{1,0:T(8,128)(2,1)S(1)}, bf16[256,256]{1,0:T(8,128)(2,1)S(1)}, u32[]{:S(2)}, u32[]{:S(2)}) collective-permute-start(bf16[256,256]{1,0:T(8,128)(2,1)S(1)} %get-tuple-element.38), channel_id=1, source_target_pairs={{0,128},{128,0},{1,129},{129,1},{2,130},{130,2},{3,131},{131,3},{4... | collective-permute-start | bytes 393224 | tf_op jit(solution)/shard_map/ppermute | solution.py:53
  29.8 7.4 %collective-permute-start.9 = (bf16[256,256]{1,0:T(8,128)(2,1)S(1)}, bf16[256,256]{1,0:T(8,128)(2,1)S(1)}, u32[]{:S(2)}, u32[]{:S(2)}) collective-permute-start(bf16[256,256]{1,0:T(8,128)(2,1)S(1)} %add_convert_fusion), channel_id=1, source_target_pairs={{0,3},{1,0},{2,1},{3,2},{4,7},{5,4},{6,5},{7,6},{8,11},{9,8},{10,9... | collective-permute-start | bytes 393224 | tf_op jit(solution)/shard_map/ppermute | solution.py:42
  31.6 6.0 %collective-permute-start.8 = (bf16[256,256]{1,0:T(8,128)(2,1)S(1)}, bf16[256,256]{1,0:T(8,128)(2,1)S(1)}, u32[]{:S(2)}, u32[]{:S(2)}) collective-permute-start(bf16[256,256]{1,0:T(8,128)(2,1)S(1)} %add_convert_fusion), channel_id=1, source_target_pairs={{0,2},{1,3},{2,0},{3,1},{4,6},{5,7},{6,4},{7,5},{8,10},{9,11},{10,... | collective-permute-start | bytes 393224 | tf_op jit(solution)/shard_map/ppermute | solution.py:42
  31.6 9.1 %collective-permute-start.7 = (bf16[256,256]{1,0:T(8,128)(2,1)S(1)}, bf16[256,256]{1,0:T(8,128)(2,1)S(1)}, u32[]{:S(2)}, u32[]{:S(2)}) collective-permute-start(bf16[256,256]{1,0:T(8,128)(2,1)S(1)} %add_convert_fusion), channel_id=1, source_target_pairs={{0,1},{1,2},{2,3},{3,0},{4,5},{5,6},{6,7},{7,4},{8,9},{9,10},{10,1... | collective-permute-start | bytes 393224 | tf_op jit(solution)/shard_map/ppermute | solution.py:42
  40.8 1.9 %collective-permute-start.10 = (bf16[256,256]{1,0:T(8,128)(2,1)S(1)}, bf16[256,256]{1,0:T(8,128)(2,1)S(1)}, u32[]{:S(2)}, u32[]{:S(2)}) collective-permute-start(bf16[256,256]{1,0:T(8,128)(2,1)S(1)} %get-tuple-element.50), channel_id=1, source_target_pairs={{0,128},{128,0},{1,129},{129,1},{2,130},{130,2},{3,131},{131,3},{4... | collective-permute-start | bytes 393224 | tf_op jit(solution)/shard_map/ppermute | solution.py:53
  43.2 2.7 %collective-permute-start.11 = (bf16[2048,256]{1,0:T(8,128)(2,1)S(1)}, bf16[2048,256]{1,0:T(8,128)(2,1)S(1)}, u32[]{:S(2)}, u32[]{:S(2)}) collective-permute-start(bf16[2048,256]{1,0:T(8,128)(2,1)S(1)} %convolution_convert_fusion.2), channel_id=1, source_target_pairs={{0,128},{128,0},{1,129},{129,1},{2,130},{130,2},{3,131},{131,3},{4... | collective-permute-start | bytes 3145736 | tf_op jit(solution)/shard_map/ppermute | solution.py:53
  85.1 13.5 %all-to-all-start.2 = ((bf16[8,80,256]{2,1,0:T(8,128)(2,1)}), bf16[8,80,256]{2,1,0:T(8,128)(2,1)S(1)}, u32[]{:S(2)}, u32[]{:S(2)}) async-start(bf16[8,80,256]{2,1,0:T(8,128)(2,1)} %sum_over_z.1), calls=%async_computation.2 | async-start | bytes 655360 | tf_op jit(solution)/shard_map/all_to_all | solution.py:86
  99.7 6.7 %collective-permute-start.14 = (f32[64,256]{1,0:T(8,128)S(1)}, f32[64,256]{1,0:T(8,128)S(1)}, u32[]{:S(2)}, u32[]{:S(2)}) collective-permute-start(f32[64,256]{1,0:T(8,128)S(1)} %get-tuple-element.52), channel_id=1, source_target_pairs={{0,96},{4,100},{8,104},{12,108},{16,112},{20,116},{24,120},{28,124... | collective-permute-start | bytes 196616 | tf_op jit(solution)/shard_map/ppermute | solution.py:49
  100.6 5.7 %collective-permute-start.13 = (f32[64,256]{1,0:T(8,128)S(1)}, f32[64,256]{1,0:T(8,128)S(1)}, u32[]{:S(2)}, u32[]{:S(2)}) collective-permute-start(f32[64,256]{1,0:T(8,128)S(1)} %get-tuple-element.52), channel_id=1, source_target_pairs={{0,64},{4,68},{8,72},{12,76},{16,80},{20,84},{24,88},{28,92},{32,9... | collective-permute-start | bytes 196616 | tf_op jit(solution)/shard_map/ppermute | solution.py:49
  101.7 4.5 %collective-permute-start.12 = (f32[64,256]{1,0:T(8,128)S(1)}, f32[64,256]{1,0:T(8,128)S(1)}, u32[]{:S(2)}, u32[]{:S(2)}) collective-permute-start(f32[64,256]{1,0:T(8,128)S(1)} %get-tuple-element.52), channel_id=1, source_target_pairs={{0,32},{4,36},{8,40},{12,44},{16,48},{20,52},{24,56},{28,60},{32,6... | collective-permute-start | bytes 196616 | tf_op jit(solution)/shard_map/ppermute | solution.py:49
  101.7 16.0 %all-to-all-start.3 = ((bf16[4,512,256]{2,1,0:T(8,128)(2,1)}), bf16[4,512,256]{2,1,0:T(8,128)(2,1)}, u32[]{:S(2)}, u32[]{:S(2)}) async-start(bf16[4,512,256]{2,1,0:T(8,128)(2,1)} %get-tuple-element.54), calls=%async_computation.3 | async-start | bytes 2097152 | tf_op jit(solution)/shard_map/all_to_all | solution.py:86
  119.6 8.6 %collective-permute-start.19 = (bf16[2048,256]{1,0:T(8,128)(2,1)S(1)}, bf16[2048,256]{1,0:T(8,128)(2,1)S(1)}, u32[]{:S(2)}, u32[]{:S(2)}) collective-permute-start(bf16[2048,256]{1,0:T(8,128)(2,1)S(1)} %get-tuple-element.67), channel_id=1, source_target_pairs={{0,128},{128,0},{1,129},{129,1},{2,130},{130,2},{3,131},{131,3},{4... | collective-permute-start | bytes 3145736 | tf_op jit(solution)/shard_map/ppermute | solution.py:53
  125.5 2.7 %collective-permute-start.15 = (f32[256,256]{1,0:T(8,128)S(1)}, f32[256,256]{1,0:T(8,128)S(1)}, u32[]{:S(2)}, u32[]{:S(2)}) collective-permute-start(f32[256,256]{1,0:T(8,128)S(1)} %fusion.15), channel_id=1, source_target_pairs={{0,128},{128,0},{1,129},{129,1},{2,130},{130,2},{3,131},{131,3},{4... | collective-permute-start | bytes 786440 | tf_op jit(solution)/shard_map/ppermute | solution.py:53
  125.6 4.1 %collective-permute-start.18 = (f32[1,256]{1,0:T(1,128)S(1)}, f32[1,256]{1,0:T(1,128)S(1)}, u32[]{:S(2)}, u32[]{:S(2)}) collective-permute-start(f32[1,256]{1,0:T(1,128)S(1)} %bitcast.54), channel_id=1, source_target_pairs={{0,3},{1,0},{2,1},{3,2},{4,7},{5,4},{6,5},{7,6},{8,11},{9,8},{10,9... | collective-permute-start | bytes 3080 | tf_op jit(solution)/shard_map/ppermute | solution.py:42
  126.2 3.9 %collective-permute-start.17 = (f32[1,256]{1,0:T(1,128)S(1)}, f32[1,256]{1,0:T(1,128)S(1)}, u32[]{:S(2)}, u32[]{:S(2)}) collective-permute-start(f32[1,256]{1,0:T(1,128)S(1)} %bitcast.55), channel_id=1, source_target_pairs={{0,2},{1,3},{2,0},{3,1},{4,6},{5,7},{6,4},{7,5},{8,10},{9,11},{10,... | collective-permute-start | bytes 3080 | tf_op jit(solution)/shard_map/ppermute | solution.py:42
  126.2 4.2 %collective-permute-start.16 = (f32[1,256]{1,0:T(1,128)S(1)}, f32[1,256]{1,0:T(1,128)S(1)}, u32[]{:S(2)}, u32[]{:S(2)}) collective-permute-start(f32[1,256]{1,0:T(1,128)S(1)} %bitcast.56), channel_id=1, source_target_pairs={{0,1},{1,2},{2,3},{3,0},{4,5},{5,6},{6,7},{7,4},{8,9},{9,10},{10,1... | collective-permute-start | bytes 3080 | tf_op jit(solution)/shard_map/ppermute | solution.py:42
  130.4 3.4 %collective-permute-start.20 = (f32[1,256]{1,0:T(1,128)S(1)}, f32[1,256]{1,0:T(1,128)S(1)}, u32[]{:S(2)}, u32[]{:S(2)}) collective-permute-start(f32[1,256]{1,0:T(1,128)S(1)} %rsqrt_multiply_fusion), channel_id=1, source_target_pairs={{0,128},{128,0},{1,129},{129,1},{2,130},{130,2},{3,131},{131,3},{4... | collective-permute-start | bytes 3080 | tf_op jit(solution)/shard_map/ppermute | solution.py:53
  (11 other events, 111.1 us)

commit v9 on v8

--- a/solution.py
+++ b/solution.py
@@ -354,7 +354,9 @@
     inverse = inverse_factor(gram)
     ortho = jnp.dot(power, inverse.T, precision=lax.Precision.HIGHEST)
     inverse, ortho = lax.optimization_barrier((inverse, ortho))
-    orthos = split([ortho, swap_cores(ortho)])
+    orthos = [ortho, swap_cores(ortho)]
+    inverse, *orthos = lax.optimization_barrier((inverse, *orthos))
+    orthos = split(orthos)
     raw = exchange(raw, Y_GROUPS).reshape(-1, width)
 
     right = jnp.dot(raw, inverse.T.astype(jnp.bfloat16), preferred_element_type=jnp.float32)

time: 137 us -> 137 us (level)
  waiting for transfers between devices: 22.9 us -> 21 us
  starting transfers between devices: 34.7 us -> 36.2 us
    all_to_all x2, waiting for transfers between devices: 13.1 us -> 9.96 us  [exchange(): return lax.all_to_all(x, 'fsdp', 0, 0, axis_index_groups=groups)]
    ppermute x6, starting transfers between devices: 11.2 us -> 12.7 us  [swap_cores(): return lax.ppermute(x, 'rep', [(0, 1), (1, 0)])]
  transfers between devices with their start and end apart: 23 -> 23, of which waited for: 11 -> 11; matrix products, arithmetic and copies ran while one was open for 15% -> 16% of each run, Pallas kernels for 7% -> 7%
where the time goes in v9:
time: 137 us; the launch traced here: 136 us
  blocking collectives  38 us (28%)
  starting transfers between devices  36.2 us (26%)
  matrix products  26.5 us (19%)
  waiting for transfers between devices  21 us (15%)
  Pallas kernels  13.3 us (10%)
    all_to_all x2, blocking collectives, exchange(): return lax.all_to_all(x, 'fsdp', 0, 0, axis_index_groups=groups)  38 us
    ppermute x12, starting transfers between devices, shift_tp(): return lax.ppermute(x, 'tp', [(i, (i + by) % N_TP) for i in range(N_TP)])  13.6 us
    ppermute x6, starting transfers between devices, swap_cores(): return lax.ppermute(x, 'rep', [(0, 1), (1, 0)])  12.7 us
    dot_general x2, matrix products, per_device(): product = jnp.dot(grad, bases[w], preferred_element_type=jnp.float32)  11.8 us
    all_to_all x2, waiting for transfers between devices, exchange(): return lax.all_to_all(x, 'fsdp', 0, 0, axis_index_groups=groups)  9.96 us
    all_to_all x2, starting transfers between devices, exchange(): return lax.all_to_all(x, 'fsdp', 0, 0, axis_index_groups=groups)  7.9 us
    pallas_call x1, Pallas kernels, inverse_factor(): pl.pallas_call(inverse_kernel, out_shape=jax.ShapeDtypeStruct((RANK, RANK...  7.84 us
    ppermute x12, waiting for transfers between devices, shift_tp(): return lax.ppermute(x, 'tp', [(i, (i + by) % N_TP) for i in range(N_TP)])  6.64 us
  transfers between devices with their start and end apart: 23, of which 11 were waited for; matrix products, arithmetic and copies ran while one was open for 16% of the time, Pallas kernels for 7%

profile of v9, /device:TPU:1, one launch (start us, length us, event | category | flops | bytes accessed | tf_op | source)
XLA Modules:
  0.0 136.5 jit_solution(6695651725699030692)
XLA Ops:
  0.6 3.4 %collective-permute-start.5 = (bf16[512,256]{1,0:T(8,128)(2,1)}, bf16[512,256]{1,0:T(8,128)(2,1)S(1)}, u32[]{:S(2)}, u32[]{:S(2)}) collective-permute-start(bf16[512,256]{1,0:T(8,128)(2,1)} %refs_2_.1), channel_id=1, source_target_pairs={{0,3},{1,0},{2,1},{3,2},{4,7},{5,4},{6,5},{7,6},{8,11},{9,8},{10,9... | collective-permute-start | bytes 786440 | tf_op jit(solution)/shard_map/ppermute | solution.py:42
  4.2 2.5 %collective-permute-start.2 = (bf16[512,256]{1,0:T(8,128)(2,1)}, bf16[512,256]{1,0:T(8,128)(2,1)S(1)}, u32[]{:S(2)}, u32[]{:S(2)}) collective-permute-start(bf16[512,256]{1,0:T(8,128)(2,1)} %refs_3_.1), channel_id=1, source_target_pairs={{0,3},{1,0},{2,1},{3,2},{4,7},{5,4},{6,5},{7,6},{8,11},{9,8},{10,9... | collective-permute-start | bytes 786440 | tf_op jit(solution)/shard_map/ppermute | solution.py:42
  6.7 6.0 %convolution_convert_fusion.5.refs_6_.refs_8_.refs_10_.refs_2_ = bf16[2048,256]{1,0:T(8,128)(2,1)S(1)} fusion(bf16[2048,2048]{1,0:T(8,128)(2,1)} %param.9, bf16[2048,256]{1,0:T(8,128)(2,1)} %refs_14_.1), kind=kOutput, calls=%fused_computation.11 | convolution fusion | flops 2148007936 | bytes 10485760 | tf_op jit(solution)/shard_map/dot_general | solution.py:290
  12.9 2.0 %collective-permute-done.2.refs_5_.refs_7_ = bf16[512,256]{1,0:T(8,128)(2,1)S(1)} collective-permute-done((bf16[512,256]{1,0:T(8,128)(2,1)}, bf16[512,256]{1,0:T(8,128)(2,1)S(1)}, u32[]{:S(2)}, u32[]{:S(2)}) %collective-permute-start.2) | collective-permute-done | bytes 262176 | tf_op jit(solution)/shard_map/ppermute | solution.py:42
  15.8 2.5 %collective-permute-start.3 = (bf16[512,256]{1,0:T(8,128)(2,1)S(1)}, bf16[512,256]{1,0:T(8,128)(2,1)S(1)}, u32[]{:S(2)}, u32[]{:S(2)}) collective-permute-start(bf16[512,256]{1,0:T(8,128)(2,1)S(1)} %collective-permute-done.2.refs_5_.refs_7_), channel_id=1, source_target_pairs={{0,3},{1,0},{2,1},{3,2},{4,7},{5,4},{6,5},{7,6},{8,11},{9,8},{10,9... | collective-permute-start | bytes 786440 | tf_op jit(solution)/shard_map/ppermute | solution.py:42
  18.2 5.9 %convolution_convert_fusion.4.refs_7_.refs_9_.refs_11_.refs_3_ = bf16[2048,256]{1,0:T(8,128)(2,1)S(1)} fusion(bf16[2048,2048]{1,0:T(8,128)(2,1)} %param.11, bf16[2048,256]{1,0:T(8,128)(2,1)S(1)} %copy-done.3), kind=kOutput, calls=%fused_computation.10 | convolution fusion | flops 2148007936 | bytes 10485760 | tf_op jit(solution)/shard_map/dot_general | solution.py:290
  24.2 1.7 %near_tokens.1 = (f32[256,256]{1,0:T(8,128)S(1)}, f32[256,256]{1,0:T(8,128)S(1)}) custom-call(s32[5]{0:T(128)S(1)} %stack.23.index, bf16[512,256]{1,0:T(8,128)(2,1)S(1)} %copy-done.4, bf16[512,256]{1,0:T(8,128)(2,1)S(1)} %copy-done.5, bf16[512,256]{1,0:T(8,128)(2,1)S(1)} %collective-permute-done.refs_2_.refs_4_, ...), custom_call_target="tpu_custom_call" | custom-call | flops 1048576 | bytes 1048576 | tf_op jit(solution)/shard_map/near_tokens/pallas_call | solution.py:130
  26.9 1.9 %collective-permute-start.6 = (bf16[256,256]{1,0:T(8,128)(2,1)S(1)}, bf16[256,256]{1,0:T(8,128)(2,1)S(1)}, u32[]{:S(2)}, u32[]{:S(2)}) collective-permute-start(bf16[256,256]{1,0:T(8,128)(2,1)S(1)} %get-tuple-element.41), channel_id=1, source_target_pairs={{0,128},{128,0},{1,129},{129,1},{2,130},{130,2},{3,131},{131,3},{4... | collective-permute-start | bytes 393224 | tf_op jit(solution)/shard_map/ppermute | solution.py:53
  29.8 1.8 %collective-permute-start.9 = (bf16[256,256]{1,0:T(8,128)(2,1)S(1)}, bf16[256,256]{1,0:T(8,128)(2,1)S(1)}, u32[]{:S(2)}, u32[]{:S(2)}) collective-permute-start(bf16[256,256]{1,0:T(8,128)(2,1)S(1)} %add_convert_fusion), channel_id=1, source_target_pairs={{0,3},{1,0},{2,1},{3,2},{4,7},{5,4},{6,5},{7,6},{8,11},{9,8},{10,9... | collective-permute-start | bytes 393224 | tf_op jit(solution)/shard_map/ppermute | solution.py:42
  32.5 2.3 %fusion = bf16[256,2048]{1,0:T(8,128)(2,1)S(1)} fusion(bf16[2048,256]{1,0:T(8,128)(2,1)S(1)} %bitcast.46, bf16[2048,2048]{1,0:T(8,128)(2,1)S(1)} %bitcast.49, bf16[1,256,2048]{2,1,0:T(8,128)(2,1)S(1)} %copy-done), kind=kOutput, calls=%fused_computation.4 | convolution fusion | flops 2149056512 | bytes 11534336 | tf_op jit(solution)/shard_map/dot_general | solution.py:27
  34.9 2.3 %fusion.1 = bf16[256,2048]{1,0:T(8,128)(2,1)S(1)} fusion(bf16[2048,256]{1,0:T(8,128)(2,1)S(1)} %bitcast.45, bf16[2048,2048]{1,0:T(8,128)(2,1)S(1)} %bitcast.51, bf16[1,256,2048]{2,1,0:T(8,128)(2,1)S(1)} %copy-done.1), kind=kOutput, calls=%fused_computation.5 | convolution fusion | flops 2149056512 | bytes 11534336 | tf_op jit(solution)/shard_map/dot_general | solution.py:27
  37.6 3.1 %collective-permute-done.7 = bf16[256,256]{1,0:T(8,128)(2,1)S(1)} collective-permute-done((bf16[256,256]{1,0:T(8,128)(2,1)S(1)}, bf16[256,256]{1,0:T(8,128)(2,1)S(1)}, u32[]{:S(2)}, u32[]{:S(2)}) %collective-permute-start.7) | collective-permute-done | bytes 131104 | tf_op jit(solution)/shard_map/ppermute | solution.py:42
  46.2 19.6 %all_to_all.20.pieces = bf16[4,576,256]{2,1,0:T(8,128)(2,1)S(1)} all-to-all(bf16[4,576,256]{2,1,0:T(8,128)(2,1)S(1)} %pack_quarters.1), channel_id=1, replica_groups={{0,32,64,96},{4,36,68,100},{8,40,72,104},{12,44,76,108},{16,48,80,112},..., dimensions={0} | all-to-all | bytes 2359296 | tf_op jit(solution)/shard_map/all_to_all | solution.py:86
  66.0 18.3 %all_to_all.21.pieces = bf16[8,80,256]{2,1,0:T(8,128)(2,1)S(1)} all-to-all(bf16[8,80,256]{2,1,0:T(8,128)(2,1)S(1)} %sum_over_y.1), channel_id=1, replica_groups={{0,4,8,12,16,20,24,28},{32,36,40,44,48,52,56,60},{64,68,72,76,80,84,88,..., dimensions={0} | all-to-all | bytes 655360 | tf_op jit(solution)/shard_map/all_to_all | solution.py:86
  85.1 3.4 %all-to-all-start.2 = ((bf16[8,80,256]{2,1,0:T(8,128)(2,1)}), bf16[8,80,256]{2,1,0:T(8,128)(2,1)S(1)}, u32[]{:S(2)}, u32[]{:S(2)}) async-start(bf16[8,80,256]{2,1,0:T(8,128)(2,1)} %sum_over_z.1), calls=%async_computation.2 | async-start | bytes 655360 | tf_op jit(solution)/shard_map/all_to_all | solution.py:86
  88.7 10.0 %all-to-all-done.2.pieces = bf16[8,80,256]{2,1,0:T(8,128)(2,1)S(1)} async-done(((bf16[8,80,256]{2,1,0:T(8,128)(2,1)}), bf16[8,80,256]{2,1,0:T(8,128)(2,1)S(1)}, u32[]{:S(2)}, u32[]{:S(2)}) %all-to-all-start.2) | async-done | bytes 327712 | tf_op jit(solution)/shard_map/all_to_all | solution.py:86
  101.7 4.5 %all-to-all-start.3 = ((bf16[4,512,256]{2,1,0:T(8,128)(2,1)}), bf16[4,512,256]{2,1,0:T(8,128)(2,1)}, u32[]{:S(2)}, u32[]{:S(2)}) async-start(bf16[4,512,256]{2,1,0:T(8,128)(2,1)} %get-tuple-element.60), calls=%async_computation.3 | async-start | bytes 2097152 | tf_op jit(solution)/shard_map/all_to_all | solution.py:86
  106.4 7.8 %inverse_factor.1 = f32[256,256]{1,0:T(8,128)S(1)} custom-call(f32[256,256]{1,0:T(8,128)S(1)} %bitcast.47), custom_call_target="tpu_custom_call" | custom-call | flops 8000000000 | bytes 1048576 | tf_op jit(solution)/shard_map/inverse_factor/pallas_call | solution.py:245
  114.6 7.3 %collective-permute-start.15 = (f32[256,256]{1,0:T(8,128)S(1)}, f32[256,256]{1,0:T(8,128)S(1)}, u32[]{:S(2)}, u32[]{:S(2)}) collective-permute-start(f32[256,256]{1,0:T(8,128)S(1)} %fusion.15), channel_id=1, source_target_pairs={{0,128},{128,0},{1,129},{129,1},{2,130},{130,2},{3,131},{131,3},{4... | collective-permute-start | bytes 786440 | tf_op jit(solution)/shard_map/ppermute | solution.py:53
  123.1 1.8 %multiply_reduce_fusion = (f32[256]{0:T(256)S(1)}, bf16[2048,256]{1,0:T(8,128)(2,1)S(1)}) fusion(bf16[2048,256]{1,0:T(8,128)(2,1)} %bitcast.14, f32[256,256]{1,0:T(8,128)S(1)} %inverse_factor.1), kind=kOutput, calls=%fused_computation.14 | convolution fusion | flops 270073600 | bytes 2360320 | tf_op jit(solution)/shard_map/dot_general | solution.py:362
  127.8 1.5 %fusion.2 = bf16[1,256,2048]{2,1,0:T(8,128)(2,1)} fusion(bf16[256,2048]{1,0:T(8,128)(2,1)S(1)} %copy-done.7, bf16[2048,256]{1,0:T(8,128)(2,1)S(1)} %get-tuple-element.73, bf16[2048,256]{1,0:T(8,128)(2,1)S(1)} %collective-permute-done.19, pred[]{:T(512)S(6)} %eq.12, f32[256,256]{1,0:T(8,128)S(1)} %fusion.15, f32[256,256]{1,0:T(8,128)S(1)} %collective-permute-done.15), kind=kOutput, calls=%fused_computation.16 | convolution fusion | flops 271122432 | bytes 4718593 | tf_op jit(solution)/shard_map/dot_general | solution.py:368
  130.4 1.6 %collective-permute-start.20 = (f32[1,256]{1,0:T(1,128)S(1)}, f32[1,256]{1,0:T(1,128)S(1)}, u32[]{:S(2)}, u32[]{:S(2)}) collective-permute-start(f32[1,256]{1,0:T(1,128)S(1)} %rsqrt_multiply_fusion), channel_id=1, source_target_pairs={{0,128},{128,0},{1,129},{129,1},{2,130},{130,2},{3,131},{131,3},{4... | collective-permute-start | bytes 3080 | tf_op jit(solution)/shard_map/ppermute | solution.py:53
  133.4 1.5 %convolution_convert_fusion = bf16[256,2048]{1,0:T(8,128)(2,1)} fusion(bf16[2048,256]{1,0:T(8,128)(2,1)S(1)} %collective-permute-done.19, bf16[2048,256]{1,0:T(8,128)(2,1)S(1)} %get-tuple-element.73, pred[]{:T(512)S(6)} %eq.12, f32[256]{0:T(256)S(1)} %bitcast.53, f32[256,256]{1,0:T(8,128)S(1)} %collective-permute-done.15, f32[256,256]{1,0:T(8,128)S(1)} %fusion.15), kind=kOutput, calls=%fused_computation.6 | convolution fusion | flops 269680640 | bytes 3671041 | tf_op jit(solution)/shard_map/dot_general | solution.py:381
  135.0 1.5 %convolution_convert_fusion.1 = bf16[256,2048]{1,0:T(8,128)(2,1)} fusion(bf16[2048,256]{1,0:T(8,128)(2,1)S(1)} %get-tuple-element.73, bf16[2048,256]{1,0:T(8,128)(2,1)S(1)} %collective-permute-done.19, pred[]{:T(512)S(6)} %eq.12, f32[256]{0:T(256)S(1)} %bitcast.52, f32[256,256]{1,0:T(8,128)S(1)} %fusion.15, f32[256,256]{1,0:T(8,128)S(1)} %collective-permute-done.15), kind=kOutput, calls=%fused_computation.7 | convolution fusion | flops 269680640 | bytes 3671041 | tf_op jit(solution)/shard_map/dot_general | solution.py:381
  (81 shorter events, 20.9 us)
Async XLA Ops:
  0.6 17.6 %copy-start.3 = (bf16[2048,256]{1,0:T(8,128)(2,1)S(1)}, bf16[2048,256]{1,0:T(8,128)(2,1)}, u32[]{:S(2)}) copy-start(bf16[2048,256]{1,0:T(8,128)(2,1)} %refs_15_.1) | copy-start | bytes 3145732
  0.6 23.5 %collective-permute-start.5 = (bf16[512,256]{1,0:T(8,128)(2,1)}, bf16[512,256]{1,0:T(8,128)(2,1)S(1)}, u32[]{:S(2)}, u32[]{:S(2)}) collective-permute-start(bf16[512,256]{1,0:T(8,128)(2,1)} %refs_2_.1), channel_id=1, source_target_pairs={{0,3},{1,0},{2,1},{3,2},{4,7},{5,4},{6,5},{7,6},{8,11},{9,8},{10,9... | collective-permute-start | bytes 786440 | tf_op jit(solution)/shard_map/ppermute | solution.py:42
  4.0 8.8 %collective-permute-start = (bf16[512,256]{1,0:T(8,128)(2,1)}, bf16[512,256]{1,0:T(8,128)(2,1)S(1)}, u32[]{:S(2)}, u32[]{:S(2)}) collective-permute-start(bf16[512,256]{1,0:T(8,128)(2,1)} %refs_2_.1), channel_id=1, source_target_pairs={{0,1},{1,2},{2,3},{3,0},{4,5},{5,6},{6,7},{7,4},{8,9},{9,10},{10,1... | collective-permute-start | bytes 786440 | tf_op jit(solution)/shard_map/ppermute | solution.py:42
  4.0 20.1 %collective-permute-start.4 = (bf16[512,256]{1,0:T(8,128)(2,1)}, bf16[512,256]{1,0:T(8,128)(2,1)S(1)}, u32[]{:S(2)}, u32[]{:S(2)}) collective-permute-start(bf16[512,256]{1,0:T(8,128)(2,1)} %refs_3_.1), channel_id=1, source_target_pairs={{0,1},{1,2},{2,3},{3,0},{4,5},{5,6},{6,7},{7,4},{8,9},{9,10},{10,1... | collective-permute-start | bytes 786440 | tf_op jit(solution)/shard_map/ppermute | solution.py:42
  4.2 10.7 %collective-permute-start.2 = (bf16[512,256]{1,0:T(8,128)(2,1)}, bf16[512,256]{1,0:T(8,128)(2,1)S(1)}, u32[]{:S(2)}, u32[]{:S(2)}) collective-permute-start(bf16[512,256]{1,0:T(8,128)(2,1)} %refs_3_.1), channel_id=1, source_target_pairs={{0,3},{1,0},{2,1},{3,2},{4,7},{5,4},{6,5},{7,6},{8,11},{9,8},{10,9... | collective-permute-start | bytes 786440 | tf_op jit(solution)/shard_map/ppermute | solution.py:42
  14.9 11.0 %collective-permute-start.1 = (bf16[512,256]{1,0:T(8,128)(2,1)S(1)}, bf16[512,256]{1,0:T(8,128)(2,1)S(1)}, u32[]{:S(2)}, u32[]{:S(2)}) collective-permute-start(bf16[512,256]{1,0:T(8,128)(2,1)S(1)} %collective-permute-done.refs_2_.refs_4_), channel_id=1, source_target_pairs={{0,1},{1,2},{2,3},{3,0},{4,5},{5,6},{6,7},{7,4},{8,9},{9,10},{10,1... | collective-permute-start | bytes 786440 | tf_op jit(solution)/shard_map/ppermute | solution.py:42
  15.8 10.2 %collective-permute-start.3 = (bf16[512,256]{1,0:T(8,128)(2,1)S(1)}, bf16[512,256]{1,0:T(8,128)(2,1)S(1)}, u32[]{:S(2)}, u32[]{:S(2)}) collective-permute-start(bf16[512,256]{1,0:T(8,128)(2,1)S(1)} %collective-permute-done.2.refs_5_.refs_7_), channel_id=1, source_target_pairs={{0,3},{1,0},{2,1},{3,2},{4,7},{5,4},{6,5},{7,6},{8,11},{9,8},{10,9... | collective-permute-start | bytes 786440 | tf_op jit(solution)/shard_map/ppermute | solution.py:42
  26.9 2.9 %collective-permute-start.6 = (bf16[256,256]{1,0:T(8,128)(2,1)S(1)}, bf16[256,256]{1,0:T(8,128)(2,1)S(1)}, u32[]{:S(2)}, u32[]{:S(2)}) collective-permute-start(bf16[256,256]{1,0:T(8,128)(2,1)S(1)} %get-tuple-element.41), channel_id=1, source_target_pairs={{0,128},{128,0},{1,129},{129,1},{2,130},{130,2},{3,131},{131,3},{4... | collective-permute-start | bytes 393224 | tf_op jit(solution)/shard_map/ppermute | solution.py:53
  29.8 7.4 %collective-permute-start.9 = (bf16[256,256]{1,0:T(8,128)(2,1)S(1)}, bf16[256,256]{1,0:T(8,128)(2,1)S(1)}, u32[]{:S(2)}, u32[]{:S(2)}) collective-permute-start(bf16[256,256]{1,0:T(8,128)(2,1)S(1)} %add_convert_fusion), channel_id=1, source_target_pairs={{0,3},{1,0},{2,1},{3,2},{4,7},{5,4},{6,5},{7,6},{8,11},{9,8},{10,9... | collective-permute-start | bytes 393224 | tf_op jit(solution)/shard_map/ppermute | solution.py:42
  31.6 6.0 %collective-permute-start.8 = (bf16[256,256]{1,0:T(8,128)(2,1)S(1)}, bf16[256,256]{1,0:T(8,128)(2,1)S(1)}, u32[]{:S(2)}, u32[]{:S(2)}) collective-permute-start(bf16[256,256]{1,0:T(8,128)(2,1)S(1)} %add_convert_fusion), channel_id=1, source_target_pairs={{0,2},{1,3},{2,0},{3,1},{4,6},{5,7},{6,4},{7,5},{8,10},{9,11},{10,... | collective-permute-start | bytes 393224 | tf_op jit(solution)/shard_map/ppermute | solution.py:42
  31.6 9.1 %collective-permute-start.7 = (bf16[256,256]{1,0:T(8,128)(2,1)S(1)}, bf16[256,256]{1,0:T(8,128)(2,1)S(1)}, u32[]{:S(2)}, u32[]{:S(2)}) collective-permute-start(bf16[256,256]{1,0:T(8,128)(2,1)S(1)} %add_convert_fusion), channel_id=1, source_target_pairs={{0,1},{1,2},{2,3},{3,0},{4,5},{5,6},{6,7},{7,4},{8,9},{9,10},{10,1... | collective-permute-start | bytes 393224 | tf_op jit(solution)/shard_map/ppermute | solution.py:42
  40.8 1.9 %collective-permute-start.10 = (bf16[256,256]{1,0:T(8,128)(2,1)S(1)}, bf16[256,256]{1,0:T(8,128)(2,1)S(1)}, u32[]{:S(2)}, u32[]{:S(2)}) collective-permute-start(bf16[256,256]{1,0:T(8,128)(2,1)S(1)} %get-tuple-element.53), channel_id=1, source_target_pairs={{0,128},{128,0},{1,129},{129,1},{2,130},{130,2},{3,131},{131,3},{4... | collective-permute-start | bytes 393224 | tf_op jit(solution)/shard_map/ppermute | solution.py:53
  43.2 2.7 %collective-permute-start.11 = (bf16[2048,256]{1,0:T(8,128)(2,1)S(1)}, bf16[2048,256]{1,0:T(8,128)(2,1)S(1)}, u32[]{:S(2)}, u32[]{:S(2)}) collective-permute-start(bf16[2048,256]{1,0:T(8,128)(2,1)S(1)} %convolution_convert_fusion.2), channel_id=1, source_target_pairs={{0,128},{128,0},{1,129},{129,1},{2,130},{130,2},{3,131},{131,3},{4... | collective-permute-start | bytes 3145736 | tf_op jit(solution)/shard_map/ppermute | solution.py:53
  85.1 13.5 %all-to-all-start.2 = ((bf16[8,80,256]{2,1,0:T(8,128)(2,1)}), bf16[8,80,256]{2,1,0:T(8,128)(2,1)S(1)}, u32[]{:S(2)}, u32[]{:S(2)}) async-start(bf16[8,80,256]{2,1,0:T(8,128)(2,1)} %sum_over_z.1), calls=%async_computation.2 | async-start | bytes 655360 | tf_op jit(solution)/shard_map/all_to_all | solution.py:86
  99.7 6.7 %collective-permute-start.14 = (f32[64,256]{1,0:T(8,128)S(1)}, f32[64,256]{1,0:T(8,128)S(1)}, u32[]{:S(2)}, u32[]{:S(2)}) collective-permute-start(f32[64,256]{1,0:T(8,128)S(1)} %get-tuple-element.55), channel_id=1, source_target_pairs={{0,96},{4,100},{8,104},{12,108},{16,112},{20,116},{24,120},{28,124... | collective-permute-start | bytes 196616 | tf_op jit(solution)/shard_map/ppermute | solution.py:49
  100.6 5.7 %collective-permute-start.13 = (f32[64,256]{1,0:T(8,128)S(1)}, f32[64,256]{1,0:T(8,128)S(1)}, u32[]{:S(2)}, u32[]{:S(2)}) collective-permute-start(f32[64,256]{1,0:T(8,128)S(1)} %get-tuple-element.55), channel_id=1, source_target_pairs={{0,64},{4,68},{8,72},{12,76},{16,80},{20,84},{24,88},{28,92},{32,9... | collective-permute-start | bytes 196616 | tf_op jit(solution)/shard_map/ppermute | solution.py:49
  101.7 4.5 %collective-permute-start.12 = (f32[64,256]{1,0:T(8,128)S(1)}, f32[64,256]{1,0:T(8,128)S(1)}, u32[]{:S(2)}, u32[]{:S(2)}) collective-permute-start(f32[64,256]{1,0:T(8,128)S(1)} %get-tuple-element.55), channel_id=1, source_target_pairs={{0,32},{4,36},{8,40},{12,44},{16,48},{20,52},{24,56},{28,60},{32,6... | collective-permute-start | bytes 196616 | tf_op jit(solution)/shard_map/ppermute | solution.py:49
  101.7 21.4 %all-to-all-start.3 = ((bf16[4,512,256]{2,1,0:T(8,128)(2,1)}), bf16[4,512,256]{2,1,0:T(8,128)(2,1)}, u32[]{:S(2)}, u32[]{:S(2)}) async-start(bf16[4,512,256]{2,1,0:T(8,128)(2,1)} %get-tuple-element.60), calls=%async_computation.3 | async-start | bytes 2097152 | tf_op jit(solution)/shard_map/all_to_all | solution.py:86
  114.6 8.4 %collective-permute-start.15 = (f32[256,256]{1,0:T(8,128)S(1)}, f32[256,256]{1,0:T(8,128)S(1)}, u32[]{:S(2)}, u32[]{:S(2)}) collective-permute-start(f32[256,256]{1,0:T(8,128)S(1)} %fusion.15), channel_id=1, source_target_pairs={{0,128},{128,0},{1,129},{129,1},{2,130},{130,2},{3,131},{131,3},{4... | collective-permute-start | bytes 786440 | tf_op jit(solution)/shard_map/ppermute | solution.py:53
  124.9 2.9 %collective-permute-start.19 = (bf16[2048,256]{1,0:T(8,128)(2,1)S(1)}, bf16[2048,256]{1,0:T(8,128)(2,1)S(1)}, u32[]{:S(2)}, u32[]{:S(2)}) collective-permute-start(bf16[2048,256]{1,0:T(8,128)(2,1)S(1)} %get-tuple-element.73), channel_id=1, source_target_pairs={{0,128},{128,0},{1,129},{129,1},{2,130},{130,2},{3,131},{131,3},{4... | collective-permute-start | bytes 3145736 | tf_op jit(solution)/shard_map/ppermute | solution.py:53
  125.5 3.8 %collective-permute-start.18 = (f32[1,256]{1,0:T(1,128)S(1)}, f32[1,256]{1,0:T(1,128)S(1)}, u32[]{:S(2)}, u32[]{:S(2)}) collective-permute-start(f32[1,256]{1,0:T(1,128)S(1)} %bitcast.54), channel_id=1, source_target_pairs={{0,3},{1,0},{2,1},{3,2},{4,7},{5,4},{6,5},{7,6},{8,11},{9,8},{10,9... | collective-permute-start | bytes 3080 | tf_op jit(solution)/shard_map/ppermute | solution.py:42
  126.1 3.9 %collective-permute-start.17 = (f32[1,256]{1,0:T(1,128)S(1)}, f32[1,256]{1,0:T(1,128)S(1)}, u32[]{:S(2)}, u32[]{:S(2)}) collective-permute-start(f32[1,256]{1,0:T(1,128)S(1)} %bitcast.55), channel_id=1, source_target_pairs={{0,2},{1,3},{2,0},{3,1},{4,6},{5,7},{6,4},{7,5},{8,10},{9,11},{10,... | collective-permute-start | bytes 3080 | tf_op jit(solution)/shard_map/ppermute | solution.py:42
  126.1 4.2 %collective-permute-start.16 = (f32[1,256]{1,0:T(1,128)S(1)}, f32[1,256]{1,0:T(1,128)S(1)}, u32[]{:S(2)}, u32[]{:S(2)}) collective-permute-start(f32[1,256]{1,0:T(1,128)S(1)} %bitcast.56), channel_id=1, source_target_pairs={{0,1},{1,2},{2,3},{3,0},{4,5},{5,6},{6,7},{7,4},{8,9},{9,10},{10,1... | collective-permute-start | bytes 3080 | tf_op jit(solution)/shard_map/ppermute | solution.py:42
  130.4 3.1 %collective-permute-start.20 = (f32[1,256]{1,0:T(1,128)S(1)}, f32[1,256]{1,0:T(1,128)S(1)}, u32[]{:S(2)}, u32[]{:S(2)}) collective-permute-start(f32[1,256]{1,0:T(1,128)S(1)} %rsqrt_multiply_fusion), channel_id=1, source_target_pairs={{0,128},{128,0},{1,129},{129,1},{2,130},{130,2},{3,131},{131,3},{4... | collective-permute-start | bytes 3080 | tf_op jit(solution)/shard_map/ppermute | solution.py:53
  (11 other events, 110.8 us)
